TPU v7x, 32 devices: a whole 2x2x4 slice. The times are simulated.
32 devices in a mesh: fsdp: 4 (over z), ctx: 4 (over y, core), tp: 2 (over x).
Axes of the slice: x: 2, y: 2, z: 4, core: 2. Of those that a mesh axis runs over, the one named last changes fastest.
Arguments:
- tokens: bfloat16 [8, 1024, 1024], P('fsdp', 'ctx', 'tp'), may hold values from -6 to 6
- prefix: int32 [8], P('fsdp'), may hold values from 102 to 512
- routes: int32 [4, 8, 256, 8], P('ctx', 'fsdp'), may hold values from 0 to 15, all different within a row; in each aligned block of 512 rows (0 to 511, 512 to 1023, ..., all dimensions but the last counted through in order) at most 384 rows name the same one
- w_query: bfloat16 [1024, 1024], P(('fsdp', 'ctx'), 'tp'), may hold values from -0.5 to 0.5
- w_key: bfloat16 [1024, 512], P(('fsdp', 'ctx'), 'tp'), may hold values from -0.5 to 0.5
- w_value: bfloat16 [1024, 512], P(('fsdp', 'ctx'), 'tp'), may hold values from -0.1875 to 0.1875
- w_out: bfloat16 [1024, 1024], P('tp', ('fsdp', 'ctx')), may hold values from -6 to 6
- w_router: bfloat16 [1024, 16], P(('fsdp', 'ctx')), may hold values from -0.09375 to 0.09375
- gain_attn: bfloat16 [1024], P(('fsdp', 'ctx')), may hold values from 0.5 to 1.5
- gain_ffn: bfloat16 [1024], P(('fsdp', 'ctx')), may hold values from 0.5 to 1.5
- w_gate: bfloat16 [16, 1024, 512], P(None, ('fsdp', 'ctx'), 'tp'), may hold values from -0.1875 to 0.1875
- w_up: bfloat16 [16, 1024, 512], P(None, ('fsdp', 'ctx'), 'tp'), may hold values from -0.1875 to 0.1875
- w_down: bfloat16 [16, 512, 1024], P(None, 'tp', ('fsdp', 'ctx')), may hold values from -6 to 6
- cotangent: bfloat16 [8, 1024, 1024], P('fsdp', 'ctx', 'tp'), may hold values from -6 to 6
Outputs:
- output: bfloat16 [8, 1024, 1024], P('fsdp', 'ctx', 'tp')
- grad_tokens: float32 [8, 1024, 1024], P('fsdp', 'ctx', 'tp')
- grad_query: float32 [1024, 1024], P(('fsdp', 'ctx'), 'tp')
- grad_key: float32 [1024, 512], P(('fsdp', 'ctx'), 'tp')
- grad_value: float32 [1024, 512], P(('fsdp', 'ctx'), 'tp')
- grad_out: float32 [1024, 1024], P('tp', ('fsdp', 'ctx'))
- grad_router: float32 [1024, 16], P(('fsdp', 'ctx'))
- grad_gain_attn: float32 [1024], P(('fsdp', 'ctx'))
- grad_gain_ffn: float32 [1024], P(('fsdp', 'ctx'))
- grad_gate: float32 [16, 1024, 512], P(None, ('fsdp', 'ctx'), 'tp')
- grad_up: float32 [16, 1024, 512], P(None, ('fsdp', 'ctx'), 'tp')
- grad_down: float32 [16, 512, 1024], P(None, 'tp', ('fsdp', 'ctx'))
Inputs may be any that keep to these rules, and one draw needn't show every extreme that they name: `routes`: each row names 8 different experts. In each aligned block of 512 rows in the array's order (the rows of one device), no expert is named by more than 384 rows, a bound that some block reaches.
All inputs are finite; a program needn't handle non-finite values.
Results may differ from a plain program's by a relative error of at most 0.02.
Values may be sent and summed in bfloat16 or wider, within the bound.
No kernel may reach another device: no remote copies, remote signals or barrier semaphores. Data moves between devices by JAX's collectives and lax.ppermute only.
A program may use at most 512 MiB of HBM per device.

v0:
```python
import jax
import jax.numpy as jnp
from jax import lax
from jax.sharding import PartitionSpec as P

HD = 64
TOP = 8


EPSILON = 1e-06
ATTN_SCALE = 0.015625
RESIDUAL_SCALE = 0.22
MASKED_SCORE = -1e30


def rms_scale(hidden, gain):
    return hidden * lax.rsqrt(jnp.mean(hidden * hidden, axis=-1, keepdims=True) + EPSILON) * gain


def rotate(vectors, positions):
    half_width = vectors.shape[-1] // 2
    freqs = 10000.0 ** (-jnp.arange(half_width, dtype=jnp.float32) / half_width)
    angles = positions.astype(jnp.float32)[:, None] * freqs[None, :]
    cosine = jnp.cos(angles)[:, None, :]
    sine = jnp.sin(angles)[:, None, :]
    first = vectors[..., :half_width]
    second = vectors[..., half_width:]
    return jnp.concatenate(
        [first * cosine - second * sine, second * cosine + first * sine], axis=-1
    )


def softmax_rows(values):
    row_max = jnp.max(values, axis=-1, keepdims=True)
    expo = jnp.exp(values - row_max)
    return expo / jnp.sum(expo, axis=-1, keepdims=True)


def swiglu(gate_pre, up_pre):
    return gate_pre * jax.nn.sigmoid(gate_pre) * up_pre


def build_slots(route_rows, experts, capacity):
    route_flat = route_rows.reshape(-1)
    one_hot = (route_flat[:, None] == jnp.arange(experts, dtype=jnp.int32)[None, :]).astype(
        jnp.int32
    )
    before = jnp.cumsum(one_hot, axis=0, dtype=jnp.int32) - one_hot
    slot_place = jnp.sum(before * one_hot, axis=1) + route_flat * capacity
    route_order = jnp.arange(route_flat.shape[0], dtype=jnp.int32)
    slot_route = jnp.zeros((experts * capacity,), jnp.int32).at[slot_place].set(route_order)
    filled = jnp.zeros((experts * capacity,), jnp.float32).at[slot_place].set(1.0)
    return (slot_place, slot_route, filled)


def masked_scores(grouped, key_heads, prefix_len, local_pos):
    scores = (
        jnp.einsum("qgrd,kgd->grqk", grouped, key_heads, preferred_element_type=jnp.float32)
        * ATTN_SCALE
    )
    key_pos = jnp.arange(key_heads.shape[0], dtype=jnp.int32)
    visible = (key_pos[None, :] <= local_pos[:, None]) | (key_pos[None, :] < prefix_len)
    return jnp.where(visible, scores, MASKED_SCORE)


def attend_forward(record, local_pos):
    queries, key_heads, value_heads, prefix_len = record
    block_len, head_count, head_width = queries.shape
    kv_count = key_heads.shape[1]
    grouped = queries.reshape(block_len, kv_count, head_count // kv_count, head_width)
    scores = masked_scores(grouped, key_heads, prefix_len, local_pos)
    row_max = jnp.max(scores, axis=-1, keepdims=True)
    expo = jnp.exp(scores - row_max)
    totals = jnp.sum(expo, axis=-1, keepdims=True)
    probs = (expo / totals).astype(jnp.bfloat16)
    attended = jnp.einsum("grqk,kgd->qgrd", probs, value_heads, preferred_element_type=jnp.float32)
    log_total = (row_max + jnp.log(totals))[..., 0]
    return (attended.reshape(block_len, head_count * head_width).astype(jnp.bfloat16), log_total)


def attend_backward(record, local_pos):
    queries, key_heads, value_heads, prefix_len, log_total, attended_grad = record
    block_len, head_count, head_width = queries.shape
    kv_count = key_heads.shape[1]
    grouped = queries.reshape(block_len, kv_count, head_count // kv_count, head_width)
    scores = masked_scores(grouped, key_heads, prefix_len, local_pos)
    probs = jnp.exp(scores - log_total[..., None])
    rounded = probs.astype(jnp.bfloat16)
    grad_grouped = attended_grad.reshape(block_len, kv_count, head_count // kv_count, head_width)
    grad_probs = jnp.einsum(
        "qgrd,kgd->grqk", grad_grouped, value_heads, preferred_element_type=jnp.float32
    )
    inner = jnp.sum(probs * grad_probs, axis=-1, keepdims=True)
    grad_scores = (probs * (grad_probs - inner)).astype(jnp.bfloat16)
    grad_queries = (
        jnp.einsum("grqk,kgd->qgrd", grad_scores, key_heads, preferred_element_type=jnp.float32)
        * ATTN_SCALE
    )
    grad_keys = (
        jnp.einsum("grqk,qgrd->kgd", grad_scores, grouped, preferred_element_type=jnp.float32)
        * ATTN_SCALE
    )
    grad_values = jnp.einsum(
        "grqk,qgrd->kgd", rounded, grad_grouped, preferred_element_type=jnp.float32
    )
    return (grad_queries.reshape(block_len, head_count, head_width), grad_keys, grad_values)


def per_device(
    tokens,
    prefix,
    routes,
    w_query,
    w_key,
    w_value,
    w_out,
    w_router,
    gain_attn,
    gain_ffn,
    w_gate,
    w_up,
    w_down,
    cotangent,
):
    seq_count, block_len, feature_part = tokens.shape
    row_count = seq_count * block_len
    full_tokens, full_cotangent = (
        lax.all_gather(tokens, "tp", axis=2, tiled=True),
        lax.all_gather(cotangent, "tp", axis=2, tiled=True),
    )
    query_full, key_full, value_full, router_full, gain_one, gain_two, out_full = (
        lax.all_gather(w_query, ("fsdp", "ctx"), axis=0, tiled=True),
        lax.all_gather(w_key, ("fsdp", "ctx"), axis=0, tiled=True),
        lax.all_gather(w_value, ("fsdp", "ctx"), axis=0, tiled=True),
        lax.all_gather(w_router, ("fsdp", "ctx"), axis=0, tiled=True),
        lax.all_gather(gain_attn, ("fsdp", "ctx"), axis=0, tiled=True),
        lax.all_gather(gain_ffn, ("fsdp", "ctx"), axis=0, tiled=True),
        lax.all_gather(w_out, ("fsdp", "ctx"), axis=1, tiled=True),
    )
    model_width = full_tokens.shape[2]
    gain_one = gain_one.astype(jnp.float32)
    gain_two = gain_two.astype(jnp.float32)
    source = full_tokens.reshape(row_count, model_width).astype(jnp.float32)
    normed = rms_scale(source, gain_one).astype(jnp.bfloat16)
    head_count = query_full.shape[1] // HD
    kv_count = key_full.shape[1] // HD
    offset = lax.axis_index("ctx") * block_len
    local_pos = offset + jnp.arange(block_len, dtype=jnp.int32)
    positions = jnp.tile(local_pos, seq_count)
    queries = rotate(
        jnp.dot(normed, query_full, preferred_element_type=jnp.float32).reshape(
            row_count, head_count, HD
        ),
        positions,
    ).astype(jnp.bfloat16)
    key_rows = rotate(
        jnp.dot(normed, key_full, preferred_element_type=jnp.float32).reshape(
            row_count, kv_count, HD
        ),
        positions,
    ).astype(jnp.bfloat16)
    value_rows = jnp.dot(normed, value_full, preferred_element_type=jnp.float32).astype(
        jnp.bfloat16
    )
    all_keys, all_values = (
        lax.all_gather(
            key_rows.reshape(seq_count, block_len, kv_count * HD), "ctx", axis=1, tiled=True
        ),
        lax.all_gather(
            value_rows.reshape(seq_count, block_len, kv_count * HD), "ctx", axis=1, tiled=True
        ),
    )
    length = all_keys.shape[1]
    key_heads = all_keys.reshape(seq_count, length, kv_count, HD)
    value_heads = all_values.reshape(seq_count, length, kv_count, HD)
    query_seq = queries.reshape(seq_count, block_len, head_count, HD)
    attended, log_total = lax.map(
        lambda record: attend_forward(record, local_pos),
        (query_seq, key_heads, value_heads, prefix),
    )
    attended_flat = attended.reshape(row_count, head_count * HD)
    branch = jnp.dot(attended_flat, out_full, preferred_element_type=jnp.float32)
    branch_sum = lax.psum(branch, "tp")
    middle = source + RESIDUAL_SCALE * branch_sum
    middle_part = lax.dynamic_slice_in_dim(
        middle, lax.axis_index("tp") * feature_part, feature_part, 1
    )
    normed_two = rms_scale(middle, gain_two).astype(jnp.bfloat16)
    logits = jnp.dot(normed_two, router_full, preferred_element_type=jnp.float32)
    experts = router_full.shape[1]
    route_rows = routes.reshape(row_count, TOP)
    one_hot = (
        route_rows[:, :, None] == jnp.arange(experts, dtype=jnp.int32)[None, None, :]
    ).astype(jnp.float32)
    chosen = jnp.sum(one_hot * logits[:, None, :], axis=-1)
    gate_weights, gate_pull = jax.vjp(softmax_rows, chosen)
    capacity = row_count * TOP * 3 // (2 * experts)
    slot_place, slot_route, filled = build_slots(route_rows, experts, capacity)
    token_of = (slot_route // TOP).reshape(experts, capacity)
    slot_gate = (gate_weights.reshape(-1)[slot_route] * filled).reshape(experts, capacity)
    scaled_grad = (
        full_cotangent.reshape(row_count, model_width).astype(jnp.float32) * RESIDUAL_SCALE
    )
    empty_rows = jnp.zeros((row_count, model_width), jnp.float32)
    gate_stack, up_stack, down_stack = (
        lax.all_gather(w_gate, ("fsdp", "ctx"), axis=1, tiled=True),
        lax.all_gather(w_up, ("fsdp", "ctx"), axis=1, tiled=True),
        lax.all_gather(w_down, ("fsdp", "ctx"), axis=2, tiled=True),
    )

    def expert_forward(totals, record):
        gate_w, up_w, down_w, token_ids, weight = record
        picked = normed_two[token_ids]
        gate_pre = jnp.dot(picked, gate_w, preferred_element_type=jnp.float32)
        up_pre = jnp.dot(picked, up_w, preferred_element_type=jnp.float32)
        hidden = swiglu(gate_pre, up_pre).astype(jnp.bfloat16)
        result = jnp.dot(hidden, down_w, preferred_element_type=jnp.float32)
        totals = totals.at[token_ids].add(weight[:, None] * result)
        return (totals, (gate_pre, up_pre, jnp.sum(scaled_grad[token_ids] * result, axis=-1)))

    moe, (gate_keep, up_keep, slot_grad_part) = lax.scan(
        expert_forward, empty_rows, (gate_stack, up_stack, down_stack, token_of, slot_gate)
    )
    moe_part = lax.psum_scatter(
        moe.astype(jnp.bfloat16), "tp", scatter_dimension=1, tiled=True
    ).astype(jnp.float32)
    output = (
        (middle_part + RESIDUAL_SCALE * moe_part)
        .astype(jnp.bfloat16)
        .reshape(seq_count, block_len, feature_part)
    )

    def expert_backward(totals, record):
        gate_w, up_w, down_w, token_ids, weight, gate_pre, up_pre = record
        picked = normed_two[token_ids]
        result_grad = (weight[:, None] * scaled_grad[token_ids]).astype(jnp.bfloat16)
        hidden_float, hidden_pull = jax.vjp(swiglu, gate_pre, up_pre)
        hidden = hidden_float.astype(jnp.bfloat16)
        hidden_grad = jnp.dot(result_grad, down_w.T, preferred_element_type=jnp.float32)
        gate_grad, up_grad = hidden_pull(hidden_grad)
        gate_grad = gate_grad.astype(jnp.bfloat16)
        up_grad = up_grad.astype(jnp.bfloat16)
        down_term = jnp.dot(hidden.T, result_grad, preferred_element_type=jnp.float32)
        gate_term = jnp.dot(picked.T, gate_grad, preferred_element_type=jnp.float32)
        up_term = jnp.dot(picked.T, up_grad, preferred_element_type=jnp.float32)
        picked_grad = jnp.dot(gate_grad, gate_w.T, preferred_element_type=jnp.float32) + jnp.dot(
            up_grad, up_w.T, preferred_element_type=jnp.float32
        )
        return (totals.at[token_ids].add(picked_grad), (gate_term, up_term, down_term))

    normed_grad_part, (gate_terms, up_terms, down_terms) = lax.scan(
        expert_backward,
        empty_rows,
        (gate_stack, up_stack, down_stack, token_of, slot_gate, gate_keep, up_keep),
    )
    normed_grad_sum, slot_grad = (
        lax.psum(normed_grad_part.astype(jnp.bfloat16), "tp").astype(jnp.float32),
        lax.psum(slot_grad_part.astype(jnp.bfloat16), "tp").astype(jnp.float32),
    )
    route_grad = slot_grad.reshape(-1)[slot_place].reshape(row_count, TOP)
    chosen_grad = gate_pull(route_grad)[0]
    logit_grad = jnp.sum(one_hot * chosen_grad[:, :, None], axis=1).astype(jnp.bfloat16)
    router_term = jnp.dot(normed_two.T, logit_grad, preferred_element_type=jnp.float32)
    normed_two_grad = normed_grad_sum + jnp.dot(
        logit_grad, router_full.T, preferred_element_type=jnp.float32
    )
    _, second_pull = jax.vjp(rms_scale, middle, gain_two)
    middle_grad, gain_two_term = second_pull(normed_two_grad)
    middle_grad = middle_grad + full_cotangent.reshape(row_count, model_width).astype(jnp.float32)
    branch_grad = (RESIDUAL_SCALE * middle_grad).astype(jnp.bfloat16)
    out_term = jnp.dot(attended_flat.T, branch_grad, preferred_element_type=jnp.float32)
    attended_grad = (
        jnp.dot(branch_grad, out_full.T, preferred_element_type=jnp.float32)
        .astype(jnp.bfloat16)
        .reshape(seq_count, block_len, head_count * HD)
    )
    query_grad, key_grad, value_grad = lax.map(
        lambda record: attend_backward(record, local_pos),
        (query_seq, key_heads, value_heads, prefix, log_total, attended_grad),
    )
    key_sum, value_sum = (
        lax.psum_scatter(
            key_grad.reshape(seq_count, length, kv_count * HD).astype(jnp.bfloat16),
            "ctx",
            scatter_dimension=1,
            tiled=True,
        ).astype(jnp.float32),
        lax.psum_scatter(
            value_grad.reshape(seq_count, length, kv_count * HD).astype(jnp.bfloat16),
            "ctx",
            scatter_dimension=1,
            tiled=True,
        ).astype(jnp.float32),
    )
    query_raw = (
        rotate(query_grad.reshape(row_count, head_count, HD), -positions)
        .reshape(row_count, head_count * HD)
        .astype(jnp.bfloat16)
    )
    key_raw = (
        rotate(key_sum.reshape(row_count, kv_count, HD), -positions)
        .reshape(row_count, kv_count * HD)
        .astype(jnp.bfloat16)
    )
    value_raw = value_sum.reshape(row_count, kv_count * HD).astype(jnp.bfloat16)
    query_term = jnp.dot(normed.T, query_raw, preferred_element_type=jnp.float32)
    key_term = jnp.dot(normed.T, key_raw, preferred_element_type=jnp.float32)
    value_term = jnp.dot(normed.T, value_raw, preferred_element_type=jnp.float32)
    normed_grad_local = (
        jnp.dot(query_raw, query_full.T, preferred_element_type=jnp.float32)
        + jnp.dot(key_raw, key_full.T, preferred_element_type=jnp.float32)
        + jnp.dot(value_raw, value_full.T, preferred_element_type=jnp.float32)
    )
    normed_grad = lax.psum(normed_grad_local.astype(jnp.bfloat16), "tp").astype(jnp.float32)
    _, first_pull = jax.vjp(rms_scale, source, gain_one)
    source_grad, gain_one_term = first_pull(normed_grad)
    tokens_grad_full = middle_grad + source_grad
    tokens_grad = lax.dynamic_slice_in_dim(
        tokens_grad_full, lax.axis_index("tp") * feature_part, feature_part, 1
    ).reshape(seq_count, block_len, feature_part)
    (
        grad_query,
        grad_key,
        grad_value,
        grad_router,
        grad_gain_attn,
        grad_gain_ffn,
        grad_out,
        grad_gate,
        grad_up,
        grad_down,
    ) = (
        lax.psum_scatter(query_term, ("fsdp", "ctx"), scatter_dimension=0, tiled=True),
        lax.psum_scatter(key_term, ("fsdp", "ctx"), scatter_dimension=0, tiled=True),
        lax.psum_scatter(value_term, ("fsdp", "ctx"), scatter_dimension=0, tiled=True),
        lax.psum_scatter(router_term, ("fsdp", "ctx"), scatter_dimension=0, tiled=True),
        lax.psum_scatter(gain_one_term, ("fsdp", "ctx"), scatter_dimension=0, tiled=True),
        lax.psum_scatter(gain_two_term, ("fsdp", "ctx"), scatter_dimension=0, tiled=True),
        lax.psum_scatter(out_term, ("fsdp", "ctx"), scatter_dimension=1, tiled=True),
        lax.psum_scatter(gate_terms, ("fsdp", "ctx"), scatter_dimension=1, tiled=True),
        lax.psum_scatter(up_terms, ("fsdp", "ctx"), scatter_dimension=1, tiled=True),
        lax.psum_scatter(down_terms, ("fsdp", "ctx"), scatter_dimension=2, tiled=True),
    )
    return (
        output,
        tokens_grad,
        grad_query,
        grad_key,
        grad_value,
        grad_out,
        grad_router,
        grad_gain_attn,
        grad_gain_ffn,
        grad_gate,
        grad_up,
        grad_down,
    )


def solution(mesh):
    in_specs = (
        P("fsdp", "ctx", "tp"),
        P("fsdp"),
        P("ctx", "fsdp", None, None),
        P(("fsdp", "ctx"), "tp"),
        P(("fsdp", "ctx"), "tp"),
        P(("fsdp", "ctx"), "tp"),
        P("tp", ("fsdp", "ctx")),
        P(("fsdp", "ctx"), None),
        P(("fsdp", "ctx")),
        P(("fsdp", "ctx")),
        P(None, ("fsdp", "ctx"), "tp"),
        P(None, ("fsdp", "ctx"), "tp"),
        P(None, "tp", ("fsdp", "ctx")),
        P("fsdp", "ctx", "tp"),
    )
    out_specs = (
        P("fsdp", "ctx", "tp"),
        P("fsdp", "ctx", "tp"),
        P(("fsdp", "ctx"), "tp"),
        P(("fsdp", "ctx"), "tp"),
        P(("fsdp", "ctx"), "tp"),
        P("tp", ("fsdp", "ctx")),
        P(("fsdp", "ctx"), None),
        P(("fsdp", "ctx")),
        P(("fsdp", "ctx")),
        P(None, ("fsdp", "ctx"), "tp"),
        P(None, ("fsdp", "ctx"), "tp"),
        P(None, "tp", ("fsdp", "ctx")),
    )
    return jax.shard_map(
        per_device, mesh=mesh, in_specs=in_specs, out_specs=out_specs, check_vma=False
    )
```

profile of v0, /device:TPU:0, one launch (start us, length us, event | category | flops | bytes accessed | tf_op | source)
XLA Modules:
  0.0 2558.9 jit_solution(954034129737198886)
XLA Ops:
  12.4 35.0 %all-reduce.5 = (bf16[1024]{0:T(1024)(128)(2,1)S(1)}, bf16[1024]{0:T(1024)(128)(2,1)S(1)}) all-reduce(bf16[1024]{0:T(1024)(128)(2,1)S(1)} %dynamic-update-slice, bf16[1024]{0:T(1024)(128)(2,1)S(1)} %dynamic-update-slice.1), channel_id=1, replica_groups=mesh['fsdp'=4,'ctx'=4,'tp'=2] {'fsdp','ctx'}, use_global_device_ids=true, to_apply=%add | all-reduce | flops 2048 | bytes 8192
  47.5 19.5 all_gather.44
  67.0 20.9 all_gather.46
  109.5 17.4 all-gather.15.cloned.1.call-done
  128.4 15.9 while.62
  144.3 22.6 all-gather.19.cloned.1.call-done
  179.8 15.5 scatter_custom_fusion.2
  196.0 19.5 all-gather
  233.3 20.5 all-reduce.10.cloned.1.call-done
  257.8 34.3 %gather_fusion.4 = f32[6144]{0:T(1024)S(1)} fusion(f32[4096]{0:T(1024)S(1)} %div.102, s32[6144]{0:T(1024)S(1)} %get-tuple-element.530), kind=kCustom, calls=%fused_computation.4 | custom fusion | bytes 73728 | tf_op jit(solution)/shard_map/gather | solution.py:200
  292.1 39.6 %all-gather.25.cloned.1.call-done = bf16[16,256,1024]{1,0,2:T(8,128)(2,1)} async-done(((bf16[16,256,64]{1,0,2:T(8,128)(2,1)}), bf16[16,256,1024]{1,0,2:T(8,128)(2,1)}) %all-gather.25.cloned.1.call-update) | async-done | bytes 8388624 | tf_op jit(solution)/shard_map/all_gather | solution.py:208
  344.0 63.3 %all-gather.21.cloned.1.call-done = bf16[16,1024,256]{2,1,0:T(8,128)(2,1)} async-done(((bf16[16,64,256]{2,1,0:T(8,128)(2,1)}), bf16[16,1024,256]{2,1,0:T(8,128)(2,1)}) %all-gather.21.cloned.1.call-update) | async-done | bytes 8388624 | tf_op jit(solution)/shard_map/all_gather | solution.py:206
  407.3 75.5 %all-gather.23.cloned.1.call-done = bf16[16,1024,256]{2,1,0:T(8,128)(2,1)} async-done(((bf16[16,64,256]{2,1,0:T(8,128)(2,1)}), bf16[16,1024,256]{2,1,0:T(8,128)(2,1)}) %all-gather.23.cloned.1.call-update) | async-done | bytes 8388624 | tf_op jit(solution)/shard_map/all_gather | solution.py:207
  484.4 354.3 %while.60 = (s32[]{:T(128)}, f32[512,1024]{1,0:T(8,128)}, f32[16,384,256]{2,1,0:T(8,128)}, f32[16,384,256]{2,1,0:T(8,128)}, bf16[16,384]{1,0:T(8,128)(2,1)}, /*i...) while((s32[]{:T(128)}, f32[512,1024]{1,0:T(8,128)}, ...), condition=%wide.region_18.19_spmd, body=%wide.region_15.18_spmd.sunk | while | flops 606144256 | bytes 26499540 | solution.py:221
  840.3 457.8 %while.61 = (s32[]{:T(128)}, f32[512,1024]{1,0:T(8,128)}, f32[16,1024,256]{2,1,0:T(8,128)}, f32[16,1024,256]{2,1,0:T(8,128)}, f32[16,256,1024]{1,2,0:T(8,128)}, ...) while((s32[]{:T(128)}, f32[512,1024]{1,0:T(8,128)}, ...), condition=%wide.region_22.23_spmd, body=%wide.region_20.22_spmd.sunk | while | flops 1212287104 | bytes 34985868 | solution.py:251
  1309.6 23.2 gather_fusion.5
  1345.7 79.5 %while.63 = (s32[]{:T(128)}, f32[2,256,8,64]{1,0,3,2:T(2,128)}, bf16[2,1024,4,64]{1,3,2,0:T(8,128)(2,1)}, bf16[2,1024,4,64]{1,3,2,0:T(8,128)(2,1)}, bf16[2,1024,...) while((s32[]{:T(128)}, f32[2,256,8,64]{1,0,3,2:T(2,128)}, ...), condition=%wide.region_32.33_spmd.clone, body=%wide.region_30.32_spmd.clone.sunk | while | flops 1374551296 | bytes 123269432 | solution.py:277
  1427.5 49.3 %copy.134 = bf16[2,1024,256]{0,2,1:T(8,128)(2,1)} copy(bf16[2,1024,256]{1,0,2:T(2,128)(2,1)S(1)} %bitcast.449) | data formatting | bytes 2097152
  1476.8 97.4 %reshape.727 = bf16[1024,512]{1,0:T(8,128)(2,1)} reshape(bf16[1024,256,2]{2,1,0:T(8,128)(2,1)} %bitcast.80) | data formatting | bytes 2097152
  1582.4 16.9 reduce-scatter.34.cloned.1.call-done
  1599.3 37.9 %reshape.728 = bf16[256,256,2]{2,1,0:T(8,128)(2,1)} reshape(bf16[256,512]{1,0:T(8,128)(2,1)} %reduce-scatter.34.cloned.1.call-done) | data formatting | bytes 524288
  1637.2 16.4 copy.135
  1688.1 20.7 reduce-scatter.16.cloned.1.call-done
  1710.8 40.2 %all-reduce.14.cloned.1.call-done = bf16[512,1024]{1,0:T(8,128)(2,1)} async-done(((bf16[512,1024]{1,0:T(8,128)(2,1)}), bf16[512,1024]{1,0:T(8,128)(2,1)}) %all-reduce.14.cloned.1.call-update) | async-done | bytes 1048592 | tf_op jit(solution)/shard_map/psum | solution.py:314
  1754.5 33.9 %all-reduce.4 = (f32[1024]{0:T(1024)S(1)}, f32[1024]{0:T(1024)S(1)}) all-reduce(f32[1024]{0:T(1024)S(1)} %get-tuple-element.409, f32[1024]{0:T(1024)S(1)} %copy-done.70), channel_id=10, replica_groups=mesh['fsdp'=4,'ctx'=4,'tp'=2] {'fsdp','ctx'}, use_global_device_ids=true, to_apply=%region_43.44.clone | all-reduce | flops 2048 | bytes 16384
  1792.4 24.9 reduce-scatter.20.cloned.1.call-done
  1817.3 64.7 %reduce-scatter.26.cloned.1.call-done = f32[512,64]{0,1:T(8,128)} async-done(((f32[512,1024]{0,1:T(8,128)}), f32[512,64]{0,1:T(8,128)}) %reduce-scatter.26.cloned.1.call-update) | async-done | bytes 131088 | tf_op jit(solution)/shard_map/reduce_scatter | solution.py:339
  1882.0 61.0 %reduce-scatter.22.cloned.1.call-done = f32[64,256]{1,0:T(8,128)} async-done(((f32[1024,256]{1,0:T(8,128)}), f32[64,256]{1,0:T(8,128)}) %reduce-scatter.22.cloned.1.call-update) | async-done | bytes 65552 | tf_op jit(solution)/shard_map/reduce_scatter | solution.py:334
  1943.0 60.6 %reduce-scatter.24.cloned.1.call-done = f32[64,256]{1,0:T(8,128)} async-done(((f32[1024,256]{1,0:T(8,128)}), f32[64,256]{1,0:T(8,128)}) %reduce-scatter.24.cloned.1.call-update) | async-done | bytes 65552 | tf_op jit(solution)/shard_map/reduce_scatter | solution.py:335
  2003.6 182.8 %reduce-scatter.28.cloned.1.call-done = f32[16,64,256]{2,1,0:T(8,128)} async-done(((f32[16,1024,256]{2,1,0:T(8,128)}), f32[16,64,256]{2,1,0:T(8,128)}) %reduce-scatter.28.cloned.1.call-update) | async-done | bytes 1048592 | tf_op jit(solution)/shard_map/reduce_scatter | solution.py:340
  2186.4 182.8 %reduce-scatter.30.cloned.1.call-done = f32[16,64,256]{2,1,0:T(8,128)} async-done(((f32[16,1024,256]{2,1,0:T(8,128)}), f32[16,64,256]{2,1,0:T(8,128)}) %reduce-scatter.30.cloned.1.call-update) | async-done | bytes 1048592 | tf_op jit(solution)/shard_map/reduce_scatter | solution.py:341
  2369.2 182.8 %reduce-scatter.32.cloned.1.call-done = f32[16,256,64]{1,2,0:T(8,128)} async-done(((f32[16,256,1024]{1,2,0:T(8,128)}), f32[16,256,64]{1,2,0:T(8,128)}) %reduce-scatter.32.cloned.1.call-update) | async-done | bytes 1048592 | tf_op jit(solution)/shard_map/reduce_scatter | solution.py:342
  (1065 shorter events, 1061.1 us)
Async XLA Ops:
  7.2 80.7 %all-gather.11.cloned.1.call-start = ((), (), s32[]{:S(2)}) async-start(), calls=%async_computation.11 | async-start | bytes 1572864 | tf_op jit(solution)/shard_map/all_gather | solution.py:128
  7.9 90.2 %all-gather.17.cloned.1.call-start = ((), (), s32[]{:S(2)}) async-start(), calls=%async_computation.14 | async-start | bytes 1114112 | tf_op jit(solution)/shard_map/all_gather | solution.py:132
  8.7 99.3 %all-gather.13.cloned.1.call-start = ((), (), s32[]{:S(2)}) async-start(), calls=%async_computation.12 | async-start | bytes 1310720 | tf_op jit(solution)/shard_map/all_gather | solution.py:169
  47.4 47.7 %copy-start.53 = (f32[1024]{0:T(1024)}, f32[1024]{0:T(1024)S(1)}, u32[]{:S(2)}) copy-start(f32[1024]{0:T(1024)S(1)} %convert_element_type.209) | copy-start | bytes 12292
  93.7 33.2 %all-gather.15.cloned.1.call-start = ((), (), s32[]{:S(2)}) async-start(), calls=%async_computation.13 | async-start | bytes 1310720 | tf_op jit(solution)/shard_map/all_gather | solution.py:166
  96.9 70.0 %all-gather.19.cloned.1.call-start = ((), (), s32[]{:S(2)}) async-start(), calls=%async_computation.15 | async-start | bytes 1114112 | tf_op jit(solution)/shard_map/all_gather | solution.py:138
  97.5 134.3 %all-gather.27.cloned.1.call-start = ((), (), s32[]{:S(2)}) async-start(), calls=%async_computation.20 | async-start | bytes 1572864 | tf_op jit(solution)/shard_map/all_gather | solution.py:129
  98.0 155.7 %all-reduce.10.cloned.1.call-start = ((), (), s32[]{:S(2)}) async-start(), calls=%async_computation.16 | async-start | bytes 4194304 | tf_op jit(solution)/shard_map/psum | solution.py:183
  170.4 161.2 %all-gather.25.cloned.1.call-start = ((), (), s32[]{:S(2)}) async-start(), calls=%async_computation.19 | async-start | bytes 8912896 | tf_op jit(solution)/shard_map/all_gather | solution.py:208
  171.6 235.7 %all-gather.21.cloned.1.call-start = ((), (), s32[]{:S(2)}) async-start(), calls=%async_computation.17 | async-start | bytes 8912896 | tf_op jit(solution)/shard_map/all_gather | solution.py:206
  172.4 310.4 %all-gather.23.cloned.1.call-start = ((), (), s32[]{:S(2)}) async-start(), calls=%async_computation.18 | async-start | bytes 8912896 | tf_op jit(solution)/shard_map/all_gather | solution.py:207
  173.0 1166.7 %all-reduce.12.cloned.1.call-start = ((), (), s32[]{:S(2)}) async-start(), calls=%async_computation.22 | async-start | bytes 2097152 | tf_op jit(solution)/shard_map/psum | solution.py:257
  179.5 74.2 %copy-start.13 = (bf16[2,256,1024]{2,1,0:T(8,128)(2,1)S(1)}, bf16[2,256,1024]{2,1,0:T(8,128)(2,1)}, u32[]{:S(2)}) copy-start(bf16[2,256,1024]{2,1,0:T(8,128)(2,1)} %all-gather.11.cloned.1.call-done) | copy-start | bytes 3145732
  196.0 59.8 %copy-start.55 = (f32[1024]{0:T(1024)}, f32[1024]{0:T(1024)S(1)}, u32[]{:S(2)}) copy-start(f32[1024]{0:T(1024)S(1)} %convert_element_type.219) | copy-start | bytes 12292
  1301.2 298.1 %reduce-scatter.34.cloned.1.call-start = ((), (), s32[]{:S(2)}) async-start(), calls=%async_computation.32 | async-start | bytes 1310720
  1476.8 97.5 %copy-start.35 = (bf16[2,1024,4,64]{1,3,2,0:T(8,128)(2,1)S(1)}, bf16[2,1024,4,64]{1,3,2,0:T(8,128)(2,1)}, u32[]{:S(2)}) copy-start(bf16[2,1024,4,64]{1,3,2,0:T(8,128)(2,1)} %get-tuple-element.263) | copy-start | bytes 3145732
  1574.2 82.3 %reduce-scatter.18.cloned.1.call-start = ((), (), s32[]{:S(2)}) async-start(), calls=%async_computation.23 | async-start | bytes 1310720 | tf_op jit(solution)/shard_map/reduce_scatter | solution.py:288
  1575.6 111.1 %reduce-scatter.36.cloned.1.call-start = ((), (), s32[]{:S(2)}) async-start(), calls=%async_computation.33 | async-start | bytes 557056
  1577.1 131.7 %reduce-scatter.16.cloned.1.call-start = ((), (), s32[]{:S(2)}) async-start(), calls=%async_computation.21 | async-start | bytes 1572864 | tf_op jit(solution)/shard_map/reduce_scatter | solution.py:224
  1578.3 172.7 %all-reduce.14.cloned.1.call-start = ((), (), s32[]{:S(2)}) async-start(), calls=%async_computation.24 | async-start | bytes 2097152 | tf_op jit(solution)/shard_map/psum | solution.py:314
  1660.0 157.3 %reduce-scatter.20.cloned.1.call-start = ((), (), s32[]{:S(2)}) async-start(), calls=%async_computation.25 | async-start | bytes 2228224 | tf_op jit(solution)/shard_map/reduce_scatter | solution.py:333
  1663.4 218.6 %reduce-scatter.26.cloned.1.call-start = ((), (), s32[]{:S(2)}) async-start(), calls=%async_computation.28 | async-start | bytes 2228224 | tf_op jit(solution)/shard_map/reduce_scatter | solution.py:339
  1666.6 276.4 %reduce-scatter.22.cloned.1.call-start = ((), (), s32[]{:S(2)}) async-start(), calls=%async_computation.26 | async-start | bytes 1114112 | tf_op jit(solution)/shard_map/reduce_scatter | solution.py:334
  1668.1 335.5 %reduce-scatter.24.cloned.1.call-start = ((), (), s32[]{:S(2)}) async-start(), calls=%async_computation.27 | async-start | bytes 1114112 | tf_op jit(solution)/shard_map/reduce_scatter | solution.py:335
  1669.7 516.7 %reduce-scatter.28.cloned.1.call-start = ((), (), s32[]{:S(2)}) async-start(), calls=%async_computation.29 | async-start | bytes 17825792 | tf_op jit(solution)/shard_map/reduce_scatter | solution.py:340
  1670.4 698.7 %reduce-scatter.30.cloned.1.call-start = ((), (), s32[]{:S(2)}) async-start(), calls=%async_computation.30 | async-start | bytes 17825792 | tf_op jit(solution)/shard_map/reduce_scatter | solution.py:341
  1671.2 880.8 %reduce-scatter.32.cloned.1.call-start = ((), (), s32[]{:S(2)}) async-start(), calls=%async_computation.31 | async-start | bytes 17825792 | tf_op jit(solution)/shard_map/reduce_scatter | solution.py:342
  1671.9 79.2 %copy-start.14 = (bf16[2,256,1024]{2,1,0:T(8,128)(2,1)S(1)}, bf16[2,256,1024]{2,1,0:T(8,128)(2,1)}, u32[]{:S(2)}) copy-start(bf16[2,256,1024]{2,1,0:T(8,128)(2,1)} %all-gather.11.cloned.1.call-done) | copy-start | bytes 3145732
  1671.9 79.2 %copy-start.54 = (f32[1024]{0:T(1024)S(1)}, f32[1024]{0:T(1024)}, u32[]{:S(2)}) copy-start(f32[1024]{0:T(1024)} %copy-done.53) | copy-start | bytes 12292
  1671.9 79.2 %copy-start.63 = (f32[512]{0:T(512)S(1)}, f32[512]{0:T(512)}, u32[]{:S(2)}) copy-start(f32[512]{0:T(512)} %copy-done.62) | copy-start | bytes 6148
  1710.8 78.7 %copy-start.69 = (f32[1,2,2,128]{3,1,2,0:T(2,128)S(1)}, f32[1,2,2,128]{3,1,2,0:T(2,128)}, u32[]{:S(2)}) copy-start(f32[1,2,2,128]{3,1,2,0:T(2,128)} %copy-done.68) | copy-start | bytes 6148
  1710.8 78.7 %copy-start.17 = (f32[512,1024]{1,0:T(8,128)S(1)}, f32[512,1024]{1,0:T(8,128)}, u32[]{:S(2)}) copy-start(f32[512,1024]{1,0:T(8,128)} %copy-done.15) | copy-start | bytes 6291460
  (223 other events, 1165.6 us)
Sparse Core Ops, SparseCore 0:
  9.6 23.9 all-gather.10
  35.7 38.1 all-gather.16
  93.8 14.1 all-gather.12
  110.0 16.8 all-gather.14
  128.9 37.9 all-gather.18
  168.3 20.2 all-gather.26
  190.8 62.8 all-reduce.9
  256.7 74.9 all-gather.24
  334.1 73.1 all-gather.20
  409.6 73.1 all-gather.22
  1301.4 38.2 all-reduce.11
  1574.3 24.9 reduce-scatter.33
  1602.6 24.8 reduce-scatter.17
  1630.9 55.7 reduce-scatter.35
  1689.4 19.3 reduce-scatter.15
  1711.0 40.0 all-reduce.13
  1755.7 61.5 reduce-scatter.19
  1821.5 60.4 reduce-scatter.25
  1886.6 56.3 reduce-scatter.21
  1947.0 56.5 reduce-scatter.23
  2008.8 177.4 reduce-scatter.27
  2191.6 177.5 reduce-scatter.29
  2374.4 177.5 reduce-scatter.31
where the time goes:
time: 2580 us; the launch traced here: 2560 us
  waiting for transfers between devices  1110 us (43%)
  local copies, waits for them, and re-layouts  556 us (22%)
  matrix products  423 us (16%)
  other arithmetic  313 us (12%)
  blocking collectives  137 us (5%)
    unnamed x145, local copies, waits for them, and re-layouts  214 us
    reduce_scatter x1, waiting for transfers between devices, per_device(): lax.psum_scatter(down_terms, ('fsdp', 'ctx'), scatter_dimension=2, tiled=...  183 us
    reduce_scatter x1, waiting for transfers between devices, per_device(): lax.psum_scatter(up_terms, ('fsdp', 'ctx'), scatter_dimension=1, tiled=True)  183 us
    reduce_scatter x1, waiting for transfers between devices, per_device(): lax.psum_scatter(gate_terms, ('fsdp', 'ctx'), scatter_dimension=1, tiled=...  183 us
    scatter-add x16, other arithmetic, expert_backward(): totals.at[token_ids].add(picked_grad)  129 us
    scatter-add x16, other arithmetic, expert_forward(): totals = totals.at[token_ids].add(weight[:, None] * result)  121 us
    all_gather x1, waiting for transfers between devices, per_device(): lax.all_gather(w_up, ('fsdp', 'ctx'), axis=1, tiled=True)  75.5 us
    unnamed x2, blocking collectives  68.9 us
  transfers between devices with their start and end apart: 23, of which 19 were waited for; matrix products, arithmetic and copies ran while one was open for 9% of the time, Pallas kernels for 0%

commit v1 on v0

v1 whole, which is shorter than its diff:
```python
import functools

import jax
import jax.numpy as jnp
from jax import lax
from jax.experimental import pallas as pl
from jax.experimental.pallas import tpu as pltpu
from jax.sharding import PartitionSpec as P

HD = 64
TOP = 8
LANES = 128

EPSILON = 1e-06
ATTN_SCALE = 0.015625
RESIDUAL_SCALE = 0.22
MASKED_SCORE = -1e30
GROUPS = 4
RING = ("fsdp", "ctx")
BF = jnp.bfloat16
F32 = jnp.float32
VMEM_LIMIT = 60 * 1024 * 1024


def nt(a, b):
    return lax.dot_general(a, b, (((1,), (1,)), ((), ())), preferred_element_type=F32)


def nn(a, b):
    return lax.dot_general(a, b, (((1,), (0,)), ((), ())), preferred_element_type=F32)


def tn(a, b):
    return lax.dot_general(a, b, (((0,), (0,)), ((), ())), preferred_element_type=F32)


def params(*semantics):
    return pltpu.CompilerParams(
        dimension_semantics=semantics, vmem_limit_bytes=VMEM_LIMIT
    )


def whole(shape):
    zeros = (0,) * len(shape)
    return pl.BlockSpec(shape, lambda *_: zeros, pipeline_mode=pl.Buffered(1))


def swap_halves(slab):
    lane = lax.broadcasted_iota(jnp.int32, slab.shape, 1) % HD
    return jnp.where(
        lane < HD // 2, pltpu.roll(slab, LANES - HD // 2, 1), pltpu.roll(slab, HD // 2, 1)
    )


def project_kernel(pairs, q_width, x_ref, gain_ref, w_ref, cos_ref, sin_ref, n_ref, q_ref, kv_ref):
    x = x_ref[...].astype(F32)
    scale = lax.rsqrt(jnp.mean(x * x, axis=1, keepdims=True) + EPSILON)
    normed = (x * scale * gain_ref[...]).astype(BF)
    n_ref[...] = normed
    cosine, sine = cos_ref[...], sin_ref[...]
    raw = nn(normed, w_ref[...])
    for slab in range(q_width // LANES):
        cols = slice(slab * LANES, (slab + 1) * LANES)
        part = raw[:, cols]
        turned = (part * cosine + swap_halves(part) * sine).astype(BF)
        q_ref[:, cols] = (turned.astype(F32) * ATTN_SCALE).astype(BF)
    for pair in range(pairs):
        lo = pair * 2 * LANES
        part = raw[:, q_width + lo : q_width + lo + LANES]
        kv_ref[:, lo : lo + LANES] = (part * cosine + swap_halves(part) * sine).astype(BF)
        kv_ref[:, lo + LANES : lo + 2 * LANES] = raw[
            :, q_width + lo + LANES : q_width + lo + 2 * LANES
        ].astype(BF)


def attend_kernel(blocks, span, prefix_ref, base_ref, q_ref, *refs):
    kv_refs = refs[:blocks]
    out_ref, p_ref = refs[blocks:]
    limit_len = prefix_ref[pl.program_id(0)]
    local = base_ref[0] + lax.broadcasted_iota(jnp.int32, (span, 1), 0)
    limit = jnp.maximum(local + 1, limit_len)
    key_pos = jnp.concatenate(
        [
            base_ref[j] + lax.broadcasted_iota(jnp.int32, (1, span), 1)
            for j in range(blocks)
        ],
        axis=1,
    )
    visible = key_pos < limit
    visible = jnp.concatenate([visible, visible], axis=0)
    for g in range(2):
        keys = jnp.concatenate([r[:, g * HD : (g + 1) * HD] for r in kv_refs], axis=0)
        vals = jnp.concatenate(
            [r[:, LANES + g * HD : LANES + (g + 1) * HD] for r in kv_refs], axis=0
        )
        first, second = 2 * g * HD, (2 * g + 1) * HD
        queries = jnp.concatenate(
            [q_ref[:, first : first + HD], q_ref[:, second : second + HD]], axis=0
        )
        scores = jnp.where(visible, nt(queries, keys), MASKED_SCORE)
        expo = jnp.exp(scores - jnp.max(scores, axis=1, keepdims=True))
        probs = (expo * (1.0 / jnp.sum(expo, axis=1, keepdims=True))).astype(BF)
        p_ref[0, g] = probs
        att = nn(probs, vals).astype(BF)
        out_ref[:, first : first + HD] = att[:span]
        out_ref[:, second : second + HD] = att[span:]


def attend_back_kernel(blocks, span, p_ref, q_ref, g_ref, *refs):
    kv_refs = refs[:blocks]
    dq_ref, own_ref, other_ref = refs[blocks:]
    parts = []
    for g in range(2):
        keys = jnp.concatenate([r[:, g * HD : (g + 1) * HD] for r in kv_refs], axis=0)
        vals = jnp.concatenate(
            [r[:, LANES + g * HD : LANES + (g + 1) * HD] for r in kv_refs], axis=0
        )
        first, second = 2 * g * HD, (2 * g + 1) * HD
        queries = jnp.concatenate(
            [q_ref[:, first : first + HD], q_ref[:, second : second + HD]], axis=0
        )
        grads = jnp.concatenate(
            [g_ref[:, first : first + HD], g_ref[:, second : second + HD]], axis=0
        )
        probs = p_ref[0, g]
        wide = probs.astype(F32)
        grad_probs = nt(grads, vals)
        inner = jnp.sum(wide * grad_probs, axis=1, keepdims=True)
        grad_scores = (wide * (grad_probs - inner)).astype(BF)
        dq = nn(grad_scores, keys) * ATTN_SCALE
        dq_ref[:, first : first + HD] = dq[:span]
        dq_ref[:, second : second + HD] = dq[span:]
        parts.append((nn(queries.T, grad_scores), nn(grads.T, probs)))
    stacked = jnp.concatenate([parts[0][0], parts[1][0], parts[0][1], parts[1][1]], axis=0)
    turned = stacked.T.astype(BF)
    half = blocks // 2
    for j in range(half):
        own_ref[j] = turned[j * span : (j + 1) * span]
        other_ref[j] = turned[(half + j) * span : (half + j + 1) * span]


def middle_kernel(
    a_ref, b_ref, wa_ref, wb_ref, x_ref, gain_ref, router_ref, routes_ref, m_ref, n_ref, nt_ref, g_ref
):
    branch = nt(a_ref[...], wa_ref[...]) + nt(b_ref[...], wb_ref[...])
    middle = x_ref[...].astype(F32) + RESIDUAL_SCALE * branch
    m_ref[...] = middle
    scale = lax.rsqrt(jnp.mean(middle * middle, axis=1, keepdims=True) + EPSILON)
    wide = middle * scale * gain_ref[...]
    normed = wide.astype(BF)
    n_ref[...] = normed
    nt_ref[...] = normed.T
    logits = nn(normed, router_ref[...])
    lane = lax.broadcasted_iota(jnp.int32, logits.shape, 1)
    routes = routes_ref[...]
    routed = lane == routes[:, 0:1]
    for k in range(1, TOP):
        routed = routed | (lane == routes[:, k : k + 1])
    logits = jnp.where(routed, logits, MASKED_SCORE)
    expo = jnp.where(routed, jnp.exp(logits - jnp.max(logits, axis=1, keepdims=True)), 0.0)
    g_ref[...] = expo / jnp.sum(expo, axis=1, keepdims=True)


def moe_kernel(
    first_call,
    column_ref,
    w_ref,
    xa_ref,
    xb_ref,
    xta_ref,
    xtb_ref,
    ya_ref,
    yb_ref,
    yta_ref,
    ytb_ref,
    ga_ref,
    gb_ref,
    *refs,
):
    if first_call:
        accs = refs[:6]
        dw_ref = refs[6]
    else:
        inits, accs = refs[:6], refs[6:12]
        dw_ref = refs[12]

    @pl.when(pl.program_id(0) == 0)
    def _():
        for i in range(6):
            if first_call:
                accs[i][...] = jnp.zeros(accs[i].shape, accs[i].dtype)
            else:
                accs[i][...] = inits[i][...]

    expert = column_ref[0] + pl.program_id(0)
    rows, cols = w_ref.shape[0] * w_ref.shape[2], w_ref.shape[3]
    hid = cols // 3
    weights = w_ref[...].reshape(rows, cols)
    w_gu, w_d = weights[:, : 2 * hid], weights[:, 2 * hid :]
    kept = []
    for x_ref, y_ref, gate_ref, moe_ref, dx_ref, gg_ref in (
        (xa_ref, ya_ref, ga_ref, accs[0], accs[2], accs[4]),
        (xb_ref, yb_ref, gb_ref, accs[1], accs[3], accs[5]),
    ):
        pre = nn(x_ref[...], w_gu)
        back = nn(y_ref[...], w_d)
        gates = gate_ref[...]
        lane = lax.broadcasted_iota(jnp.int32, gates.shape, 1)
        here = lane == expert
        weight = RESIDUAL_SCALE * jnp.sum(jnp.where(here, gates, 0.0), axis=1, keepdims=True)
        gate_pre, up_pre = pre[:, :hid], pre[:, hid:]
        sig = jax.nn.sigmoid(gate_pre)
        act = gate_pre * sig
        hidden = act * up_pre
        pull = RESIDUAL_SCALE * jnp.sum(back * hidden, axis=1, keepdims=True)
        gg_ref[...] += jnp.where(here, pull, 0.0)
        scaled = weight * back
        d_up = scaled * act
        d_gate = scaled * up_pre * (sig + act * (1.0 - sig))
        d_gu = jnp.concatenate([d_gate.astype(BF), d_up.astype(BF)], axis=1)
        mixed = (weight * hidden).astype(BF)
        moe_ref[...] += nt(mixed, w_d)
        dx_ref[...] += nt(d_gu, w_gu)
        kept.append((d_gu, mixed))
    dw_gu = nn(xta_ref[...], kept[0][0]) + nn(xtb_ref[...], kept[1][0])
    dw_d = nn(yta_ref[...], kept[0][1]) + nn(ytb_ref[...], kept[1][1])
    shape = dw_ref.shape[:3]
    dw_ref[:, :, :, : 2 * hid] = dw_gu.astype(BF).reshape(shape + (2 * hid,))
    dw_ref[:, :, :, 2 * hid :] = dw_d.astype(BF).reshape(shape + (hid,))


def middle_back_kernel(
    tp_ref,
    sa_ref,
    sb_ref,
    gga_ref,
    ggb_ref,
    gates_ref,
    m_ref,
    y_ref,
    gain_ref,
    router_ref,
    wo_ref,
    gm_ref,
    branch_ref,
    att_ref,
    logit_ref,
    dgain_ref,
):
    @pl.when(pl.program_id(0) == 0)
    def _():
        dgain_ref[...] = jnp.zeros(dgain_ref.shape, F32)

    gates = gates_ref[...]
    pull = gga_ref[...] + ggb_ref[...]
    weighted = gates * pull
    grad_logits = (weighted - gates * jnp.sum(weighted, axis=1, keepdims=True)).astype(BF)
    logit_ref[...] = grad_logits
    grad = (
        sa_ref[...].astype(F32) + sb_ref[...].astype(F32) + nt(grad_logits, router_ref[...])
    )
    middle = m_ref[...]
    width = middle.shape[1]
    scale = lax.rsqrt(jnp.mean(middle * middle, axis=1, keepdims=True) + EPSILON)
    unit = middle * scale
    dgain_ref[...] += jnp.sum(grad * unit, axis=0, keepdims=True)
    scaled = grad * gain_ref[...]
    inner = jnp.sum(scaled * unit, axis=1, keepdims=True) * (1.0 / width)
    grad_middle = y_ref[...].astype(F32) + scale * (scaled - unit * inner)
    half = width // 2
    gm_ref[...] = jnp.where(tp_ref[0] == 0, grad_middle[:, :half], grad_middle[:, half:])
    branch = (RESIDUAL_SCALE * grad_middle).astype(BF)
    branch_ref[...] = branch
    att_ref[...] = nn(branch, wo_ref[...]).astype(BF)


def project_back_kernel(
    pairs,
    tp_ref,
    dq_ref,
    kva_ref,
    kvb_ref,
    kvc_ref,
    cos_ref,
    sin_ref,
    w_ref,
    x_ref,
    gain_ref,
    d_ref,
    own_ref,
    other_ref,
    dot_ref,
    dgain_ref,
):
    @pl.when(pl.program_id(0) == 0)
    def _():
        dgain_ref[...] = jnp.zeros(dgain_ref.shape, F32)

    cosine, sine = cos_ref[...], sin_ref[...]
    q_width = dq_ref.shape[1]
    for slab in range(q_width // LANES):
        cols = slice(slab * LANES, (slab + 1) * LANES)
        part = dq_ref[:, cols]
        d_ref[:, cols] = (part * cosine - swap_halves(part) * sine).astype(BF)
    kv = kva_ref[...].astype(F32) + kvb_ref[...].astype(F32) + kvc_ref[...].astype(F32)
    for pair in range(pairs):
        lo = pair * 2 * LANES
        part = kv[:, lo : lo + LANES]
        d_ref[:, q_width + lo : q_width + lo + LANES] = (
            part * cosine - swap_halves(part) * sine
        ).astype(BF)
        d_ref[:, q_width + lo + LANES : q_width + lo + 2 * LANES] = kv[
            :, lo + LANES : lo + 2 * LANES
        ].astype(BF)
    grad = nt(d_ref[...], w_ref[...])
    x = x_ref[...].astype(F32)
    width = x.shape[1]
    scale = lax.rsqrt(jnp.mean(x * x, axis=1, keepdims=True) + EPSILON)
    unit = x * scale
    dgain_ref[...] += jnp.sum(grad * unit, axis=0, keepdims=True)
    scaled = grad * gain_ref[...]
    inner = jnp.sum(scaled * unit, axis=1, keepdims=True) * (1.0 / width) * scale * scale
    dot_ref[...] = jnp.broadcast_to(inner, dot_ref.shape)
    scaled = scaled * scale
    half = width // 2
    is_first = tp_ref[0] == 0
    own_ref[...] = jnp.where(is_first, scaled[:, :half], scaled[:, half:])
    other_ref[...] = jnp.where(is_first, scaled[:, half:], scaled[:, :half]).astype(BF)


class Ring:
    def __init__(self, wide, ctx):
        self.wide, self.ctx, self.deep = wide, ctx, ctx // 2
        self.size = wide * self.deep
        deep = self.deep
        order = [
            (f, y)
            for y in range(deep)
            for f in (range(wide) if y % 2 == 0 else range(wide - 1, -1, -1))
        ]
        flat = [[f * ctx + y * 2 + c for f, y in order] for c in range(2)]
        n = self.size
        self.forward = [(row[i], row[(i + 1) % n]) for row in flat for i in range(n)]
        self.backward = [(b, a) for a, b in self.forward]
        f, c = lax.axis_index("fsdp"), lax.axis_index("ctx")
        y = c // 2
        self.place = y * wide + jnp.where(y % 2 == 0, f, wide - 1 - f)

    def chip(self, offset):
        place = (self.place + offset) % self.size
        y, q = place // self.wide, place % self.wide
        f = jnp.where(y % 2 == 0, q, self.wide - 1 - q)
        return f * self.deep + y

    def send(self, array, forward=True):
        return lax.ppermute(array, RING, self.forward if forward else self.backward)

    def gather(self, block):
        n, rows = self.size, block.shape[1]
        half = rows // 2
        full = jnp.zeros((n,) + block.shape, block.dtype)

        def put(full, part, offset, row):
            return lax.dynamic_update_slice(full, part[None], (self.chip(offset), 0, row, 0))

        full = put(full, block, 0, 0)
        ahead = back = block
        for step in range(1, n // 2):
            ahead, back = self.send(ahead), self.send(back, False)
            full = put(full, ahead, -step, 0)
            full = put(full, back, step, 0)
        ahead = self.send(ahead[:, :half])
        back = self.send(back[:, half:], False)
        full = put(full, ahead, -(n // 2), 0)
        return put(full, back, n // 2, half)

    def scatter(self, full):
        n, rows = self.size, full.shape[2]
        half = rows // 2

        def part(offset):
            return lax.dynamic_index_in_dim(full, self.chip(offset), 0, keepdims=False)

        far = n // 2
        opposite = part(far)
        ahead = self.send(opposite[:, :half])
        back = self.send(opposite[:, half:], False)
        for step in range(far - 1, 0, -1):
            near, behind = part(step), part(-step)
            if step == far - 1:
                ahead = jnp.concatenate([near[:, :half] + ahead, near[:, half:]], axis=1)
                back = jnp.concatenate([behind[:, :half], behind[:, half:] + back], axis=1)
            else:
                ahead, back = near + ahead, behind + back
            ahead, back = self.send(ahead), self.send(back, False)
        return part(0).astype(F32) + ahead.astype(F32) + back.astype(F32)


def per_device(
    tokens,
    prefix,
    routes,
    w_query,
    w_key,
    w_value,
    w_out,
    w_router,
    gain_attn,
    gain_ffn,
    w_gate,
    w_up,
    w_down,
    cotangent,
):
    wide, ctx = lax.axis_size("fsdp"), lax.axis_size("ctx")
    seqs, span, feature = tokens.shape
    rows = seqs * span
    width = 2 * feature
    shard = w_query.shape[0]
    experts = w_router.shape[1]
    per_core = experts // 2
    group = per_core // GROUPS
    hid = w_gate.shape[2]
    q_width, kv_width = w_query.shape[1], w_key.shape[1]
    pairs = kv_width // LANES
    deep = ctx // 2
    tp, c = lax.axis_index("tp"), lax.axis_index("ctx")
    core, y = c % 2, c // 2
    ring = Ring(wide, ctx)
    n = ring.size
    core_perm = [(i, i ^ 1) for i in range(ctx)]
    swap_core = lambda a: lax.ppermute(a, "ctx", core_perm)
    swap_tp = lambda a: lax.ppermute(a, "tp", [(0, 1), (1, 0)])
    up_y = [(i, (i + 2) % ctx) for i in range(ctx)]
    down_y = [(i, (i - 2) % ctx) for i in range(ctx)]
    tp_scalar = tp.astype(jnp.int32).reshape(1)

    def by_core(mine, other, axis):
        return jnp.where(
            core == 0,
            jnp.concatenate([mine, other], axis),
            jnp.concatenate([other, mine], axis),
        )

    def by_tp(mine, other):
        return jnp.where(
            tp == 0, jnp.concatenate([mine, other], 1), jnp.concatenate([other, mine], 1)
        )

    kv_cols = []
    for pair in range(pairs):
        cols = slice(pair * LANES, (pair + 1) * LANES)
        kv_cols += [w_key[:, cols], w_value[:, cols]]
    small = jnp.concatenate([w_router, gain_attn[:, None], gain_ffn[:, None]], axis=1)
    small = jnp.pad(small, ((0, 0), (0, LANES - experts - 2)))
    bundle = jnp.concatenate([w_query, *kv_cols, w_out.T, small], axis=1)
    own_tokens = tokens.reshape(rows, feature)
    own_cot = cotangent.reshape(rows, feature)
    other_tokens = swap_tp(own_tokens)
    mine = ring.gather(bundle[None])[:, 0]
    theirs = swap_core(mine)
    bundle_full = by_core(mine[:, None], theirs[:, None], 1).reshape(width, -1)
    qkv_width = q_width + 2 * kv_width
    w_qkv = bundle_full[:, :qkv_width]
    wo_mine = bundle_full[:, qkv_width : qkv_width + q_width]
    w_small = bundle_full[:, qkv_width + q_width :]
    router = jnp.where(jnp.arange(LANES)[None, :] < experts, w_small, 0).astype(BF)
    gain_one = w_small[:, experts].astype(F32)[None, :]
    gain_two = w_small[:, experts + 1].astype(F32)[None, :]
    wo_other = swap_tp(wo_mine)

    packed = jnp.concatenate([w_gate, w_up, w_down.transpose(0, 2, 1)], axis=2)
    packed = packed.reshape(2, per_core, shard, 3 * hid)
    mine_w = lax.dynamic_index_in_dim(packed, core, 0, keepdims=False)
    other_w = swap_core(lax.dynamic_index_in_dim(packed, 1 - core, 0, keepdims=False))
    chip_w = by_core(mine_w, other_w, 1)
    group_w = [
        ring.gather(chip_w[i * group : (i + 1) * group]) for i in range(GROUPS)
    ]

    full_tokens = by_tp(own_tokens, other_tokens)
    half_width = HD // 2
    freqs = 10000.0 ** (-jnp.arange(half_width, dtype=F32) / half_width)
    local_pos = c * span + jnp.arange(span, dtype=jnp.int32)
    angles = local_pos.astype(F32)[:, None] * freqs[None, :]
    cosine, sine = jnp.cos(angles), jnp.sin(angles)
    cosine = jnp.tile(jnp.concatenate([cosine] * 4, axis=1), (seqs, 1))
    sine = jnp.tile(jnp.concatenate([-sine, sine, -sine, sine], axis=1), (seqs, 1))
    step_rows = min(rows, 256)
    steps = rows // step_rows
    row_spec = lambda cols: pl.BlockSpec((step_rows, cols), lambda i, *_: (i, 0))
    smem = pl.BlockSpec(memory_space=pltpu.SMEM)
    normed, queries, kv = pl.pallas_call(
        functools.partial(project_kernel, pairs, q_width),
        grid=(steps,),
        in_specs=[
            row_spec(width),
            whole((1, width)),
            whole((width, qkv_width)),
            row_spec(LANES),
            row_spec(LANES),
        ],
        out_specs=[row_spec(width), row_spec(q_width), row_spec(2 * kv_width)],
        out_shape=[
            jax.ShapeDtypeStruct((rows, width), BF),
            jax.ShapeDtypeStruct((rows, q_width), BF),
            jax.ShapeDtypeStruct((rows, 2 * kv_width), BF),
        ],
        compiler_params=params("arbitrary"),
        name="project",
    )(full_tokens, gain_one, w_qkv, cosine, sine)

    own_side = [kv]
    for _ in range(deep - 1):
        own_side.append(lax.ppermute(own_side[-1], "ctx", up_y))
    other_side = [swap_core(block) for block in own_side]
    kv_blocks = own_side + other_side
    base = jnp.stack(
        [(((y - k) % deep) * 2 + core) * span for k in range(deep)]
        + [(((y - k) % deep) * 2 + 1 - core) * span for k in range(deep)]
    ).astype(jnp.int32)
    length = ctx * span
    head_spec = lambda *_: pl.BlockSpec((span, 2 * LANES), lambda s, p, *_: (s, p))
    prob_spec = pl.BlockSpec((1, 2, 2 * span, length), lambda s, p, *_: (s, p, 0, 0))
    attended, probs = pl.pallas_call(
        functools.partial(attend_kernel, ctx, span),
        grid_spec=pltpu.PrefetchScalarGridSpec(
            num_scalar_prefetch=2,
            grid=(seqs, pairs),
            in_specs=[head_spec()] * (1 + ctx),
            out_specs=[head_spec(), prob_spec],
        ),
        out_shape=[
            jax.ShapeDtypeStruct((rows, q_width), BF),
            jax.ShapeDtypeStruct((seqs, 2 * pairs, 2 * span, length), BF),
        ],
        compiler_params=params("arbitrary", "arbitrary"),
        name="attend",
    )(prefix, base, queries, *kv_blocks)
    attended_other = swap_tp(attended)

    full_cot = by_tp(own_cot, swap_tp(own_cot))
    peer_cot = swap_core(full_cot)
    cot_t, peer_cot_t = full_cot.T, peer_cot.T

    route_rows = routes.reshape(rows, TOP)
    middle, normed_two, normed_two_t, gates = pl.pallas_call(
        middle_kernel,
        grid=(steps,),
        in_specs=[
            row_spec(q_width),
            row_spec(q_width),
            whole((width, q_width)),
            whole((width, q_width)),
            row_spec(width),
            whole((1, width)),
            whole((width, LANES)),
            row_spec(TOP),
        ],
        out_specs=[
            row_spec(width),
            row_spec(width),
            pl.BlockSpec((width, step_rows), lambda i: (0, i)),
            row_spec(LANES),
        ],
        out_shape=[
            jax.ShapeDtypeStruct((rows, width), F32),
            jax.ShapeDtypeStruct((rows, width), BF),
            jax.ShapeDtypeStruct((width, rows), BF),
            jax.ShapeDtypeStruct((rows, LANES), F32),
        ],
        compiler_params=params("arbitrary"),
        name="middle",
    )(attended, attended_other, wo_mine, wo_other, full_tokens, gain_two, router, route_rows)

    peer_two, peer_two_t, peer_gates = (
        swap_core(normed_two),
        swap_core(normed_two_t),
        swap_core(gates),
    )
    acc_shapes = [jax.ShapeDtypeStruct((rows, width), F32)] * 4 + [
        jax.ShapeDtypeStruct((rows, LANES), F32)
    ] * 2
    acc_specs = [whole((rows, width))] * 4 + [whole((rows, LANES))] * 2
    chip_rows = 2 * shard
    w_spec = pl.BlockSpec((n, 1, chip_rows, 3 * hid), lambda e, *_: (0, e, 0, 0))
    accs = ()
    shards = []
    for i in range(GROUPS):
        column = (core * per_core + i * group).astype(jnp.int32).reshape(1)
        *accs, grads = pl.pallas_call(
            functools.partial(moe_kernel, i == 0),
            grid=(group,),
            in_specs=[smem, w_spec]
            + [whole((rows, width))] * 2
            + [whole((width, rows))] * 2
            + [whole((rows, width))] * 2
            + [whole((width, rows))] * 2
            + [whole((rows, LANES))] * 2
            + (acc_specs if i else []),
            out_specs=acc_specs + [w_spec],
            out_shape=acc_shapes
            + [jax.ShapeDtypeStruct((n, group, chip_rows, 3 * hid), BF)],
            compiler_params=params("arbitrary"),
            name="experts",
        )(
            column,
            group_w[i],
            normed_two,
            peer_two,
            normed_two_t,
            peer_two_t,
            full_cot,
            peer_cot,
            cot_t,
            peer_cot_t,
            gates,
            peer_gates,
            *accs,
        )
        shards.append(ring.scatter(grads))
    moe, moe_peer, grad_two, grad_two_peer, pull, pull_peer = accs

    part = (grad_two + swap_core(grad_two_peer.astype(BF)).astype(F32)).astype(BF)
    part_other = swap_tp(part)
    pull_mine = pull + swap_core(pull_peer)
    pull_other = swap_tp(pull_mine)
    grad_middle, grad_branch, grad_attended, grad_logits, gain_two_term = pl.pallas_call(
        middle_back_kernel,
        grid=(steps,),
        in_specs=[
            smem,
            row_spec(width),
            row_spec(width),
            row_spec(LANES),
            row_spec(LANES),
            row_spec(LANES),
            row_spec(width),
            row_spec(width),
            whole((1, width)),
            whole((width, LANES)),
            whole((width, q_width)),
        ],
        out_specs=[
            row_spec(feature),
            row_spec(width),
            row_spec(q_width),
            row_spec(LANES),
            whole((1, width)),
        ],
        out_shape=[
            jax.ShapeDtypeStruct((rows, feature), F32),
            jax.ShapeDtypeStruct((rows, width), BF),
            jax.ShapeDtypeStruct((rows, q_width), BF),
            jax.ShapeDtypeStruct((rows, LANES), BF),
            jax.ShapeDtypeStruct((1, width), F32),
        ],
        compiler_params=params("arbitrary"),
        name="middle_back",
    )(
        tp_scalar,
        part,
        part_other,
        pull_mine,
        pull_other,
        gates,
        middle,
        full_cot,
        gain_two,
        router,
        wo_mine,
    )

    moe_sum = moe + swap_core(moe_peer.astype(BF)).astype(F32)
    moe_halves = moe_sum.reshape(rows, 2, feature)
    moe_own = lax.dynamic_index_in_dim(moe_halves, tp, 1, keepdims=False)
    moe_send = lax.dynamic_index_in_dim(moe_halves, 1 - tp, 1, keepdims=False).astype(BF)
    middle_own = lax.dynamic_index_in_dim(
        middle.reshape(rows, 2, feature), tp, 1, keepdims=False
    )
    output = (middle_own + moe_own + swap_tp(moe_send).astype(F32)).astype(BF)

    back_spec = pl.BlockSpec((deep, span, 2 * LANES), lambda s, p: (0, s, p))
    grad_q, grad_kv_own, grad_kv_peer = pl.pallas_call(
        functools.partial(attend_back_kernel, ctx, span),
        grid=(seqs, pairs),
        in_specs=[prob_spec] + [head_spec()] * (2 + ctx),
        out_specs=[head_spec(), back_spec, back_spec],
        out_shape=[
            jax.ShapeDtypeStruct((rows, q_width), F32),
            jax.ShapeDtypeStruct((deep, rows, 2 * kv_width), BF),
            jax.ShapeDtypeStruct((deep, rows, 2 * kv_width), BF),
        ],
        compiler_params=params("arbitrary", "arbitrary"),
        name="attend_back",
    )(probs, queries, grad_attended, *kv_blocks)
    from_peer = swap_core(grad_kv_peer)
    travel = None
    for k in range(deep - 1, 0, -1):
        piece = grad_kv_own[k] + from_peer[k]
        if travel is not None:
            piece = piece + travel
        travel = lax.ppermute(piece, "ctx", down_y)

    grad_qkv, grad_own, grad_send, inner, gain_one_term = pl.pallas_call(
        functools.partial(project_back_kernel, pairs),
        grid=(steps,),
        in_specs=[
            smem,
            row_spec(q_width),
            row_spec(2 * kv_width),
            row_spec(2 * kv_width),
            row_spec(2 * kv_width),
            row_spec(LANES),
            row_spec(LANES),
            whole((width, qkv_width)),
            row_spec(width),
            whole((1, width)),
        ],
        out_specs=[
            row_spec(qkv_width),
            row_spec(feature),
            row_spec(feature),
            row_spec(LANES),
            whole((1, width)),
        ],
        out_shape=[
            jax.ShapeDtypeStruct((rows, qkv_width), BF),
            jax.ShapeDtypeStruct((rows, feature), F32),
            jax.ShapeDtypeStruct((rows, feature), BF),
            jax.ShapeDtypeStruct((rows, LANES), F32),
            jax.ShapeDtypeStruct((1, width), F32),
        ],
        compiler_params=params("arbitrary"),
        name="project_back",
    )(
        tp_scalar,
        grad_q,
        grad_kv_own[0],
        from_peer[0],
        travel if travel is not None else jnp.zeros_like(kv),
        cosine,
        sine,
        w_qkv,
        full_tokens,
        gain_one,
    )
    dots = inner[:, 0]
    dots = dots + swap_tp(dots)
    grad_tokens = (
        grad_middle
        + grad_own
        + swap_tp(grad_send).astype(F32)
        - own_tokens.astype(F32) * dots[:, None]
    )

    def scatter_rows(array):
        parts = array.astype(BF).reshape(n, 2, shard, array.shape[1])
        kept = lax.dynamic_index_in_dim(parts, core, 1)
        sent = swap_core(lax.dynamic_index_in_dim(parts, 1 - core, 1))
        return ring.scatter(kept + sent)[0]

    out_term = tn(grad_branch, attended)
    router_term = tn(normed_two, grad_logits)[:, :experts]
    early = jnp.concatenate([out_term, router_term, gain_two_term.T], axis=1)
    early = jnp.pad(early, ((0, 0), (0, LANES - experts - 1)))
    early = scatter_rows(early)
    late = jnp.concatenate([tn(normed, grad_qkv), gain_one_term.T], axis=1)
    late = jnp.pad(late, ((0, 0), (0, LANES - 1)))
    late = scatter_rows(late)
    grad_out = early[:, :q_width].T
    grad_router = early[:, q_width : q_width + experts]
    grad_gain_ffn = early[:, q_width + experts]
    grad_query = late[:, :q_width]
    key_cols, value_cols = [], []
    for pair in range(pairs):
        lo = q_width + pair * 2 * LANES
        key_cols.append(late[:, lo : lo + LANES])
        value_cols.append(late[:, lo + LANES : lo + 2 * LANES])
    grad_key = jnp.concatenate(key_cols, axis=1)
    grad_value = jnp.concatenate(value_cols, axis=1)
    gain_half = late[:, qkv_width]
    grad_gain_attn = gain_half + swap_tp(gain_half)

    sums = jnp.concatenate(shards, axis=0).reshape(per_core, 2, shard, 3 * hid)
    kept = lax.dynamic_index_in_dim(sums, core, 1, keepdims=False).astype(BF)
    sent = swap_core(lax.dynamic_index_in_dim(sums, 1 - core, 1, keepdims=False).astype(BF))
    all_experts = by_core(kept, sent, 0).astype(F32)
    grad_gate = all_experts[:, :, :hid]
    grad_up = all_experts[:, :, hid : 2 * hid]
    grad_down = all_experts[:, :, 2 * hid :].transpose(0, 2, 1)

    return (
        output.reshape(seqs, span, feature),
        grad_tokens.reshape(seqs, span, feature),
        grad_query,
        grad_key,
        grad_value,
        grad_out,
        grad_router,
        grad_gain_attn,
        grad_gain_ffn,
        grad_gate,
        grad_up,
        grad_down,
    )


def solution(mesh):
    in_specs = (
        P("fsdp", "ctx", "tp"),
        P("fsdp"),
        P("ctx", "fsdp", None, None),
        P(("fsdp", "ctx"), "tp"),
        P(("fsdp", "ctx"), "tp"),
        P(("fsdp", "ctx"), "tp"),
        P("tp", ("fsdp", "ctx")),
        P(("fsdp", "ctx"), None),
        P(("fsdp", "ctx")),
        P(("fsdp", "ctx")),
        P(None, ("fsdp", "ctx"), "tp"),
        P(None, ("fsdp", "ctx"), "tp"),
        P(None, "tp", ("fsdp", "ctx")),
        P("fsdp", "ctx", "tp"),
    )
    out_specs = (
        P("fsdp", "ctx", "tp"),
        P("fsdp", "ctx", "tp"),
        P(("fsdp", "ctx"), "tp"),
        P(("fsdp", "ctx"), "tp"),
        P(("fsdp", "ctx"), "tp"),
        P("tp", ("fsdp", "ctx")),
        P(("fsdp", "ctx"), None),
        P(("fsdp", "ctx")),
        P(("fsdp", "ctx")),
        P(None, ("fsdp", "ctx"), "tp"),
        P(None, ("fsdp", "ctx"), "tp"),
        P(None, "tp", ("fsdp", "ctx")),
    )
    return jax.shard_map(
        per_device, mesh=mesh, in_specs=in_specs, out_specs=out_specs, check_vma=False
    )
```

time: 2580 us -> 589 us (0.23)
  waiting for transfers between devices: 1110 us -> 151 us
  local copies, waits for them, and re-layouts: 556 us -> 117 us
  matrix products: 423 us -> 5.83 us
  other arithmetic: 313 us -> 63.3 us
  blocking collectives: 137 us -> 0 us
  Pallas kernels: 0 us -> 126 us
  starting transfers between devices: 1.14 us -> 113 us
    reduce_scatter x9 -> x0, waiting for transfers between devices: 780 us -> none  [the longest x1 183 us: per_device(): lax.psum_scatter(down_terms, ('fsdp', 'ctx'), scatter_dimension=2, tiled=...]
    dot_general x172 -> x3, matrix products: 421 us -> 5.83 us  [tn(): lax.dot_general(a, b, (((0,), (0,)), ((), ())), preferred_element_type=F32)]
    scatter-add x32 -> x0, other arithmetic: 250 us -> none  [the longest x16 129 us: expert_backward(): totals.at[token_ids].add(picked_grad)]
    all_gather x9 -> x0, waiting for transfers between devices: 226 us -> none  [the longest x1 75.5 us: per_device(): lax.all_gather(w_up, ('fsdp', 'ctx'), axis=1, tiled=True)]
    gather x66 -> x0, local copies, waits for them, and re-layouts: 225 us -> none  [the longest x16 45.1 us: expert_backward(): picked = normed_two[token_ids]]
    unnamed x145 -> x114, local copies, waits for them, and re-layouts: 214 us -> 16 us
    ppermute x0 -> x115, waiting for transfers between devices: none -> 151 us  [the longest x88 111 us: send(): return lax.ppermute(array, RING, self.forward if forward else self.backward)]
    pallas_call x0 -> x10, Pallas kernels: none -> 126 us  [the longest x4 76.2 us: per_device(): pl.pallas_call(functools.partial(moe_kernel, i == 0), grid=(group,), in_s...]
  transfers between devices with their start and end apart: 23 -> 115, of which waited for: 19 -> 51; matrix products, arithmetic and copies ran while one was open for 9% -> 29% of each run, Pallas kernels for 0% -> 15%
where the time goes in v1:
time: 589 us; the launch traced here: 578 us
  waiting for transfers between devices  151 us (26%)
  Pallas kernels  126 us (21%)
  local copies, waits for them, and re-layouts  117 us (20%)
  starting transfers between devices  113 us (19%)
  other arithmetic  63.3 us (11%)
    ppermute x88, waiting for transfers between devices, send(): return lax.ppermute(array, RING, self.forward if forward else self.backward)  111 us
    ppermute x88, starting transfers between devices, send(): return lax.ppermute(array, RING, self.forward if forward else self.backward)  100 us
    pallas_call x4, Pallas kernels, per_device(): pl.pallas_call(functools.partial(moe_kernel, i == 0), grid=(group,), in_s...  76.2 us
    dynamic_update_slice x44, local copies, waits for them, and re-layouts, put(): lax.dynamic_update_slice(full, part[None], (self.chip(offset), 0, row, 0))  50.5 us
    ppermute x10, waiting for transfers between devices, per_device(): swap_tp = lambda a: lax.ppermute(a, 'tp', [(0, 1), (1, 0)])  25.4 us
    add x18, other arithmetic, scatter(): ahead, back = (near + ahead, behind + back)  20.2 us
    unnamed x114, local copies, waits for them, and re-layouts  16 us
    pallas_call x1, Pallas kernels, per_device(): pl.pallas_call(functools.partial(attend_kernel, ctx, span), grid_spec=plt...  13.7 us
  transfers between devices with their start and end apart: 115, of which 51 were waited for; matrix products, arithmetic and copies ran while one was open for 29% of the time, Pallas kernels for 15%

profile of v1, /device:TPU:0, one launch (start us, length us, event | category | flops | bytes accessed | tf_op | source)
XLA Modules:
  0.0 578.5 jit_solution(13277107301898472661)
XLA Ops:
  6.1 3.1 collective-permute-start.1
  21.0 3.7 collective-permute-done.3
  29.9 7.7 %collective-permute-done.26 = bf16[512,512]{1,0:T(8,128)(2,1)} collective-permute-done((bf16[512,512]{1,0:T(8,128)(2,1)}, bf16[512,512]{1,0:T(8,128)(2,1)}, u32[]{:S(2)}, u32[]{:S(2)}) %collective-permute-start.26) | collective-permute-done | bytes 524320 | tf_op jit(solution)/shard_map/ppermute | solution.py:433
  71.2 4.3 collective-permute-done.37
  80.1 3.7 collective-permute-done.16
  88.2 4.0 collective-permute-done.29
  152.1 4.7 project.1
  168.4 3.5 collective-permute-done.10.refs_1_
  190.8 13.7 %attend.1 = (bf16[512,512]{1,0:T(8,128)(2,1)}, bf16[2,4,512,1024]{3,2,1,0:T(8,128)(2,1)}) custom-call(s32[2]{0:T(128)} %prefix_ref.1, s32[4]{0:T(128)} %pad_add_fusion.base_ref, bf16[512,512]{1,0:T(8,128)(2,1)} %get-tuple-element.62.q_ref, bf16[512,512]{1,0:T(8,128)(2,1)} %get-tuple-element.63.refs_0_, bf16[512,512]{1,0:T(8,128)(2,1)} %copy-done.14, ...), custom_call_target="tpu_custom_call" | custom-call | tf_op jit(solution)/shard_map/attend/pallas_call | solution.py:525
  212.7 5.2 collective-permute-done.13.b_ref
  218.6 5.7 middle.1
  230.5 4.0 reshape.169
  238.5 16.3 %experts.4 = (f32[512,1024]{1,0:T(8,128)}, f32[512,1024]{1,0:T(8,128)}, f32[512,1024]{1,0:T(8,128)}, f32[512,1024]{1,0:T(8,128)}, f32[512,128]{1,0:T(8,128)}, /*...) custom-call(s32[1]{0:T(128)} %bitcast.61.column_ref, ...), custom_call_target="tpu_custom_call" | custom-call | tf_op jit(solution)/shard_map/experts/pallas_call | solution.py:591
  254.8 20.2 %experts.5 = (f32[512,1024]{1,0:T(8,128)}, f32[512,1024]{1,0:T(8,128)}, f32[512,1024]{1,0:T(8,128)}, f32[512,1024]{1,0:T(8,128)}, f32[512,128]{1,0:T(8,128)}, /*...) custom-call(s32[1]{0:T(128)} %bitcast.51.column_ref, ...), custom_call_target="tpu_custom_call" | custom-call | tf_op jit(solution)/shard_map/experts/pallas_call | solution.py:591
  283.3 19.7 %experts.6 = (f32[512,1024]{1,0:T(8,128)}, f32[512,1024]{1,0:T(8,128)}, f32[512,1024]{1,0:T(8,128)}, f32[512,1024]{1,0:T(8,128)}, f32[512,128]{1,0:T(8,128)}, /*...) custom-call(s32[1]{0:T(128)} %bitcast.41.column_ref, bf16[8,2,128,768]{3,2,1,0:T(8,128)(2,1)} %get-tuple-element.252.w_ref, ...), custom_call_target="tpu_custom_call" | custom-call | tf_op jit(solution)/shard_map/experts/pallas_call | solution.py:591
  306.1 19.9 %experts.7 = (f32[512,1024]{1,0:T(8,128)}, f32[512,1024]{1,0:T(8,128)}, f32[512,1024]{1,0:T(8,128)}, f32[512,1024]{1,0:T(8,128)}, f32[512,128]{1,0:T(8,128)}, /*...) custom-call(s32[1]{0:T(128)} %bitcast.24.column_ref, bf16[8,2,128,768]{3,2,1,0:T(8,128)(2,1)} %get-tuple-element.253.w_ref, ...), custom_call_target="tpu_custom_call" | custom-call | tf_op jit(solution)/shard_map/experts/pallas_call | solution.py:591
  343.6 7.4 %collective-permute-done.83 = bf16[2,128,768]{2,1,0:T(8,128)(2,1)S(1)} collective-permute-done((bf16[2,128,768]{2,1,0:T(8,128)(2,1)S(1)}, bf16[2,128,768]{2,1,0:T(8,128)(2,1)S(1)}, u32[]{:S(2)}, u32[]{:S(2)}) %collective-permute-start.83) | collective-permute-done | bytes 393248 | tf_op jit(solution)/shard_map/ppermute | solution.py:356
  353.0 6.4 %collective-permute-done.91 = bf16[2,128,768]{2,1,0:T(8,128)(2,1)S(1)} collective-permute-done((bf16[2,128,768]{2,1,0:T(8,128)(2,1)S(1)}, bf16[2,128,768]{2,1,0:T(8,128)(2,1)S(1)}, u32[]{:S(2)}, u32[]{:S(2)}) %collective-permute-start.91) | collective-permute-done | bytes 393248 | tf_op jit(solution)/shard_map/ppermute | solution.py:356
  361.4 6.4 %collective-permute-done.99 = bf16[2,128,768]{2,1,0:T(8,128)(2,1)S(1)} collective-permute-done((bf16[2,128,768]{2,1,0:T(8,128)(2,1)S(1)}, bf16[2,128,768]{2,1,0:T(8,128)(2,1)S(1)}, u32[]{:S(2)}, u32[]{:S(2)}) %collective-permute-start.99) | collective-permute-done | bytes 393248 | tf_op jit(solution)/shard_map/ppermute | solution.py:356
  369.8 6.4 %collective-permute-done.107 = bf16[2,128,768]{2,1,0:T(8,128)(2,1)S(1)} collective-permute-done((bf16[2,128,768]{2,1,0:T(8,128)(2,1)S(1)}, bf16[2,128,768]{2,1,0:T(8,128)(2,1)S(1)}, u32[]{:S(2)}, u32[]{:S(2)}) %collective-permute-start.107) | collective-permute-done | bytes 393248 | tf_op jit(solution)/shard_map/ppermute | solution.py:356
  378.3 6.3 %collective-permute-done.84 = bf16[2,128,768]{2,1,0:T(8,128)(2,1)S(1)} collective-permute-done((bf16[2,128,768]{2,1,0:T(8,128)(2,1)S(1)}, bf16[2,128,768]{2,1,0:T(8,128)(2,1)S(1)}, u32[]{:S(2)}, u32[]{:S(2)}) %collective-permute-start.84) | collective-permute-done | bytes 393248 | tf_op jit(solution)/shard_map/ppermute | solution.py:356
  388.9 4.2 collective-permute-done.92
  396.1 5.4 collective-permute-done.100
  405.6 4.3 collective-permute-done.108
  418.2 3.2 reshape.176
  433.2 3.6 collective-permute-done.112
  445.0 3.9 collective-permute-done.89
  458.4 7.9 %collective-permute-done.58.ggb_ref = f32[512,128]{1,0:T(8,128)S(1)} collective-permute-done((f32[512,128]{1,0:T(8,128)S(1)}, f32[512,128]{1,0:T(8,128)S(1)}, u32[]{:S(2)}, u32[]{:S(2)}) %collective-permute-start.58) | collective-permute-done | bytes 262176 | tf_op jit(solution)/shard_map/ppermute | solution.py:433
  469.1 6.0 %middle_back.1 = (f32[512,512]{1,0:T(8,128)}, bf16[512,1024]{1,0:T(8,128)(2,1)}, bf16[512,512]{1,0:T(8,128)(2,1)}, bf16[512,128]{1,0:T(8,128)(2,1)}, f32[1,1024]{1,0:T(1,128)}) custom-call(s32[1]{0:T(128)} %bitcast.74.tp_ref, bf16[512,1024]{1,0:T(8,128)(2,1)} %add_convert_fusion.sa_ref, bf16[512,1024]{1,0:T(8,128)(2,1)} %copy-done.25, ...), custom_call_target="tpu_custom_call" | custom-call | tf_op jit(solution)/shard_map/middle_back/pallas_call | solution.py:628
  481.7 13.3 %attend_back.1 = (f32[512,512]{1,0:T(8,128)}, bf16[2,512,512]{2,1,0:T(8,128)(2,1)}, bf16[2,512,512]{2,1,0:T(8,128)(2,1)}) custom-call(bf16[2,4,512,1024]{3,2,1,0:T(8,128)(2,1)} %get-tuple-element.94.p_ref, bf16[512,512]{1,0:T(8,128)(2,1)} %get-tuple-element.62.q_ref, bf16[512,512]{1,0:T(8,128)(2,1)} %get-tuple-element.95.g_ref, ...), custom_call_target="tpu_custom_call" | custom-call | tf_op jit(solution)/shard_map/attend_back/pallas_call | solution.py:684
  505.9 11.4 %collective-permute-done.60.kvc_ref = bf16[512,512]{1,0:T(8,128)(2,1)S(1)} collective-permute-done((bf16[512,512]{1,0:T(8,128)(2,1)S(1)}, bf16[512,512]{1,0:T(8,128)(2,1)S(1)}, u32[]{:S(2)}, u32[]{:S(2)}) %collective-permute-start.60) | collective-permute-done | bytes 524320 | tf_op jit(solution)/shard_map/ppermute | solution.py:703
  518.1 6.2 %project_back.1 = (bf16[512,1024]{1,0:T(8,128)(2,1)}, f32[512,512]{1,0:T(8,128)}, bf16[512,512]{1,0:T(8,128)(2,1)}, f32[512,128]{1,0:T(8,128)}, f32[1,1024]{1,0:T(1,128)}) custom-call(s32[1]{0:T(128)} %bitcast.74.tp_ref, f32[512,512]{1,0:T(8,128)} %get-tuple-element.96.dq_ref, bf16[512,512]{1,0:T(8,128)(2,1)} %get-tuple-element.199.kva_ref, ...), custom_call_target="tpu_custom_call" | custom-call | tf_op jit(solution)/shard_map/project_back/pallas_call | solution.py:705
  (508 shorter events, 334.2 us)
Async XLA Ops:
  11.7 41.1 %collective-permute-start.15 = (bf16[8,64,768]{2,1,0:T(8,128)(2,1)}, bf16[8,64,768]{2,1,0:T(8,128)(2,1)}, u32[]{:S(2)}, u32[]{:S(2)}) collective-permute-start(bf16[8,64,768]{2,1,0:T(8,128)(2,1)} %get-tuple-element.192), channel_id=1, source_target_pairs={{0,2},{2,0},{4,6},{6,4},{1,3},{3,1},{5,7},{7,5},{8,10},{10,8},{12,... | collective-permute-start | bytes 2359304 | tf_op jit(solution)/shard_map/ppermute | solution.py:432
  11.7 29.1 %collective-permute-start = (bf16[512,512]{1,0:T(8,128)(2,1)S(1)}, bf16[512,512]{1,0:T(8,128)(2,1)}, u32[]{:S(2)}, u32[]{:S(2)}) collective-permute-start(bf16[512,512]{1,0:T(8,128)(2,1)S(1)} %bitcast.292), channel_id=1, source_target_pairs={{0,1},{1,0},{2,3},{3,2},{4,5},{5,4},{6,7},{7,6},{8,9},{9,8},{10,11... | collective-permute-start | bytes 1572872 | tf_op jit(solution)/shard_map/ppermute | solution.py:433
  13.7 23.9 %collective-permute-start.26 = (bf16[512,512]{1,0:T(8,128)(2,1)}, bf16[512,512]{1,0:T(8,128)(2,1)}, u32[]{:S(2)}, u32[]{:S(2)}) collective-permute-start(bf16[512,512]{1,0:T(8,128)(2,1)} %bitcast.38), channel_id=1, source_target_pairs={{0,1},{1,0},{2,3},{3,2},{4,5},{5,4},{6,7},{7,6},{8,9},{9,8},{10,11... | collective-permute-start | bytes 1572872 | tf_op jit(solution)/shard_map/ppermute | solution.py:433
  39.5 57.1 %collective-permute-start.27 = (bf16[512,1024]{1,0:T(8,128)(2,1)S(1)}, bf16[512,1024]{1,0:T(8,128)(2,1)S(1)}, u32[]{:S(2)}, u32[]{:S(2)}) collective-permute-start(bf16[512,1024]{1,0:T(8,128)(2,1)S(1)} %maximum_select_fusion.4.ya_ref.y_ref), channel_id=1, source_target_pairs={{0,2},{2,0},{4,6},{6,4},{1,3},{3,1},{5,7},{7,5},{8,10},{10,8},{12,... | collective-permute-start | bytes 3145736 | tf_op jit(solution)/shard_map/ppermute | solution.py:432
  52.9 92.2 %collective-permute-start.9 = (bf16[8,64,1664]{2,1,0:T(8,128)(2,1)}, bf16[8,64,1664]{2,1,0:T(8,128)(2,1)}, u32[]{:S(2)}, u32[]{:S(2)}) collective-permute-start(bf16[8,64,1664]{2,1,0:T(8,128)(2,1)} %bitcast.283), channel_id=1, source_target_pairs={{0,2},{2,0},{4,6},{6,4},{1,3},{3,1},{5,7},{7,5},{8,10},{10,8},{12,... | collective-permute-start | bytes 5111816 | tf_op jit(solution)/shard_map/ppermute | solution.py:432
  129.8 31.6 %collective-permute-start.42 = (bf16[2,128,768]{2,1,0:T(8,128)(2,1)}, bf16[2,128,768]{2,1,0:T(8,128)(2,1)}, u32[]{:S(2)}, u32[]{:S(2)}) collective-permute-start(bf16[2,128,768]{2,1,0:T(8,128)(2,1)} %collective-permute-done.40), channel_id=1, source_target_pairs={{8,0},{16,8},{24,16},{28,24},{20,28},{12,20},{4,12},{0,4},{10,2},{... | collective-permute-start | bytes 1179656 | tf_op jit(solution)/shard_map/ppermute | solution.py:356
  134.3 22.5 %collective-permute-start.20 = (bf16[2,128,768]{2,1,0:T(8,128)(2,1)}, bf16[2,128,768]{2,1,0:T(8,128)(2,1)}, u32[]{:S(2)}, u32[]{:S(2)}) collective-permute-start(bf16[2,128,768]{2,1,0:T(8,128)(2,1)} %collective-permute-done.18), channel_id=1, source_target_pairs={{0,8},{8,16},{16,24},{24,28},{28,20},{20,12},{12,4},{4,0},{2,10},{... | collective-permute-start | bytes 1179656 | tf_op jit(solution)/shard_map/ppermute | solution.py:356
  138.2 26.7 %collective-permute-start.21 = (bf16[2,128,768]{2,1,0:T(8,128)(2,1)}, bf16[2,128,768]{2,1,0:T(8,128)(2,1)}, u32[]{:S(2)}, u32[]{:S(2)}) collective-permute-start(bf16[2,128,768]{2,1,0:T(8,128)(2,1)} %collective-permute-done.19), channel_id=1, source_target_pairs={{8,0},{16,8},{24,16},{28,24},{20,28},{12,20},{4,12},{0,4},{10,2},{... | collective-permute-start | bytes 1179656 | tf_op jit(solution)/shard_map/ppermute | solution.py:356
  142.7 25.7 %collective-permute-start.33 = (bf16[2,128,768]{2,1,0:T(8,128)(2,1)}, bf16[2,128,768]{2,1,0:T(8,128)(2,1)}, u32[]{:S(2)}, u32[]{:S(2)}) collective-permute-start(bf16[2,128,768]{2,1,0:T(8,128)(2,1)} %collective-permute-done.31), channel_id=1, source_target_pairs={{0,8},{8,16},{16,24},{24,28},{28,20},{20,12},{12,4},{4,0},{2,10},{... | collective-permute-start | bytes 1179656 | tf_op jit(solution)/shard_map/ppermute | solution.py:356
  145.1 29.9 %collective-permute-start.34 = (bf16[2,128,768]{2,1,0:T(8,128)(2,1)}, bf16[2,128,768]{2,1,0:T(8,128)(2,1)}, u32[]{:S(2)}, u32[]{:S(2)}) collective-permute-start(bf16[2,128,768]{2,1,0:T(8,128)(2,1)} %collective-permute-done.32), channel_id=1, source_target_pairs={{8,0},{16,8},{24,16},{28,24},{20,28},{12,20},{4,12},{0,4},{10,2},{... | collective-permute-start | bytes 1179656 | tf_op jit(solution)/shard_map/ppermute | solution.py:356
  161.4 63.0 %collective-permute-start.51 = (bf16[2,64,768]{2,1,0:T(8,128)(2,1)S(1)}, bf16[2,64,768]{2,1,0:T(8,128)(2,1)}, u32[]{:S(2)}, u32[]{:S(2)}) collective-permute-start(bf16[2,64,768]{2,1,0:T(8,128)(2,1)S(1)} %slice.328), channel_id=1, source_target_pairs={{0,8},{8,16},{16,24},{24,28},{28,20},{20,12},{12,4},{4,0},{2,10},{... | collective-permute-start | bytes 589832 | tf_op jit(solution)/shard_map/ppermute | solution.py:356
  175.0 36.9 %collective-permute-start.14 = (bf16[1024,512]{1,0:T(8,128)(2,1)}, bf16[1024,512]{1,0:T(8,128)(2,1)}, u32[]{:S(2)}, u32[]{:S(2)}) collective-permute-start(bf16[1024,512]{1,0:T(8,128)(2,1)} %slice.315.wa_ref.wo_ref), channel_id=1, source_target_pairs={{0,1},{1,0},{2,3},{3,2},{4,5},{5,4},{6,7},{7,6},{8,9},{9,8},{10,11... | collective-permute-start | bytes 3145736 | tf_op jit(solution)/shard_map/ppermute | solution.py:433
  278.4 51.1 %collective-permute-start.86 = (bf16[2,64,768]{2,1,0:T(8,128)(2,1)}, bf16[2,64,768]{2,1,0:T(8,128)(2,1)}, u32[]{:S(2)}, u32[]{:S(2)}) collective-permute-start(bf16[2,64,768]{2,1,0:T(8,128)(2,1)} %get-tuple-element.209), channel_id=1, source_target_pairs={{8,0},{16,8},{24,16},{28,24},{20,28},{12,20},{4,12},{0,4},{10,2},{... | collective-permute-start | bytes 589832 | tf_op jit(solution)/shard_map/ppermute | solution.py:356
  279.5 52.0 %collective-permute-start.82 = (bf16[2,64,768]{2,1,0:T(8,128)(2,1)}, bf16[2,64,768]{2,1,0:T(8,128)(2,1)}, u32[]{:S(2)}, u32[]{:S(2)}) collective-permute-start(bf16[2,64,768]{2,1,0:T(8,128)(2,1)} %get-tuple-element.208), channel_id=1, source_target_pairs={{0,8},{8,16},{16,24},{24,28},{28,20},{20,12},{12,4},{4,0},{2,10},{... | collective-permute-start | bytes 589832 | tf_op jit(solution)/shard_map/ppermute | solution.py:356
  281.2 52.5 %collective-permute-start.94 = (bf16[2,64,768]{2,1,0:T(8,128)(2,1)}, bf16[2,64,768]{2,1,0:T(8,128)(2,1)}, u32[]{:S(2)}, u32[]{:S(2)}) collective-permute-start(bf16[2,64,768]{2,1,0:T(8,128)(2,1)} %get-tuple-element.215), channel_id=1, source_target_pairs={{8,0},{16,8},{24,16},{28,24},{20,28},{12,20},{4,12},{0,4},{10,2},{... | collective-permute-start | bytes 589832 | tf_op jit(solution)/shard_map/ppermute | solution.py:356
  282.3 53.4 %collective-permute-start.90 = (bf16[2,64,768]{2,1,0:T(8,128)(2,1)}, bf16[2,64,768]{2,1,0:T(8,128)(2,1)}, u32[]{:S(2)}, u32[]{:S(2)}) collective-permute-start(bf16[2,64,768]{2,1,0:T(8,128)(2,1)} %get-tuple-element.214), channel_id=1, source_target_pairs={{0,8},{8,16},{16,24},{24,28},{28,20},{20,12},{12,4},{4,0},{2,10},{... | collective-permute-start | bytes 589832 | tf_op jit(solution)/shard_map/ppermute | solution.py:356
  305.0 31.8 %collective-permute-start.102 = (bf16[2,64,768]{2,1,0:T(8,128)(2,1)}, bf16[2,64,768]{2,1,0:T(8,128)(2,1)}, u32[]{:S(2)}, u32[]{:S(2)}) collective-permute-start(bf16[2,64,768]{2,1,0:T(8,128)(2,1)} %get-tuple-element.221), channel_id=1, source_target_pairs={{8,0},{16,8},{24,16},{28,24},{20,28},{12,20},{4,12},{0,4},{10,2},{... | collective-permute-start | bytes 589832 | tf_op jit(solution)/shard_map/ppermute | solution.py:356
  336.9 41.4 %collective-permute-start.87 = (bf16[2,128,768]{2,1,0:T(8,128)(2,1)S(1)}, bf16[2,128,768]{2,1,0:T(8,128)(2,1)S(1)}, u32[]{:S(2)}, u32[]{:S(2)}) collective-permute-start(bf16[2,128,768]{2,1,0:T(8,128)(2,1)S(1)} %pad_maximum_fusion.5), channel_id=1, source_target_pairs={{8,0},{16,8},{24,16},{28,24},{20,28},{12,20},{4,12},{0,4},{10,2},{... | collective-permute-start | bytes 1179656 | tf_op jit(solution)/shard_map/ppermute | solution.py:356
  340.0 47.7 %collective-permute-start.95 = (bf16[2,128,768]{2,1,0:T(8,128)(2,1)S(1)}, bf16[2,128,768]{2,1,0:T(8,128)(2,1)S(1)}, u32[]{:S(2)}, u32[]{:S(2)}) collective-permute-start(bf16[2,128,768]{2,1,0:T(8,128)(2,1)S(1)} %pad_maximum_fusion.7), channel_id=1, source_target_pairs={{8,0},{16,8},{24,16},{28,24},{20,28},{12,20},{4,12},{0,4},{10,2},{... | collective-permute-start | bytes 1179656 | tf_op jit(solution)/shard_map/ppermute | solution.py:356
  342.4 45.4 %collective-permute-start.103 = (bf16[2,128,768]{2,1,0:T(8,128)(2,1)S(1)}, bf16[2,128,768]{2,1,0:T(8,128)(2,1)S(1)}, u32[]{:S(2)}, u32[]{:S(2)}) collective-permute-start(bf16[2,128,768]{2,1,0:T(8,128)(2,1)S(1)} %pad_maximum_fusion.9), channel_id=1, source_target_pairs={{8,0},{16,8},{24,16},{28,24},{20,28},{12,20},{4,12},{0,4},{10,2},{... | collective-permute-start | bytes 1179656 | tf_op jit(solution)/shard_map/ppermute | solution.py:356
  378.2 34.8 %collective-permute-start.53 = (bf16[512,1024]{1,0:T(8,128)(2,1)S(1)}, bf16[512,1024]{1,0:T(8,128)(2,1)S(1)}, u32[]{:S(2)}, u32[]{:S(2)}) collective-permute-start(bf16[512,1024]{1,0:T(8,128)(2,1)S(1)} %convert_element_type.184), channel_id=1, source_target_pairs={{0,2},{2,0},{4,6},{6,4},{1,3},{3,1},{5,7},{7,5},{8,10},{10,8},{12,... | collective-permute-start | bytes 3145736 | tf_op jit(solution)/shard_map/ppermute | solution.py:432
  387.7 28.0 %collective-permute-start.55 = (bf16[512,1024]{1,0:T(8,128)(2,1)S(1)}, bf16[512,1024]{1,0:T(8,128)(2,1)S(1)}, u32[]{:S(2)}, u32[]{:S(2)}) collective-permute-start(bf16[512,1024]{1,0:T(8,128)(2,1)S(1)} %convert_element_type.190), channel_id=1, source_target_pairs={{0,2},{2,0},{4,6},{6,4},{1,3},{3,1},{5,7},{7,5},{8,10},{10,8},{12,... | collective-permute-start | bytes 3145736 | tf_op jit(solution)/shard_map/ppermute | solution.py:432
  404.7 39.8 %collective-permute-start.85 = (bf16[2,128,768]{2,1,0:T(8,128)(2,1)}, bf16[2,128,768]{2,1,0:T(8,128)(2,1)}, u32[]{:S(2)}, u32[]{:S(2)}) collective-permute-start(bf16[2,128,768]{2,1,0:T(8,128)(2,1)} %get-tuple-element.165), channel_id=1, source_target_pairs={{0,8},{8,16},{16,24},{24,28},{28,20},{20,12},{12,4},{4,0},{2,10},{... | collective-permute-start | bytes 1179656 | tf_op jit(solution)/shard_map/ppermute | solution.py:356
  413.1 38.8 %collective-permute-start.93 = (bf16[2,128,768]{2,1,0:T(8,128)(2,1)}, bf16[2,128,768]{2,1,0:T(8,128)(2,1)}, u32[]{:S(2)}, u32[]{:S(2)}) collective-permute-start(bf16[2,128,768]{2,1,0:T(8,128)(2,1)} %get-tuple-element.170), channel_id=1, source_target_pairs={{0,8},{8,16},{16,24},{24,28},{28,20},{20,12},{12,4},{4,0},{2,10},{... | collective-permute-start | bytes 1179656 | tf_op jit(solution)/shard_map/ppermute | solution.py:356
  430.7 37.3 %collective-permute-start.56 = (bf16[512,1024]{1,0:T(8,128)(2,1)S(1)}, bf16[512,1024]{1,0:T(8,128)(2,1)S(1)}, u32[]{:S(2)}, u32[]{:S(2)}) collective-permute-start(bf16[512,1024]{1,0:T(8,128)(2,1)S(1)} %copy-done.10), channel_id=1, source_target_pairs={{0,1},{1,0},{2,3},{3,2},{4,5},{5,4},{6,7},{7,6},{8,9},{9,8},{10,11... | collective-permute-start | bytes 3145736 | tf_op jit(solution)/shard_map/ppermute | solution.py:433
  448.9 31.5 %collective-permute-start.101 = (bf16[2,128,768]{2,1,0:T(8,128)(2,1)}, bf16[2,128,768]{2,1,0:T(8,128)(2,1)}, u32[]{:S(2)}, u32[]{:S(2)}) collective-permute-start(bf16[2,128,768]{2,1,0:T(8,128)(2,1)} %get-tuple-element.175), channel_id=1, source_target_pairs={{0,8},{8,16},{16,24},{24,28},{28,20},{20,12},{12,4},{4,0},{2,10},{... | collective-permute-start | bytes 1179656 | tf_op jit(solution)/shard_map/ppermute | solution.py:356
  451.9 43.7 %collective-permute-start.109 = (bf16[2,128,768]{2,1,0:T(8,128)(2,1)}, bf16[2,128,768]{2,1,0:T(8,128)(2,1)}, u32[]{:S(2)}, u32[]{:S(2)}) collective-permute-start(bf16[2,128,768]{2,1,0:T(8,128)(2,1)} %get-tuple-element.180), channel_id=1, source_target_pairs={{0,8},{8,16},{16,24},{24,28},{28,20},{20,12},{12,4},{4,0},{2,10},{... | collective-permute-start | bytes 1179656 | tf_op jit(solution)/shard_map/ppermute | solution.py:356
  454.8 25.5 %collective-permute-start.105 = (bf16[2,128,768]{2,1,0:T(8,128)(2,1)}, bf16[2,128,768]{2,1,0:T(8,128)(2,1)}, u32[]{:S(2)}, u32[]{:S(2)}) collective-permute-start(bf16[2,128,768]{2,1,0:T(8,128)(2,1)} %bitcast_add_fusion.5), channel_id=1, source_target_pairs={{8,0},{16,8},{24,16},{28,24},{20,28},{12,20},{4,12},{0,4},{10,2},{... | collective-permute-start | bytes 1179656 | tf_op jit(solution)/shard_map/ppermute | solution.py:356
  466.3 29.2 %collective-permute-start.113 = (bf16[2,128,768]{2,1,0:T(8,128)(2,1)}, bf16[2,128,768]{2,1,0:T(8,128)(2,1)}, u32[]{:S(2)}, u32[]{:S(2)}) collective-permute-start(bf16[2,128,768]{2,1,0:T(8,128)(2,1)} %bitcast_add_fusion.1), channel_id=1, source_target_pairs={{8,0},{16,8},{24,16},{28,24},{20,28},{12,20},{4,12},{0,4},{10,2},{... | collective-permute-start | bytes 1179656 | tf_op jit(solution)/shard_map/ppermute | solution.py:356
  498.2 35.0 %collective-permute-start.114 = (bf16[8,64,768]{2,1,0:T(8,128)(2,1)}, bf16[8,64,768]{2,1,0:T(8,128)(2,1)}, u32[]{:S(2)}, u32[]{:S(2)}) collective-permute-start(bf16[8,64,768]{2,1,0:T(8,128)(2,1)} %get-tuple-element.186), channel_id=1, source_target_pairs={{0,2},{2,0},{4,6},{6,4},{1,3},{3,1},{5,7},{7,5},{8,10},{10,8},{12,... | collective-permute-start | bytes 2359304 | tf_op jit(solution)/shard_map/ppermute | solution.py:432
  503.7 31.2 %collective-permute-start.78 = (bf16[1,64,640]{2,1,0:T(8,128)(2,1)S(1)}, bf16[1,64,640]{2,1,0:T(8,128)(2,1)S(1)}, u32[]{:S(2)}, u32[]{:S(2)}) collective-permute-start(bf16[1,64,640]{2,1,0:T(8,128)(2,1)S(1)} %pad_maximum_fusion.17), channel_id=1, source_target_pairs={{8,0},{16,8},{24,16},{28,24},{20,28},{12,20},{4,12},{0,4},{10,2},{... | collective-permute-start | bytes 245768 | tf_op jit(solution)/shard_map/ppermute | solution.py:356
  504.8 27.6 %collective-permute-start.74 = (bf16[1,64,640]{2,1,0:T(8,128)(2,1)S(1)}, bf16[1,64,640]{2,1,0:T(8,128)(2,1)S(1)}, u32[]{:S(2)}, u32[]{:S(2)}) collective-permute-start(bf16[1,64,640]{2,1,0:T(8,128)(2,1)S(1)} %pad_maximum_fusion.16), channel_id=1, source_target_pairs={{0,8},{8,16},{16,24},{24,28},{28,20},{20,12},{12,4},{4,0},{2,10},{... | collective-permute-start | bytes 245768 | tf_op jit(solution)/shard_map/ppermute | solution.py:356
  (134 other events, 1620.1 us)

commit v2 on v1

v2 whole, which is shorter than its diff:
```python
import functools

import jax
import jax.numpy as jnp
from jax import lax
from jax.experimental import pallas as pl
from jax.experimental.pallas import tpu as pltpu
from jax.sharding import PartitionSpec as P

HD = 64
TOP = 8
LANES = 128

EPSILON = 1e-06
ATTN_SCALE = 0.015625
RESIDUAL_SCALE = 0.22
MASKED_SCORE = -1e30
GATHERS = 2
CALLS = 2
RING = ("fsdp", "ctx")
BF = jnp.bfloat16
F32 = jnp.float32
VMEM_LIMIT = 24 * 1024 * 1024
MOE_VMEM = 56 * 1024 * 1024


def nt(a, b):
    return lax.dot_general(a, b, (((1,), (1,)), ((), ())), preferred_element_type=F32)


def nn(a, b):
    return lax.dot_general(a, b, (((1,), (0,)), ((), ())), preferred_element_type=F32)


def tn(a, b):
    return lax.dot_general(a, b, (((0,), (0,)), ((), ())), preferred_element_type=F32)


def params(*semantics):
    return pltpu.CompilerParams(
        dimension_semantics=semantics, vmem_limit_bytes=VMEM_LIMIT
    )


def whole(shape):
    zeros = (0,) * len(shape)
    return pl.BlockSpec(shape, lambda *_: zeros, pipeline_mode=pl.Buffered(1))


def swap_halves(slab):
    lane = lax.broadcasted_iota(jnp.int32, slab.shape, 1) % HD
    return jnp.where(
        lane < HD // 2, pltpu.roll(slab, LANES - HD // 2, 1), pltpu.roll(slab, HD // 2, 1)
    )


def column_as_row(ref, column):
    lane = lax.broadcasted_iota(jnp.int32, (16, ref.shape[1]), 1)
    return nt(jnp.where(lane == column, 1.0, 0.0).astype(BF), ref[...])[:1]


def pack_kernel(q_ref, k_ref, v_ref, out_ref, router_ref, one_ref, two_ref, packed_ref):
    rows, q_width = q_ref.shape
    packed_ref[0, :, :q_width] = q_ref[...]
    at = q_width
    for pair in range(k_ref.shape[1] // LANES):
        cols = slice(pair * LANES, (pair + 1) * LANES)
        packed_ref[0, :, at : at + LANES] = k_ref[:, cols]
        packed_ref[0, :, at + LANES : at + 2 * LANES] = v_ref[:, cols]
        at += 2 * LANES
    packed_ref[0, :, at : at + q_width] = out_ref[...].T
    at += q_width
    experts = router_ref.shape[1]
    square = (rows, rows)
    diagonal = lax.broadcasted_iota(jnp.int32, square, 0) == lax.broadcasted_iota(
        jnp.int32, square, 1
    )
    gains = [
        jnp.sum(jnp.where(diagonal, r[...].astype(F32), 0.0), axis=1, keepdims=True)
        for r in (one_ref, two_ref)
    ]
    lane = lax.broadcasted_iota(jnp.int32, (rows, LANES), 1)
    wide = jnp.where(lane == experts, gains[0], 0.0)
    wide = jnp.where(lane == experts + 1, gains[1], wide)
    packed_ref[0, :, at:] = wide.astype(BF)
    packed_ref[0, :, at : at + experts] = router_ref[...]


def pack_experts_kernel(core_ref, gate_ref, up_ref, down_ref, mine_ref, other_ref):
    count, _, cols = mine_ref.shape
    hid = cols // 3
    for out_ref, core in ((mine_ref, core_ref[0]), (other_ref, 1 - core_ref[0])):
        for i in range(count):
            e = core * count + i
            out_ref[i, :, :hid] = gate_ref[e]
            out_ref[i, :, hid : 2 * hid] = up_ref[e]
            out_ref[i, :, 2 * hid :] = down_ref[e].T


def join_kernel(core_ref, mine_ref, other_ref, *groups):
    rows = mine_ref.shape[1]
    for mine_first in (True, False):

        @pl.when((core_ref[0] == 0) == mine_first)
        def _():
            at = 0
            for out_ref in groups:
                size = out_ref.shape[0]
                first, second = (mine_ref, other_ref) if mine_first else (other_ref, mine_ref)
                out_ref[:, :rows] = first[at : at + size]
                out_ref[:, rows:] = second[at : at + size]
                at += size


def assemble_kernel(places, where_ref, *refs):
    count = len(places)
    parts, outs, sem = refs[:count], refs[count:-1], refs[-1]

    def copies():
        for j, (_, _, rows) in enumerate(places):
            first = 0
            for out in outs:
                cols = out.shape[1]
                yield pltpu.make_async_copy(
                    parts[j].at[0, :, pl.ds(first, cols)],
                    out.at[pl.ds(pl.multiple_of(where_ref[j], 16), rows)],
                    sem,
                )
                first += cols

    for copy in copies():
        copy.start()
    for copy in copies():
        copy.wait()


def side_by_side(tp_ref, mine, other):
    first = tp_ref[0] == 0
    return jnp.concatenate([jnp.where(first, mine, other), jnp.where(first, other, mine)], axis=1)


def features_kernel(tp_ref, mine_ref, other_ref, full_ref):
    full_ref[...] = side_by_side(tp_ref, mine_ref[...], other_ref[...])


def project_kernel(
    pairs,
    q_width,
    gain_col,
    tp_ref,
    mine_ref,
    other_ref,
    small_ref,
    w_ref,
    cos_ref,
    sin_ref,
    x_ref,
    n_ref,
    q_ref,
    kv_ref,
):
    x_ref[...] = side_by_side(tp_ref, mine_ref[...], other_ref[...])
    x = x_ref[...].astype(F32)
    gain = column_as_row(small_ref, gain_col)
    scale = lax.rsqrt(jnp.mean(x * x, axis=1, keepdims=True) + EPSILON)
    normed = (x * scale * gain).astype(BF)
    n_ref[...] = normed
    cosine, sine = cos_ref[...], sin_ref[...]
    raw = nn(normed, w_ref[...])
    for slab in range(q_width // LANES):
        cols = slice(slab * LANES, (slab + 1) * LANES)
        part = raw[:, cols]
        turned = (part * cosine + swap_halves(part) * sine).astype(BF)
        q_ref[:, cols] = (turned.astype(F32) * ATTN_SCALE).astype(BF)
    for pair in range(pairs):
        lo = pair * 2 * LANES
        part = raw[:, q_width + lo : q_width + lo + LANES]
        kv_ref[:, lo : lo + LANES] = (part * cosine + swap_halves(part) * sine).astype(BF)
        kv_ref[:, lo + LANES : lo + 2 * LANES] = raw[
            :, q_width + lo + LANES : q_width + lo + 2 * LANES
        ].astype(BF)


def attend_kernel(blocks, span, prefix_ref, base_ref, q_ref, *refs):
    kv_refs = refs[:blocks]
    out_ref, p_ref = refs[blocks:]
    limit_len = prefix_ref[pl.program_id(0)]
    local = base_ref[0] + lax.broadcasted_iota(jnp.int32, (span, 1), 0)
    limit = jnp.maximum(local + 1, limit_len)
    key_pos = jnp.concatenate(
        [
            base_ref[j] + lax.broadcasted_iota(jnp.int32, (1, span), 1)
            for j in range(blocks)
        ],
        axis=1,
    )
    visible = key_pos < limit
    visible = jnp.concatenate([visible, visible], axis=0)
    for g in range(2):
        keys = jnp.concatenate([r[:, g * HD : (g + 1) * HD] for r in kv_refs], axis=0)
        vals = jnp.concatenate(
            [r[:, LANES + g * HD : LANES + (g + 1) * HD] for r in kv_refs], axis=0
        )
        first, second = 2 * g * HD, (2 * g + 1) * HD
        queries = jnp.concatenate(
            [q_ref[:, first : first + HD], q_ref[:, second : second + HD]], axis=0
        )
        scores = jnp.where(visible, nt(queries, keys), MASKED_SCORE)
        expo = jnp.exp(scores - jnp.max(scores, axis=1, keepdims=True))
        probs = (expo * (1.0 / jnp.sum(expo, axis=1, keepdims=True))).astype(BF)
        p_ref[0, g] = probs
        att = nn(probs, vals).astype(BF)
        out_ref[:, first : first + HD] = att[:span]
        out_ref[:, second : second + HD] = att[span:]


def attend_back_kernel(blocks, span, p_ref, q_ref, g_ref, cos_ref, sin_ref, *refs):
    kv_refs = refs[:blocks]
    dq_ref, own_ref, other_ref = refs[blocks:]
    cosine, sine = cos_ref[...], sin_ref[...]
    parts = []
    for g in range(2):
        keys = jnp.concatenate([r[:, g * HD : (g + 1) * HD] for r in kv_refs], axis=0)
        vals = jnp.concatenate(
            [r[:, LANES + g * HD : LANES + (g + 1) * HD] for r in kv_refs], axis=0
        )
        first, second = 2 * g * HD, (2 * g + 1) * HD
        queries = jnp.concatenate(
            [q_ref[:, first : first + HD], q_ref[:, second : second + HD]], axis=0
        )
        grads = jnp.concatenate(
            [g_ref[:, first : first + HD], g_ref[:, second : second + HD]], axis=0
        )
        probs = p_ref[0, g]
        wide = probs.astype(F32)
        grad_probs = nt(grads, vals)
        inner = jnp.sum(wide * grad_probs, axis=1, keepdims=True)
        grad_scores = (wide * (grad_probs - inner)).astype(BF)
        dq = nn(grad_scores, keys) * ATTN_SCALE
        slab = jnp.concatenate([dq[:span], dq[span:]], axis=1)
        turned = slab * cosine - swap_halves(slab) * sine
        dq_ref[:, first : first + LANES] = turned.astype(BF)
        parts.append((nn(queries.T, grad_scores), nn(grads.T, probs)))
    stacked = jnp.concatenate([parts[0][0], parts[1][0], parts[0][1], parts[1][1]], axis=0)
    turned = stacked.T.astype(BF)
    half = blocks // 2
    for j in range(half):
        own_ref[j] = turned[j * span : (j + 1) * span]
        other_ref[j] = turned[(half + j) * span : (half + j + 1) * span]


def middle_kernel(
    gain_col, a_ref, b_ref, wa_ref, wb_ref, x_ref, small_ref, routes_ref, m_ref, n_ref, g_ref
):
    branch = nt(a_ref[...], wa_ref[...]) + nt(b_ref[...], wb_ref[...])
    middle = x_ref[...].astype(F32) + RESIDUAL_SCALE * branch
    m_ref[...] = middle
    scale = lax.rsqrt(jnp.mean(middle * middle, axis=1, keepdims=True) + EPSILON)
    wide = middle * scale * column_as_row(small_ref, gain_col)
    normed = wide.astype(BF)
    width = normed.shape[1]
    n_ref[:, :width] = normed
    logits = nn(normed, small_ref[...])
    lane = lax.broadcasted_iota(jnp.int32, logits.shape, 1)
    routes = routes_ref[...]
    routed = lane == routes[:, 0:1]
    for k in range(1, TOP):
        routed = routed | (lane == routes[:, k : k + 1])
    logits = jnp.where(routed, logits, MASKED_SCORE)
    expo = jnp.where(routed, jnp.exp(logits - jnp.max(logits, axis=1, keepdims=True)), 0.0)
    gates = expo / jnp.sum(expo, axis=1, keepdims=True)
    g_ref[...] = gates
    n_ref[:, width:] = in_two(gates, gain_col - 1)


def in_two(pull, experts):
    high = pull.astype(BF).astype(F32)
    return (high + pltpu.roll(pull - high, experts, 1)).astype(BF)


def in_one(terms, experts):
    wide = terms.astype(F32)
    lane = lax.broadcasted_iota(jnp.int32, wide.shape, 1)
    both = wide + pltpu.roll(wide, LANES - experts, 1)
    return jnp.where(lane < experts, both, 0.0)


def moe_kernel(first_call, last_call, experts, start, group, places, where_ref, *refs):
    count = len(places)
    w_parts, refs = refs[:count], refs[count:]
    sources, refs = refs[:4], refs[4:]
    inits, refs = ((), refs) if first_call else (refs[:2], refs[2:])
    outs, mixed_out, dw_parts, refs = refs[:2], refs[2], refs[3 : 3 + count], refs[3 + count :]
    here, accs, refs = refs[:4], refs[4:6], refs[6:]
    mixed_all, narrow, w_all, dw_all, w_sem, dw_sem, near_sem, acc_sem, out_sem, mixed_sem = refs
    xa_ref, ya_ref, xb_ref, yb_ref = here
    rows, width = ya_ref.shape
    hid = w_all.shape[2] // 3

    def window(j):
        return pl.ds(pl.multiple_of(where_ref[1 + j], 16), places[j][2])

    def load(e, j):
        return pltpu.make_async_copy(
            w_parts[j].at[start + e], w_all.at[e, window(j)], w_sem.at[e]
        )

    def store(e, j):
        return pltpu.make_async_copy(
            dw_all.at[e % 2, window(j)], dw_parts[j].at[e], dw_sem.at[e % 2]
        )

    nears = [
        pltpu.make_async_copy(a, b, near_sem.at[i]) for i, (a, b) in enumerate(zip(sources, here))
    ]
    fetches = [
        pltpu.make_async_copy(a, b, acc_sem.at[i]) for i, (a, b) in enumerate(zip(inits, accs))
    ]
    mixed_store = pltpu.make_async_copy(mixed_all, mixed_out, mixed_sem)
    for j in range(count):
        load(0, j).start()
    for copy in nears[:2]:
        copy.start()
    results = []
    for e in range(group):
        for j in range(count):
            load(e, j).wait()
        if e == 0:
            for copy in nears[:2]:
                copy.wait()
            for copy in [*fetches[:1], *nears[2:], *fetches[1:]]:
                copy.start()
        expert = where_ref[0] + e
        w_gu, w_d = w_all[e, :, : 2 * hid], w_all[e, :, 2 * hid :]
        kept = []
        for side, (x_ref, y_ref) in enumerate(((xa_ref, ya_ref), (xb_ref, yb_ref))):
            acc = accs[side]
            if e == 0 and side == 1:
                for copy in nears[2:]:
                    copy.wait()
                for other in range(1, group):
                    for j in range(count):
                        load(other, j).start()
            pre = nn(x_ref[:, :width], w_gu)
            back = nn(y_ref[...], w_d)
            gates = in_one(x_ref[:, width:], experts)
            lane = lax.broadcasted_iota(jnp.int32, gates.shape, 1)
            mask = lane == expert
            weight = RESIDUAL_SCALE * jnp.sum(
                jnp.where(mask, gates, 0.0), axis=1, keepdims=True
            )
            gate_pre, up_pre = pre[:, :hid], pre[:, hid:]
            sig = jax.nn.sigmoid(gate_pre)
            act = gate_pre * sig
            hidden = act * up_pre
            pull = RESIDUAL_SCALE * jnp.sum(back * hidden, axis=1, keepdims=True)
            scaled = weight * back
            d_up = scaled * act
            d_gate = scaled * up_pre * (sig + act * (1.0 - sig))
            d_gu = jnp.concatenate([d_gate.astype(BF), d_up.astype(BF)], axis=1)
            mixed = (weight * hidden).astype(BF)
            mixed_all[e, side * rows : (side + 1) * rows] = mixed
            if first_call and e == 0:
                acc[:, :width] = nt(d_gu, w_gu)
                acc[:, width:] = jnp.where(mask, pull, 0.0)
            else:
                if e == 0:
                    fetches[side].wait()
                acc[:, :width] += nt(d_gu, w_gu)
                acc[:, width:] += jnp.where(mask, pull, 0.0)
            kept.append((d_gu, mixed))
            if e == group - 1:
                if last_call and side:
                    narrow[:, :width] = acc[:, :width].astype(BF)
                    narrow[:, width:] = in_two(acc[:, width:], experts)
                    acc = narrow
                results.append(pltpu.make_async_copy(acc, outs[side], out_sem.at[side]))
                results[-1].start()
        if e == group - 1:
            mixed_store.start()
        dw_gu = tn(xa_ref[:, :width], kept[0][0]) + tn(xb_ref[:, :width], kept[1][0])
        dw_d = tn(ya_ref[...], kept[0][1]) + tn(yb_ref[...], kept[1][1])
        if e >= 2:
            for j in range(count):
                store(e - 2, j).wait()
        dw_all[e % 2, :, : 2 * hid] = dw_gu.astype(BF)
        dw_all[e % 2, :, 2 * hid :] = dw_d.astype(BF)
        for j in range(count):
            store(e, j).start()
    for e in range(max(0, group - 2), group):
        for j in range(count):
            store(e, j).wait()
    for copy in results:
        copy.wait()
    mixed_store.wait()


def moe_sum_kernel(places, sets, calls, group, where_ref, *refs):
    count = len(places)
    w_sets = [refs[k * count : (k + 1) * count] for k in range(sets)]
    refs = refs[sets * count :]
    mixed_parts, refs = refs[:calls], refs[calls:]
    own_ref, peer_ref, w_all, mixed_all, total, w_sem, mixed_sem = refs
    hid = w_all.shape[2]
    rows = own_ref.shape[0]
    experts = calls * group
    set_size = experts // sets

    def loads(e):
        for j in range(count):
            yield pltpu.make_async_copy(
                w_sets[e // set_size][j].at[e % set_size, :, pl.ds(2 * hid, hid)],
                w_all.at[e % 2, pl.ds(pl.multiple_of(where_ref[1 + j], 16), places[j][2])],
                w_sem.at[e % 2],
            )
        yield pltpu.make_async_copy(
            mixed_parts[e // group].at[e % group], mixed_all.at[e % 2], mixed_sem.at[e % 2]
        )

    for copy in loads(0):
        copy.start()
    for e in range(experts):
        for copy in loads(e):
            copy.wait()
        if e + 1 < experts:
            for copy in loads(e + 1):
                copy.start()
        term = nt(mixed_all[e % 2], w_all[e % 2])
        if e == 0:
            total[...] = term
        else:
            total[...] += term
    own_ref[...] = total[:rows]
    peer_ref[...] = total[rows:].astype(BF)


def weight_grad_kernel(count, gain_at, core_ref, *refs):
    pairs, refs = refs[: 2 * count], refs[2 * count :]
    gain_ref, kept_ref, sent_ref = refs
    n, shard, _ = kept_ref.shape
    width = gain_ref.shape[1]
    terms = [tn(pairs[2 * i][:, :width], pairs[2 * i + 1][...]) for i in range(count)]
    if gain_at is not None:
        row = lax.broadcasted_iota(jnp.int32, (8, LANES), 0)
        lane = lax.broadcasted_iota(jnp.int32, (8, LANES), 1)
        place = jnp.where((row == 0) & (lane == gain_at), 1.0, 0.0)
        gains = tn(jnp.broadcast_to(gain_ref[...], (8, gain_ref.shape[1])), place)
        if terms[-1].shape[1] == LANES:
            terms[-1] = terms[-1] + gains
        else:
            terms.append(gains)
    first = 0
    for term in terms:
        cols = term.shape[1]
        parts = term.astype(BF).reshape(n, 2, shard, cols)
        for mine in range(2):

            @pl.when(core_ref[0] == mine)
            def _():
                kept_ref[:, :, first : first + cols] = parts[:, mine]
                sent_ref[:, :, first : first + cols] = parts[:, 1 - mine]

        first += cols


def order_kernel(places, chips_ref, *refs):
    count = len(places)
    pairs, parts = refs[:-count], refs[-count:]
    for j, (_, row, rows) in enumerate(places):
        chip = chips_ref[j]
        window = pl.ds(row, rows)
        first = 0
        for kept_ref, other_ref in zip(pairs[::2], pairs[1::2]):
            cols = kept_ref.shape[2]
            parts[j][0, :, first : first + cols] = kept_ref[chip, window] + other_ref[chip, window]
            first += cols


def add_terms_kernel(experts, own_ref, peer_ref, sum_ref):
    width = own_ref.shape[1] - LANES
    sum_ref[:, :width] = (own_ref[:, :width] + peer_ref[:, :width].astype(F32)).astype(BF)
    pull = own_ref[:, width:] + in_one(peer_ref[:, width:], experts)
    sum_ref[:, width:] = in_two(pull, experts)


def middle_back_kernel(
    gain_col,
    tp_ref,
    sa_ref,
    sb_ref,
    gates_ref,
    m_ref,
    y_ref,
    small_ref,
    wo_ref,
    gm_ref,
    branch_ref,
    att_ref,
    logit_ref,
    dgain_ref,
):
    @pl.when(pl.program_id(0) == 0)
    def _():
        dgain_ref[...] = jnp.zeros(dgain_ref.shape, F32)

    gates = gates_ref[...]
    width = m_ref.shape[1]
    pull = in_one(sa_ref[:, width:], gain_col - 1) + in_one(sb_ref[:, width:], gain_col - 1)
    weighted = gates * pull
    grad_logits = (weighted - gates * jnp.sum(weighted, axis=1, keepdims=True)).astype(BF)
    logit_ref[...] = grad_logits
    grad = sa_ref[:, :width].astype(F32) + sb_ref[:, :width].astype(F32)
    grad = grad + nt(grad_logits, small_ref[...])
    middle = m_ref[...]
    scale = lax.rsqrt(jnp.mean(middle * middle, axis=1, keepdims=True) + EPSILON)
    unit = middle * scale
    dgain_ref[...] += jnp.sum(grad * unit, axis=0, keepdims=True)
    scaled = grad * column_as_row(small_ref, gain_col)
    inner = jnp.sum(scaled * unit, axis=1, keepdims=True) * (1.0 / width)
    grad_middle = y_ref[...].astype(F32) + scale * (scaled - unit * inner)
    half = width // 2
    gm_ref[...] = jnp.where(tp_ref[0] == 0, grad_middle[:, :half], grad_middle[:, half:])
    branch = (RESIDUAL_SCALE * grad_middle).astype(BF)
    branch_ref[...] = branch
    att_ref[...] = nn(branch, wo_ref[...]).astype(BF)


def project_back_kernel(
    pairs,
    gain_col,
    tp_ref,
    dq_ref,
    kva_ref,
    kvb_ref,
    kvc_ref,
    cos_ref,
    sin_ref,
    w_ref,
    x_ref,
    small_ref,
    d_ref,
    own_ref,
    other_ref,
    dot_ref,
    dgain_ref,
):
    @pl.when(pl.program_id(0) == 0)
    def _():
        dgain_ref[...] = jnp.zeros(dgain_ref.shape, F32)

    cosine, sine = cos_ref[...], sin_ref[...]
    q_width = dq_ref.shape[1]
    kv = kva_ref[...].astype(F32) + kvb_ref[...].astype(F32) + kvc_ref[...].astype(F32)
    for pair in range(pairs):
        lo = pair * 2 * LANES
        part = kv[:, lo : lo + LANES]
        d_ref[:, lo : lo + LANES] = (part * cosine - swap_halves(part) * sine).astype(BF)
        d_ref[:, lo + LANES : lo + 2 * LANES] = kv[:, lo + LANES : lo + 2 * LANES].astype(BF)
    grad = nt(dq_ref[...], w_ref[:, :q_width]) + nt(d_ref[...], w_ref[:, q_width:])
    x = x_ref[...].astype(F32)
    width = x.shape[1]
    scale = lax.rsqrt(jnp.mean(x * x, axis=1, keepdims=True) + EPSILON)
    unit = x * scale
    dgain_ref[...] += jnp.sum(grad * unit, axis=0, keepdims=True)
    scaled = grad * column_as_row(small_ref, gain_col)
    inner = jnp.sum(scaled * unit, axis=1, keepdims=True) * (1.0 / width) * scale * scale
    dot_ref[...] = jnp.broadcast_to(inner, dot_ref.shape)
    scaled = scaled * scale
    half = width // 2
    is_first = tp_ref[0] == 0
    own_ref[...] = jnp.where(is_first, scaled[:, :half], scaled[:, half:])
    other_ref[...] = jnp.where(is_first, scaled[:, half:], scaled[:, :half]).astype(BF)


class Ring:
    def __init__(self, wide, ctx):
        self.wide, self.ctx, self.deep = wide, ctx, ctx // 2
        self.size = wide * self.deep
        deep = self.deep
        order = [
            (f, y)
            for y in range(deep)
            for f in (range(wide) if y % 2 == 0 else range(wide - 1, -1, -1))
        ]
        flat = [[f * ctx + y * 2 + c for f, y in order] for c in range(2)]
        n = self.size
        self.forward = [(row[i], row[(i + 1) % n]) for row in flat for i in range(n)]
        self.backward = [(b, a) for a, b in self.forward]
        f, c = lax.axis_index("fsdp"), lax.axis_index("ctx")
        y = c // 2
        self.place = y * wide + jnp.where(y % 2 == 0, f, wide - 1 - f)

    def chip(self, offset):
        place = (self.place + offset) % self.size
        y, q = place // self.wide, place % self.wide
        f = jnp.where(y % 2 == 0, q, self.wide - 1 - q)
        return f * self.deep + y

    def send(self, array, forward=True):
        return lax.ppermute(array, RING, self.forward if forward else self.backward)

    def places(self, rows):
        far, half = self.size // 2, rows // 2
        found = [(0, 0, rows)]
        for step in range(1, far):
            found += [(-step, 0, rows), (step, 0, rows)]
        if half % 16:
            return found + [(-far, 0, rows)]
        return found + [(-far, 0, half), (far, half, half)]


class Gather:
    def __init__(self, ring, block, name):
        self.ring, self.step, self.rows, self.name = ring, 0, block.shape[1], name
        self.moving = (block, block)
        self.parts = [block]

    def tick(self):
        self.step += 1
        ahead, back = self.moving
        if self.done():
            half = self.rows // 2
            if half % 16:
                self.parts.append(self.ring.send(ahead))
                return
            ahead, back = ahead[:, :half], back[:, half:]
        with jax.named_scope(f"{self.name}_step_{self.step}"):
            self.moving = (self.ring.send(ahead), self.ring.send(back, False))
        self.parts += self.moving

    def done(self):
        return self.step == self.ring.size // 2


class Scatter:
    def __init__(self, ring, parts, name):
        self.ring, self.parts, self.step, self.name = ring, parts, 0, name
        self.far = ring.size // 2
        self.halved = len(parts) == ring.size + 1
        self.moving = (parts[-2], parts[-1]) if self.halved else (parts[-1],)

    def tick(self):
        self.step += 1
        if self.step > 1:
            s = self.far - self.step + 1
            behind, near = self.parts[2 * s - 1], self.parts[2 * s]
            if self.step > 2:
                ahead, back = near + self.moving[0], behind + self.moving[1]
            elif self.halved:
                half = near.shape[1] // 2
                ahead = jnp.concatenate([near[:, :half] + self.moving[0], near[:, half:]], axis=1)
                back = jnp.concatenate(
                    [behind[:, :half], behind[:, half:] + self.moving[1]], axis=1
                )
            else:
                ahead, back = near + self.moving[0], behind
            self.moving = (ahead, back)
        with jax.named_scope(f"{self.name}_step_{self.step}"):
            self.moving = tuple(
                self.ring.send(array, i == 0) for i, array in enumerate(self.moving)
            )

    def done(self):
        return self.step == self.far

    def result(self):
        ahead, back = self.moving
        return self.parts[0].astype(F32) + ahead.astype(F32) + back.astype(F32)


def lock(*values):
    return lax.optimization_barrier(values)


def per_device(
    tokens,
    prefix,
    routes,
    w_query,
    w_key,
    w_value,
    w_out,
    w_router,
    gain_attn,
    gain_ffn,
    w_gate,
    w_up,
    w_down,
    cotangent,
):
    wide, ctx = lax.axis_size("fsdp"), lax.axis_size("ctx")
    seqs, span, feature = tokens.shape
    rows = seqs * span
    width = 2 * feature
    shard = w_query.shape[0]
    experts = w_router.shape[1]
    per_core = experts // 2
    hid = w_gate.shape[2]
    q_width, kv_width = w_query.shape[1], w_key.shape[1]
    pairs = kv_width // LANES
    deep = ctx // 2
    tp, c = lax.axis_index("tp"), lax.axis_index("ctx")
    core, y = c % 2, c // 2
    ring = Ring(wide, ctx)
    n = ring.size
    core_perm = [(i, i ^ 1) for i in range(ctx)]

    def swap_core(array, name="rows"):
        with jax.named_scope(f"{name}_over_core"):
            return lax.ppermute(array, "ctx", core_perm)

    def swap_tp(array, name="rows"):
        with jax.named_scope(f"{name}_over_tp"):
            return lax.ppermute(array, "tp", [(0, 1), (1, 0)])

    up_y = [(i, (i + 2) % ctx) for i in range(ctx)]
    down_y = [(i, (i - 2) % ctx) for i in range(ctx)]

    def shift_y(array, perm, name):
        with jax.named_scope(f"{name}_over_y"):
            return lax.ppermute(array, "ctx", perm)

    tp_scalar = tp.astype(jnp.int32).reshape(1)

    def by_core(mine, other, axis):
        return jnp.where(
            core == 0,
            jnp.concatenate([mine, other], axis),
            jnp.concatenate([other, mine], axis),
        )

    vmem = pl.BlockSpec(memory_space=pltpu.VMEM)
    smem = pl.BlockSpec(memory_space=pltpu.SMEM)
    any_spec = pl.BlockSpec(memory_space=pl.ANY)
    qkv_width = q_width + 2 * kv_width
    bundle = pl.pallas_call(
        pack_kernel,
        in_specs=[vmem] * 7,
        out_specs=vmem,
        out_shape=jax.ShapeDtypeStruct((1, shard, qkv_width + q_width + LANES), BF),
        compiler_params=params(),
        name="pack",
    )(w_query, w_key, w_value, w_out, w_router, gain_attn[None], gain_ffn[None])
    own_tokens = tokens.reshape(rows, feature)
    own_cot = cotangent.reshape(rows, feature)
    other_tokens = swap_tp(own_tokens, "own_tokens")
    first = Gather(ring, bundle, "bundle")
    from_core = [swap_core(bundle, "bundle")]
    core_scalar = core.astype(jnp.int32).reshape(1)
    half_shape = jax.ShapeDtypeStruct((per_core, shard, 3 * hid), BF)
    first.tick()
    mine_w, other_w = pl.pallas_call(
        pack_experts_kernel,
        in_specs=[smem] + [vmem] * 3,
        out_specs=[vmem] * 2,
        out_shape=[half_shape] * 2,
        compiler_params=params(),
        name="pack_experts",
    )(core_scalar, *lock(w_gate, w_up, w_down, bundle)[:3])
    blocks_w = list(
        pl.pallas_call(
            join_kernel,
            in_specs=[smem] + [vmem] * 2,
            out_specs=[vmem] * GATHERS,
            out_shape=[
                jax.ShapeDtypeStruct((per_core // GATHERS, 2 * shard, 3 * hid), BF)
            ]
            * GATHERS,
            compiler_params=params(),
            name="join",
        )(core_scalar, mine_w, swap_core(other_w, "other_w"))
    )
    first.tick()
    *first.moving, mine_w = lock(*first.moving, mine_w)
    first.tick()
    *first.moving, blocks_w[0] = lock(*first.moving, blocks_w[0])
    while not first.done():
        first.tick()
    from_core += [swap_core(part, "part") for part in first.parts[1:]]
    chips = [ring.chip(d) for d, _, _ in ring.places(shard)]
    chip_list = jnp.stack(chips).astype(jnp.int32)
    bundle_places = ring.places(shard)
    bundle_rows = [
        (chips[j] * 2 + side) * shard + row
        for side in (core, 1 - core)
        for j, (_, row, _) in enumerate(bundle_places)
    ]
    in_hbm = lambda array: pltpu.with_memory_space_constraint(array, pltpu.HBM)
    w_qkv, wo_mine, w_small = pl.pallas_call(
        functools.partial(assemble_kernel, bundle_places * 2),
        in_specs=[smem] + [any_spec] * len(bundle_rows),
        out_specs=[vmem] * 3,
        out_shape=[
            jax.ShapeDtypeStruct((width, w), BF) for w in (qkv_width, q_width, LANES)
        ],
        scratch_shapes=[pltpu.SemaphoreType.DMA(())],
        compiler_params=params(),
        name="assemble",
    )(
        jnp.stack(bundle_rows).astype(jnp.int32),
        *[in_hbm(part) for part in first.parts + from_core],
    )
    weights = [Gather(ring, block, f"weights_{i}") for i, block in enumerate(blocks_w)]
    under_way = []

    def segment(ticks, *values):
        held = [array for chain in under_way for array in chain.moving]
        out = lock(*held, *values)
        at = 0
        for chain in under_way:
            size = len(chain.moving)
            chain.moving = tuple(out[at : at + size])
            at += size
        under_way[:] = [chain for chain in ticks if not chain.done()]
        for chain in under_way:
            chain.tick()
        return out[at:]

    start_block = lock(blocks_w[0], *first.parts[-2:])[0]
    weights[0].moving = (start_block, start_block)
    segment(weights[:1], start_block)
    half_width = HD // 2
    freqs = 10000.0 ** (-jnp.arange(half_width, dtype=F32) / half_width)
    local_pos = c * span + jnp.arange(span, dtype=jnp.int32)
    angles = local_pos.astype(F32)[:, None] * freqs[None, :]
    cosine, sine = jnp.cos(angles), jnp.sin(angles)
    cosine = jnp.tile(jnp.concatenate([cosine] * 4, axis=1), (seqs, 1))
    sine = jnp.tile(jnp.concatenate([-sine, sine, -sine, sine], axis=1), (seqs, 1))
    step_rows = min(rows, 256)
    steps = rows // step_rows
    row_spec = lambda cols: pl.BlockSpec((step_rows, cols), lambda i, *_: (i, 0))
    full_tokens, normed, queries, kv = pl.pallas_call(
        functools.partial(project_kernel, pairs, q_width, experts),
        grid=(steps,),
        in_specs=[
            smem,
            row_spec(feature),
            row_spec(feature),
            whole((width, LANES)),
            whole((width, qkv_width)),
            row_spec(LANES),
            row_spec(LANES),
        ],
        out_specs=[row_spec(width), row_spec(width), row_spec(q_width), row_spec(2 * kv_width)],
        out_shape=[
            jax.ShapeDtypeStruct((rows, width), BF),
            jax.ShapeDtypeStruct((rows, width), BF),
            jax.ShapeDtypeStruct((rows, q_width), BF),
            jax.ShapeDtypeStruct((rows, 2 * kv_width), BF),
        ],
        compiler_params=params("arbitrary"),
        name="project",
    )(tp_scalar, own_tokens, other_tokens, w_small, w_qkv, cosine, sine)

    own_side = [kv]
    for _ in range(deep - 1):
        own_side.append(shift_y(own_side[-1], up_y, "kv"))
    other_side = [swap_core(block, "block") for block in own_side]
    kv_blocks = own_side + other_side
    base = jnp.stack(
        [(((y - k) % deep) * 2 + core) * span for k in range(deep)]
        + [(((y - k) % deep) * 2 + 1 - core) * span for k in range(deep)]
    ).astype(jnp.int32)
    length = ctx * span

    other_cot = swap_tp(own_cot, "own_cot")
    queries, other_cot, wo_mine, *kv_blocks = segment(
        weights[:1], queries, other_cot, wo_mine, *kv_blocks
    )
    wo_other = swap_tp(wo_mine, "wo_mine")
    head_spec = lambda: pl.BlockSpec((span, 2 * LANES), lambda s, p, *_: (s, p))
    prob_spec = pl.BlockSpec((1, 2, 2 * span, length), lambda s, p, *_: (s, p, 0, 0))
    attended, probs = pl.pallas_call(
        functools.partial(attend_kernel, ctx, span),
        grid_spec=pltpu.PrefetchScalarGridSpec(
            num_scalar_prefetch=2,
            grid=(seqs, pairs),
            in_specs=[head_spec()] * (1 + ctx),
            out_specs=[head_spec(), prob_spec],
        ),
        out_shape=[
            jax.ShapeDtypeStruct((rows, q_width), BF),
            pltpu.HBM((seqs, 2 * pairs, 2 * span, length), BF),
        ],
        compiler_params=params("arbitrary", "arbitrary"),
        name="attend",
    )(prefix, base, queries, *kv_blocks)

    full_cot = pl.pallas_call(
        features_kernel,
        in_specs=[smem] + [vmem] * 2,
        out_specs=vmem,
        out_shape=pltpu.HBM((rows, width), BF),
        compiler_params=params(),
        name="features",
    )(tp_scalar, own_cot, other_cot)
    attended, wo_other, full_cot = segment(weights[:1], attended, wo_other, full_cot)
    for _ in range(ring.size // 2 - 4):
        (attended,) = segment(weights[:1], attended)

    attended_other = swap_tp(attended, "attended")
    peer_cot = swap_core(full_cot, "full_cot")
    attended_other, peer_cot = segment(weights, attended_other, peer_cot)
    route_rows = routes.reshape(rows, TOP)
    middle, normed_two, gates = pl.pallas_call(
        functools.partial(middle_kernel, experts + 1),
        grid=(steps,),
        in_specs=[
            row_spec(q_width),
            row_spec(q_width),
            whole((width, q_width)),
            whole((width, q_width)),
            row_spec(width),
            whole((width, LANES)),
            row_spec(TOP),
        ],
        out_specs=[
            row_spec(width),
            row_spec(width + LANES),
            row_spec(LANES),
        ],
        out_shape=[
            pltpu.HBM((rows, width), F32),
            pltpu.HBM((rows, width + LANES), BF),
            jax.ShapeDtypeStruct((rows, LANES), F32),
        ],
        compiler_params=params("arbitrary"),
        name="middle",
    )(attended, attended_other, wo_mine, wo_other, full_tokens, w_small, route_rows)
    peer_two = swap_core(normed_two, "normed_two")
    (peer_two,) = segment(weights[1:], peer_two)

    near = [(normed_two, BF), (full_cot, BF), (peer_two, BF), (peer_cot, BF)]
    sources = [in_hbm(array) for array, _ in near]
    wide_acc, acc_shape = (rows, width), (rows, width + LANES)
    places = ring.places(2 * shard)
    count = len(places)
    part_rows = [ring.chip(d) * 2 * shard + row for d, row, _ in places]
    calls = GATHERS * CALLS
    call_size = per_core // calls

    def run_experts(call, accs):
        where = jnp.stack([core * per_core + call * call_size] + part_rows)
        first_call, last_call = call == 0, call == calls - 1
        outs = pl.pallas_call(
            functools.partial(
                moe_kernel,
                first_call,
                last_call,
                experts,
                call % CALLS * call_size,
                call_size,
                places,
            ),
            in_specs=[smem] + [any_spec] * (count + 4 + len(accs)),
            out_specs=[any_spec] * (3 + count),
            out_shape=[
                pltpu.HBM(acc_shape, F32),
                pltpu.HBM(acc_shape, BF if last_call else F32),
                pltpu.HBM((call_size, 2 * rows, hid), BF),
            ]
            + [pltpu.HBM((call_size, r, 3 * hid), BF) for _, _, r in places],
            scratch_shapes=[pltpu.VMEM(array.shape, kind) for array, kind in near]
            + [pltpu.VMEM(acc_shape, F32)] * 2
            + [
                pltpu.VMEM((call_size, 2 * rows, hid), BF),
                pltpu.VMEM(acc_shape, BF),
                pltpu.VMEM((call_size, width, 3 * hid), BF),
                pltpu.VMEM((2, width, 3 * hid), BF),
                pltpu.SemaphoreType.DMA((call_size,)),
                pltpu.SemaphoreType.DMA((2,)),
                pltpu.SemaphoreType.DMA((4,)),
                pltpu.SemaphoreType.DMA((2,)),
                pltpu.SemaphoreType.DMA((2,)),
                pltpu.SemaphoreType.DMA(()),
            ],
            compiler_params=pltpu.CompilerParams(vmem_limit_bytes=MOE_VMEM),
            name="experts",
        )(
            where.astype(jnp.int32),
            *[in_hbm(block) for block in weights[call // CALLS].parts],
            *sources,
            *accs,
        )
        return outs[:2], outs[2], outs[3:]

    accs, mixed_parts, sums = (), [], []

    for call in range(calls):
        for chain in weights[call // CALLS : call // CALLS + 1]:
            while not chain.done():
                accs = segment([chain, *sums[:1]], *accs)
        if call:
            accs = segment([*weights[1:], *sums][:2] if not weights[-1].done() else sums[:2], *accs)
        accs, mixed, dw_parts = run_experts(call, accs)
        mixed_parts.append(mixed)
        sums.append(Scatter(ring, dw_parts, f"sums_{call}"))

    grad_two, grad_two_peer = segment(sums[2:], *accs)
    grad_two, from_peer = segment([], grad_two, swap_core(grad_two_peer, "grad_two"))
    part = pl.pallas_call(
        functools.partial(add_terms_kernel, experts),
        grid=(steps,),
        in_specs=[row_spec(width + LANES)] * 2,
        out_specs=row_spec(width + LANES),
        out_shape=jax.ShapeDtypeStruct(acc_shape, BF),
        compiler_params=params("arbitrary"),
        name="add_terms",
    )(grad_two, from_peer)
    (part,) = segment(sums[:2], part)
    part_other = swap_tp(part, "part")

    moe, moe_peer = pl.pallas_call(
        functools.partial(moe_sum_kernel, places, GATHERS, calls, call_size),
        in_specs=[smem] + [any_spec] * (count * GATHERS + calls),
        out_specs=[vmem] * 2,
        out_shape=[
            jax.ShapeDtypeStruct(wide_acc, F32),
            jax.ShapeDtypeStruct(wide_acc, BF),
        ],
        scratch_shapes=[
            pltpu.VMEM((2, width, hid), BF),
            pltpu.VMEM((2, 2 * rows, hid), BF),
            pltpu.VMEM((2 * rows, width), F32),
            pltpu.SemaphoreType.DMA((2,)),
            pltpu.SemaphoreType.DMA((2,)),
        ],
        compiler_params=params(),
        name="experts_output",
    )(
        jnp.stack([core * 0] + part_rows).astype(jnp.int32),
        *[in_hbm(block) for chain in weights for block in chain.parts],
        *lock(*[in_hbm(mixed) for mixed in mixed_parts], part)[:-1],
    )
    part_other, moe, moe_peer = segment(sums[1:3], part_other, moe, moe_peer)
    grad_middle, grad_branch, grad_attended, grad_logits, gain_two_term = pl.pallas_call(
        functools.partial(middle_back_kernel, experts + 1),
        grid=(steps,),
        in_specs=[
            smem,
            row_spec(width + LANES),
            row_spec(width + LANES),
            row_spec(LANES),
            row_spec(width),
            row_spec(width),
            whole((width, LANES)),
            whole((width, q_width)),
        ],
        out_specs=[
            row_spec(feature),
            row_spec(width),
            row_spec(q_width),
            row_spec(LANES),
            whole((1, width)),
        ],
        out_shape=[
            jax.ShapeDtypeStruct((rows, feature), F32),
            jax.ShapeDtypeStruct((rows, width), BF),
            jax.ShapeDtypeStruct((rows, q_width), BF),
            jax.ShapeDtypeStruct((rows, LANES), BF),
            jax.ShapeDtypeStruct((1, width), F32),
        ],
        compiler_params=params("arbitrary"),
        name="middle_back",
    )(
        tp_scalar,
        part,
        part_other,
        gates,
        middle,
        full_cot,
        w_small,
        wo_mine,
    )

    back_spec = pl.BlockSpec((deep, span, 2 * LANES), lambda s, p: (0, s, p))
    turn_spec = pl.BlockSpec((span, LANES), lambda s, p: (s, 0))
    grad_q, grad_kv_own, grad_kv_peer = pl.pallas_call(
        functools.partial(attend_back_kernel, ctx, span),
        grid=(seqs, pairs),
        in_specs=[prob_spec] + [head_spec()] * 2 + [turn_spec] * 2 + [head_spec()] * ctx,
        out_specs=[head_spec(), back_spec, back_spec],
        out_shape=[
            jax.ShapeDtypeStruct((rows, q_width), BF),
            jax.ShapeDtypeStruct((deep, rows, 2 * kv_width), BF),
            jax.ShapeDtypeStruct((deep, rows, 2 * kv_width), BF),
        ],
        compiler_params=params("arbitrary", "arbitrary"),
        name="attend_back",
    )(in_hbm(probs), queries, grad_attended, cosine, sine, *kv_blocks)
    def weight_grads(name, pair_list, gain_term, gain_at, cols):
        shape = jax.ShapeDtypeStruct((n, shard, cols), BF)
        flat = [array for pair in pair_list for array in pair]
        kept, sent = pl.pallas_call(
            functools.partial(weight_grad_kernel, len(pair_list), gain_at),
            in_specs=[smem] + [vmem] * (len(flat) + 1),
            out_specs=[vmem] * 2,
            out_shape=[shape] * 2,
            compiler_params=params(),
            name="weight_grads",
        )(core_scalar, *flat, gain_term)
        return kept, sent

    early = weight_grads(
        "early",
        [(grad_branch, attended), (normed_two, grad_logits)],
        gain_two_term,
        experts,
        q_width + LANES,
    )
    grad_q, grad_kv_own, grad_kv_peer, moe_peer, *early = segment(
        [], grad_q, grad_kv_own, grad_kv_peer, moe_peer, *early
    )
    from_peer = swap_core(grad_kv_peer, "grad_kv")
    early_other = swap_core(early[1], "early")
    from_core_moe = swap_core(moe_peer, "moe")
    from_peer, early_other, from_core_moe = segment([], from_peer, early_other, from_core_moe)
    half_at = lambda array, side: lax.dynamic_slice_in_dim(array, side * feature, feature, 1)
    moe_sum = moe + from_core_moe.astype(F32)
    moe_send = half_at(moe_sum, 1 - tp).astype(BF)
    travel = jnp.zeros_like(kv)
    for k in range(deep - 1, 0, -1):
        piece = grad_kv_own[k] + from_peer[k]
        if k < deep - 1:
            piece = piece + travel
        piece, moe_send = segment([sums[2]] if k == 1 else [], piece, moe_send)
        travel = shift_y(piece, down_y, "grad_kv")
    moe_other = swap_tp(moe_send, "moe_send")
    travel, moe_other = segment(sums[2:], travel, moe_other)

    grad_kv, grad_own, grad_send, inner, gain_one_term = pl.pallas_call(
        functools.partial(project_back_kernel, pairs, experts),
        grid=(steps,),
        in_specs=[
            smem,
            row_spec(q_width),
            row_spec(2 * kv_width),
            row_spec(2 * kv_width),
            row_spec(2 * kv_width),
            row_spec(LANES),
            row_spec(LANES),
            whole((width, qkv_width)),
            row_spec(width),
            whole((width, LANES)),
        ],
        out_specs=[
            row_spec(2 * kv_width),
            row_spec(feature),
            row_spec(feature),
            row_spec(LANES),
            whole((1, width)),
        ],
        out_shape=[
            jax.ShapeDtypeStruct((rows, 2 * kv_width), BF),
            jax.ShapeDtypeStruct((rows, feature), F32),
            jax.ShapeDtypeStruct((rows, feature), BF),
            jax.ShapeDtypeStruct((rows, LANES), F32),
            jax.ShapeDtypeStruct((1, width), F32),
        ],
        compiler_params=params("arbitrary"),
        name="project_back",
    )(
        tp_scalar,
        grad_q,
        grad_kv_own[0],
        from_peer[0],
        travel,
        cosine,
        sine,
        w_qkv,
        full_tokens,
        w_small,
    )
    dots = inner[:, 0]
    late = weight_grads(
        "late",
        [(normed, grad_q), (normed, grad_kv)],
        gain_one_term,
        0,
        q_width + 2 * kv_width + LANES,
    )
    grad_send, dots, *late = segment(sums[3:], grad_send, dots, *late)
    late_other = swap_core(late[1], "late")
    dots_other = swap_tp(dots, "dots")
    grad_other = swap_tp(grad_send, "grad_send")
    late_other, dots_other, grad_other = segment([], late_other, dots_other, grad_other)
    cols = early_other.shape[2] + late_other.shape[2]
    last = Scatter(
        ring,
        pl.pallas_call(
            functools.partial(order_kernel, bundle_places),
            in_specs=[smem] + [vmem] * 4,
            out_specs=[vmem] * len(bundle_places),
            out_shape=[jax.ShapeDtypeStruct((1, r, cols), BF) for _, _, r in bundle_places],
            compiler_params=params(),
            name="order",
        )(chip_list, early[0], early_other, late[0], late_other),
        "last",
    )
    last.moving = lock(*last.moving, late_other)[:-1]
    segment([last, sums[3]])
    grad_tokens = (
        grad_middle
        + grad_own
        + grad_other.astype(F32)
        - own_tokens.astype(F32) * (dots + dots_other)[:, None]
    )
    output = (half_at(middle, tp) + half_at(moe_sum, tp) + moe_other.astype(F32)).astype(BF)
    while not all(chain.done() for chain in [last, *sums]):
        segment([last, *[chain for chain in sums if not chain.done()][:1]])
    last = last.result()[0]
    early, late = last[:, : q_width + LANES], last[:, q_width + LANES :]
    grad_out = early[:, :q_width].T
    grad_router = early[:, q_width : q_width + experts]
    grad_gain_ffn = early[:, q_width + experts]
    grad_query = late[:, :q_width]
    key_cols, value_cols = [], []
    for pair in range(pairs):
        lo = q_width + pair * 2 * LANES
        key_cols.append(late[:, lo : lo + LANES])
        value_cols.append(late[:, lo + LANES : lo + 2 * LANES])
    grad_key = jnp.concatenate(key_cols, axis=1)
    grad_value = jnp.concatenate(value_cols, axis=1)
    gain_half = late[:, q_width + 2 * kv_width]
    grad_gain_attn = gain_half + swap_tp(gain_half, "gain_half")

    totals = jnp.concatenate([chain.result() for chain in sums], axis=0)
    totals = totals.reshape(per_core, 2, shard, 3 * hid)
    kept = lax.dynamic_index_in_dim(totals, core, 1, keepdims=False).astype(BF)
    sent = swap_core(lax.dynamic_index_in_dim(totals, 1 - core, 1, keepdims=False).astype(BF))
    all_experts = by_core(kept, sent, 0).astype(F32)
    grad_gate = all_experts[:, :, :hid]
    grad_up = all_experts[:, :, hid : 2 * hid]
    grad_down = all_experts[:, :, 2 * hid :].transpose(0, 2, 1)

    return (
        output.reshape(seqs, span, feature),
        grad_tokens.reshape(seqs, span, feature),
        grad_query,
        grad_key,
        grad_value,
        grad_out,
        grad_router,
        grad_gain_attn,
        grad_gain_ffn,
        grad_gate,
        grad_up,
        grad_down,
    )


def solution(mesh):
    in_specs = (
        P("fsdp", "ctx", "tp"),
        P("fsdp"),
        P("ctx", "fsdp", None, None),
        P(("fsdp", "ctx"), "tp"),
        P(("fsdp", "ctx"), "tp"),
        P(("fsdp", "ctx"), "tp"),
        P("tp", ("fsdp", "ctx")),
        P(("fsdp", "ctx"), None),
        P(("fsdp", "ctx")),
        P(("fsdp", "ctx")),
        P(None, ("fsdp", "ctx"), "tp"),
        P(None, ("fsdp", "ctx"), "tp"),
        P(None, "tp", ("fsdp", "ctx")),
        P("fsdp", "ctx", "tp"),
    )
    out_specs = (
        P("fsdp", "ctx", "tp"),
        P("fsdp", "ctx", "tp"),
        P(("fsdp", "ctx"), "tp"),
        P(("fsdp", "ctx"), "tp"),
        P(("fsdp", "ctx"), "tp"),
        P("tp", ("fsdp", "ctx")),
        P(("fsdp", "ctx"), None),
        P(("fsdp", "ctx")),
        P(("fsdp", "ctx")),
        P(None, ("fsdp", "ctx"), "tp"),
        P(None, ("fsdp", "ctx"), "tp"),
        P(None, "tp", ("fsdp", "ctx")),
    )
    return jax.shard_map(
        per_device, mesh=mesh, in_specs=in_specs, out_specs=out_specs, check_vma=False
    )
```

time: 589 us -> 475 us (0.81)
  local copies, waits for them, and re-layouts: 117 us -> 43.7 us
  other arithmetic: 63.3 us -> 26.5 us
  starting transfers between devices: 113 us -> 84.8 us
  waiting for transfers between devices: 151 us -> 173 us
  Pallas kernels: 126 us -> 135 us
    dynamic_update_slice x44 -> x0, local copies, waits for them, and re-layouts: 50.5 us -> none  [put(): lax.dynamic_update_slice(full, part[None], (self.chip(offset), 0, row, 0))]
    ppermute x88 -> x64, starting transfers between devices: 100 us -> 67.3 us  [send(): return lax.ppermute(array, RING, self.forward if forward else self.backward)]
    ppermute x88 -> x64, waiting for transfers between devices: 111 us -> 128 us  [send(): return lax.ppermute(array, RING, self.forward if forward else self.backward)]
    add x35 -> x32, other arithmetic: 32.9 us -> 15.9 us  [the longest x20 9.95 us: tick(): ahead, back = (near + self.moving[0], behind + self.moving[1])]
    unnamed x114 -> x254, local copies, waits for them, and re-layouts: 16 us -> 32 us
    slice x22 -> x6, local copies, waits for them, and re-layouts: 17.5 us -> 3.44 us  [tick(): ahead, back = (ahead[:, :half], back[:, half:])]
    select_n x5 -> x0, other arithmetic: 10 us -> none  [the longest x2 4.36 us: by_tp(): jnp.where(tp == 0, jnp.concatenate([mine, other], 1), jnp.concatenate([ot...]
    pallas_call x8 -> x18, Pallas kernels: 98.8 us -> 108 us  [the longest x4 65 us: run_experts(): pl.pallas_call(functools.partial(moe_kernel, first_call, last_call, exper...]
  transfers between devices with their start and end apart: 115 -> 95, of which waited for: 51 -> 44; matrix products, arithmetic and copies ran while one was open for 29% -> 6% of each run, Pallas kernels for 15% -> 27%
where the time goes in v2:
time: 475 us; the launch traced here: 466 us
  waiting for transfers between devices  173 us (36%)
  Pallas kernels  135 us (28%)
  starting transfers between devices  84.8 us (18%)
  local copies, waits for them, and re-layouts  43.7 us (9%)
  other arithmetic  26.5 us (6%)
    ppermute x64, waiting for transfers between devices, send(): return lax.ppermute(array, RING, self.forward if forward else self.backward)  128 us
    ppermute x64, starting transfers between devices, send(): return lax.ppermute(array, RING, self.forward if forward else self.backward)  67.3 us
    pallas_call x4, Pallas kernels, run_experts(): pl.pallas_call(functools.partial(moe_kernel, first_call, last_call, exper...  65 us
    unnamed x254, local copies, waits for them, and re-layouts  32 us
    ppermute x9, waiting for transfers between devices, swap_tp(): return lax.ppermute(array, 'tp', [(0, 1), (1, 0)])  31 us
    pallas_call x1, Pallas kernels, per_device(): pl.pallas_call(functools.partial(attend_back_kernel, ctx, span), grid=(se...  13.4 us
    pallas_call x1, Pallas kernels, per_device(): pl.pallas_call(functools.partial(moe_sum_kernel, places, GATHERS, calls,...  13.2 us
    pallas_call x1, Pallas kernels, per_device(): pl.pallas_call(functools.partial(attend_kernel, ctx, span), grid_spec=plt...  13.1 us
  transfers between devices with their start and end apart: 95, of which 44 were waited for; matrix products, arithmetic and copies ran while one was open for 6% of the time, Pallas kernels for 27%

profile of v2, /device:TPU:0, one launch (start us, length us, event | category | flops | bytes accessed | tf_op | source)
XLA Modules:
  0.0 465.6 jit_solution(12956478535856476405)
XLA Ops:
  11.5 5.8 %collective-permute-done.2.refs_2_ = bf16[1,64,1664]{2,1,0:T(8,128)(2,1)S(1)} collective-permute-done((bf16[1,64,1664]{2,1,0:T(8,128)(2,1)S(1)}, bf16[1,64,1664]{2,1,0:T(8,128)(2,1)S(1)}, u32[]{:S(2)}, u32[]{:S(2)}) %collective-permute-start.2) | collective-permute-done | bytes 213024 | tf_op jit(solution)/shard_map/bundle_step_1/ppermute | solution.py:600
  19.3 5.1 %collective-permute-done.3.refs_4_ = bf16[1,64,1664]{2,1,0:T(8,128)(2,1)} collective-permute-done((bf16[1,64,1664]{2,1,0:T(8,128)(2,1)S(1)}, bf16[1,64,1664]{2,1,0:T(8,128)(2,1)}, u32[]{:S(2)}, u32[]{:S(2)}) %collective-permute-start.3) | collective-permute-done | bytes 213024 | tf_op jit(solution)/shard_map/bundle_step_2/ppermute | solution.py:600
  42.5 3.5 assemble.1
  46.1 3.3 project.1
  58.1 8.8 %collective-permute-done.22.refs_1_ = bf16[512,512]{1,0:T(8,128)(2,1)S(1)} collective-permute-done((bf16[512,512]{1,0:T(8,128)(2,1)S(1)}, bf16[512,512]{1,0:T(8,128)(2,1)S(1)}, u32[]{:S(2)}, u32[]{:S(2)}) %collective-permute-start.22) | collective-permute-done | bytes 524320 | tf_op jit(solution)/shard_map/kv_over_y/ppermute | solution.py:721
  70.9 11.6 %collective-permute-done.10.refs_2_ = bf16[4,128,768]{2,1,0:T(8,128)(2,1)} collective-permute-done((bf16[4,128,768]{2,1,0:T(8,128)(2,1)S(1)}, bf16[4,128,768]{2,1,0:T(8,128)(2,1)}, u32[]{:S(2)}, u32[]{:S(2)}) %collective-permute-start.10) | collective-permute-done | bytes 786464 | tf_op jit(solution)/shard_map/weights_0_step_1/ppermute | solution.py:600
  92.2 13.1 %attend.1 = (bf16[512,512]{1,0:T(8,128)(2,1)}, bf16[2,4,512,1024]{3,2,1,0:T(8,128)(2,1)}) custom-call(s32[2]{0:T(128)S(1)} %copy-done.57, s32[4]{0:T(128)S(1)} %pad_add_fusion.base_ref, bf16[512,512]{1,0:T(8,128)(2,1)S(1)} %copy-done.19, bf16[512,512]{1,0:T(8,128)(2,1)S(1)} %copy-done.22, bf16[512,512]{1,0:T(8,128)(2,1)S(1)} %copy-done.25, ...), custom_call_target="tpu_custom_call" | custom-call | tf_op jit(solution)/shard_map/attend/pallas_call | solution.py:873
  105.2 4.1 collective-permute-done.27.wb_ref
  113.7 11.8 %collective-permute-done.30.b_ref = bf16[512,512]{1,0:T(8,128)(2,1)} collective-permute-done((bf16[512,512]{1,0:T(8,128)(2,1)}, bf16[512,512]{1,0:T(8,128)(2,1)}, u32[]{:S(2)}, u32[]{:S(2)}) %collective-permute-start.30) | collective-permute-done | bytes 524320 | tf_op jit(solution)/shard_map/attended_over_tp/ppermute | solution.py:714
  125.5 4.2 collective-permute-done.28.refs_5_
  131.8 5.4 %middle.1 = (f32[512,1024]{1,0:T(8,128)}, bf16[512,1152]{1,0:T(8,128)(2,1)}, f32[512,128]{1,0:T(8,128)S(1)}) custom-call(bf16[512,512]{1,0:T(8,128)(2,1)} %get-tuple-element.244.a_ref.refs_1_, bf16[512,512]{1,0:T(8,128)(2,1)} %collective-permute-done.30.b_ref, bf16[1024,512]{1,0:T(8,128)(2,1)} %get-tuple-element.242.wa_ref.wo_ref, ...), custom_call_target="tpu_custom_call" | custom-call | tf_op jit(solution)/shard_map/middle/pallas_call | solution.py:905
  143.4 14.3 %collective-permute-done.35.refs_2_.refs_11_ = bf16[4,128,768]{2,1,0:T(8,128)(2,1)} collective-permute-done((bf16[4,128,768]{2,1,0:T(8,128)(2,1)S(1)}, bf16[4,128,768]{2,1,0:T(8,128)(2,1)}, u32[]{:S(2)}, u32[]{:S(2)}) %collective-permute-start.35) | collective-permute-done | bytes 786464 | tf_op jit(solution)/shard_map/weights_1_step_1/ppermute | solution.py:600
  159.5 6.2 %collective-permute-done.33.refs_8_ = bf16[4,64,768]{2,1,0:T(8,128)(2,1)} collective-permute-done((bf16[4,64,768]{2,1,0:T(8,128)(2,1)S(1)}, bf16[4,64,768]{2,1,0:T(8,128)(2,1)}, u32[]{:S(2)}, u32[]{:S(2)}) %collective-permute-start.33) | collective-permute-done | bytes 393248 | tf_op jit(solution)/shard_map/weights_0_step_4/ppermute | solution.py:600
  170.0 15.5 %experts.4 = (f32[512,1152]{1,0:T(8,128)}, f32[512,1152]{1,0:T(8,128)}, bf16[2,1024,256]{2,1,0:T(8,128)(2,1)}, bf16[2,128,768]{2,1,0:T(8,128)(2,1)}, bf16[2,128,...) custom-call(s32[10]{0:T(128)} %stack.228.where_ref, ...), custom_call_target="tpu_custom_call" | custom-call | tf_op jit(solution)/shard_map/experts/pallas_call | solution.py:945
  191.4 16.4 %experts.5 = (f32[512,1152]{1,0:T(8,128)}, f32[512,1152]{1,0:T(8,128)}, bf16[2,1024,256]{2,1,0:T(8,128)(2,1)}, bf16[2,128,768]{2,1,0:T(8,128)(2,1)}, bf16[2,128,...) custom-call(s32[10]{0:T(128)} %stack.226.where_ref, ...), custom_call_target="tpu_custom_call" | custom-call | tf_op jit(solution)/shard_map/experts/pallas_call | solution.py:945
  216.9 6.8 %collective-permute-done.44.refs_8_.refs_17_ = bf16[4,64,768]{2,1,0:T(8,128)(2,1)} collective-permute-done((bf16[4,64,768]{2,1,0:T(8,128)(2,1)S(1)}, bf16[4,64,768]{2,1,0:T(8,128)(2,1)}, u32[]{:S(2)}, u32[]{:S(2)}) %collective-permute-start.44) | collective-permute-done | bytes 393248 | tf_op jit(solution)/shard_map/weights_1_step_4/ppermute | solution.py:600
  224.0 4.2 collective-permute-done.46
  235.2 16.5 %experts.6 = (f32[512,1152]{1,0:T(8,128)}, f32[512,1152]{1,0:T(8,128)}, bf16[2,1024,256]{2,1,0:T(8,128)(2,1)}, bf16[2,128,768]{2,1,0:T(8,128)(2,1)}, bf16[2,128,...) custom-call(s32[10]{0:T(128)} %stack.230.where_ref, ...), custom_call_target="tpu_custom_call" | custom-call | tf_op jit(solution)/shard_map/experts/pallas_call | solution.py:945
  260.7 16.6 %experts.7 = (f32[512,1152]{1,0:T(8,128)}, bf16[512,1152]{1,0:T(8,128)(2,1)}, bf16[2,1024,256]{2,1,0:T(8,128)(2,1)}, bf16[2,128,768]{2,1,0:T(8,128)(2,1)}, bf16[...) custom-call(s32[10]{0:T(128)} %stack.232.where_ref, ...), custom_call_target="tpu_custom_call" | custom-call | tf_op jit(solution)/shard_map/experts/pallas_call | solution.py:945
  281.5 3.6 collective-permute-done.57
  303.8 13.2 %experts_output.1 = (f32[512,1024]{1,0:T(8,128)S(1)}, bf16[512,1024]{1,0:T(8,128)(2,1)}) custom-call(s32[10]{0:T(128)S(1)} %stack.233.where_ref, bf16[4,128,768]{2,1,0:T(8,128)(2,1)} %copy-done.5, bf16[4,128,768]{2,1,0:T(8,128)(2,1)} %collective-permute-done.9.refs_1_, bf16[4,128,768]{2,1,0:T(8,128)(2,1)} %collective-permute-done.10.refs_2_, ...), custom_call_target="tpu_custom_call" | custom-call | tf_op jit(solution)/shard_map/experts_output/pallas_call | solution.py:1013
  317.0 4.7 %collective-permute-done.62.sb_ref = bf16[512,1152]{1,0:T(8,128)(2,1)} collective-permute-done((bf16[512,1152]{1,0:T(8,128)(2,1)}, bf16[512,1152]{1,0:T(8,128)(2,1)}, u32[]{:S(2)}, u32[]{:S(2)}) %collective-permute-start.62) | collective-permute-done | bytes 1179680 | tf_op jit(solution)/shard_map/part_over_tp/ppermute | solution.py:714
  324.2 4.7 %middle_back.1 = (f32[512,512]{1,0:T(8,128)S(1)}, bf16[512,1024]{1,0:T(8,128)(2,1)S(1)}, bf16[512,512]{1,0:T(8,128)(2,1)S(1)}, bf16[512,128]{1,0:T(8,128)(2,1)S(1)}, f32[1,1024]{1,0:T(1,128)S(1)}) custom-call(s32[1]{0:T(128)} %bitcast.3.tp_ref, bf16[512,1152]{1,0:T(8,128)(2,1)} %add_terms.1.sa_ref, bf16[512,1152]{1,0:T(8,128)(2,1)} %collective-permute-done.62.sb_ref, ...), custom_call_target="tpu_custom_call" | custom-call | tf_op jit(solution)/shard_map/middle_back/pallas_call | solution.py:1036
  329.9 13.4 %attend_back.1 = (bf16[512,512]{1,0:T(8,128)(2,1)S(1)}, bf16[2,512,512]{2,1,0:T(8,128)(2,1)S(1)}, bf16[2,512,512]{2,1,0:T(8,128)(2,1)}) custom-call(bf16[2,4,512,1024]{3,2,1,0:T(8,128)(2,1)} %get-tuple-element.331.p_ref, bf16[512,512]{1,0:T(8,128)(2,1)S(1)} %copy-done.20, bf16[512,512]{1,0:T(8,128)(2,1)S(1)} %get-tuple-element.334.g_ref, ...), custom_call_target="tpu_custom_call" | custom-call | tf_op jit(solution)/shard_map/attend_back/pallas_call | solution.py:1078
  351.2 4.9 %collective-permute-done.68.refs_1_ = bf16[8,64,640]{2,1,0:T(8,128)(2,1)} collective-permute-done((bf16[8,64,640]{2,1,0:T(8,128)(2,1)}, bf16[8,64,640]{2,1,0:T(8,128)(2,1)}, u32[]{:S(2)}, u32[]{:S(2)}) %collective-permute-start.68) | collective-permute-done | bytes 655392 | tf_op jit(solution)/shard_map/early_over_core/ppermute | solution.py:710
  367.9 16.3 %collective-permute-done.70 = bf16[2,128,768]{2,1,0:T(8,128)(2,1)S(1)} collective-permute-done((bf16[2,128,768]{2,1,0:T(8,128)(2,1)S(1)}, bf16[2,128,768]{2,1,0:T(8,128)(2,1)S(1)}, u32[]{:S(2)}, u32[]{:S(2)}) %collective-permute-start.70) | collective-permute-done | bytes 393248 | tf_op jit(solution)/shard_map/sums_2_step_3/ppermute | solution.py:600
  392.6 3.9 collective-permute-done.76
  396.5 6.7 %collective-permute-done.74 = bf16[2,128,768]{2,1,0:T(8,128)(2,1)S(1)} collective-permute-done((bf16[2,128,768]{2,1,0:T(8,128)(2,1)S(1)}, bf16[2,128,768]{2,1,0:T(8,128)(2,1)S(1)}, u32[]{:S(2)}, u32[]{:S(2)}) %collective-permute-start.74) | collective-permute-done | bytes 393248 | tf_op jit(solution)/shard_map/sums_2_step_4/ppermute | solution.py:600
  413.7 8.8 %collective-permute-done.81 = f32[512]{0:T(512)S(1)} collective-permute-done((f32[512]{0:T(512)S(1)}, f32[512]{0:T(512)S(1)}, u32[]{:S(2)}, u32[]{:S(2)}) %collective-permute-start.81) | collective-permute-done | bytes 2080 | tf_op jit(solution)/shard_map/dots_over_tp/ppermute | solution.py:714
  429.7 5.6 %collective-permute-done.83 = bf16[1,32,1792]{2,1,0:T(8,128)(2,1)S(1)} collective-permute-done((bf16[1,32,1792]{2,1,0:T(8,128)(2,1)S(1)}, bf16[1,32,1792]{2,1,0:T(8,128)(2,1)S(1)}, u32[]{:S(2)}, u32[]{:S(2)}) %collective-permute-start.83) | collective-permute-done | bytes 114720 | tf_op jit(solution)/shard_map/last_step_1/ppermute | solution.py:600
  445.8 4.6 collective-permute-done.90
  454.1 3.5 collective-permute-done.92
  (518 shorter events, 195.2 us)
Async XLA Ops:
  8.3 24.0 %collective-permute-start.6 = (bf16[8,64,768]{2,1,0:T(8,128)(2,1)S(1)}, bf16[8,64,768]{2,1,0:T(8,128)(2,1)S(1)}, u32[]{:S(2)}, u32[]{:S(2)}) collective-permute-start(bf16[8,64,768]{2,1,0:T(8,128)(2,1)S(1)} %get-tuple-element.223), channel_id=1, source_target_pairs={{0,2},{2,0},{4,6},{6,4},{1,3},{3,1},{5,7},{7,5},{8,10},{10,8},{12,... | collective-permute-start | bytes 2359304 | tf_op jit(solution)/shard_map/other_w_over_core/ppermute | solution.py:710
  53.7 28.7 %collective-permute-start.10 = (bf16[4,128,768]{2,1,0:T(8,128)(2,1)S(1)}, bf16[4,128,768]{2,1,0:T(8,128)(2,1)}, u32[]{:S(2)}, u32[]{:S(2)}) collective-permute-start(bf16[4,128,768]{2,1,0:T(8,128)(2,1)S(1)} %get-tuple-element.228.refs_0_), channel_id=1, source_target_pairs={{8,0},{16,8},{24,16},{28,24},{20,28},{12,20},{4,12},{0,4},{10,2},{... | collective-permute-start | bytes 2359304 | tf_op jit(solution)/shard_map/weights_0_step_1/ppermute | solution.py:600
  54.2 29.3 %collective-permute-start.9 = (bf16[4,128,768]{2,1,0:T(8,128)(2,1)S(1)}, bf16[4,128,768]{2,1,0:T(8,128)(2,1)}, u32[]{:S(2)}, u32[]{:S(2)}) collective-permute-start(bf16[4,128,768]{2,1,0:T(8,128)(2,1)S(1)} %get-tuple-element.228.refs_0_), channel_id=1, source_target_pairs={{0,8},{8,16},{16,24},{24,28},{28,20},{20,12},{12,4},{4,0},{2,10},{... | collective-permute-start | bytes 2359304 | tf_op jit(solution)/shard_map/weights_0_step_1/ppermute | solution.py:600
  84.2 25.1 %collective-permute-start.27 = (bf16[1024,512]{1,0:T(8,128)(2,1)}, bf16[1024,512]{1,0:T(8,128)(2,1)}, u32[]{:S(2)}, u32[]{:S(2)}) collective-permute-start(bf16[1024,512]{1,0:T(8,128)(2,1)} %get-tuple-element.242.wa_ref.wo_ref), channel_id=1, source_target_pairs={{0,1},{1,0},{2,3},{3,2},{4,5},{5,4},{6,7},{7,6},{8,9},{9,8},{10,11... | collective-permute-start | bytes 3145736 | tf_op jit(solution)/shard_map/wo_mine_over_tp/ppermute | solution.py:714
  109.4 20.3 %collective-permute-start.31 = (bf16[512,1024]{1,0:T(8,128)(2,1)S(1)}, bf16[512,1024]{1,0:T(8,128)(2,1)}, u32[]{:S(2)}, u32[]{:S(2)}) collective-permute-start(bf16[512,1024]{1,0:T(8,128)(2,1)S(1)} %copy-done), channel_id=1, source_target_pairs={{0,2},{2,0},{4,6},{6,4},{1,3},{3,1},{5,7},{7,5},{8,10},{10,8},{12,... | collective-permute-start | bytes 3145736 | tf_op jit(solution)/shard_map/full_cot_over_core/ppermute | solution.py:710
  109.4 20.3 %collective-permute-start.28 = (bf16[4,128,768]{2,1,0:T(8,128)(2,1)}, bf16[4,128,768]{2,1,0:T(8,128)(2,1)}, u32[]{:S(2)}, u32[]{:S(2)}) collective-permute-start(bf16[4,128,768]{2,1,0:T(8,128)(2,1)} %collective-permute-done.25.refs_3_), channel_id=1, source_target_pairs={{0,8},{8,16},{16,24},{24,28},{28,20},{20,12},{12,4},{4,0},{2,10},{... | collective-permute-start | bytes 2359304 | tf_op jit(solution)/shard_map/weights_0_step_3/ppermute | solution.py:600
  109.4 20.3 %collective-permute-start.29 = (bf16[4,128,768]{2,1,0:T(8,128)(2,1)}, bf16[4,128,768]{2,1,0:T(8,128)(2,1)}, u32[]{:S(2)}, u32[]{:S(2)}) collective-permute-start(bf16[4,128,768]{2,1,0:T(8,128)(2,1)} %collective-permute-done.26.refs_4_), channel_id=1, source_target_pairs={{8,0},{16,8},{24,16},{28,24},{20,28},{12,20},{4,12},{0,4},{10,2},{... | collective-permute-start | bytes 2359304 | tf_op jit(solution)/shard_map/weights_0_step_3/ppermute | solution.py:600
  137.2 30.0 %collective-permute-start.36 = (bf16[512,1152]{1,0:T(8,128)(2,1)}, bf16[512,1152]{1,0:T(8,128)(2,1)}, u32[]{:S(2)}, u32[]{:S(2)}) collective-permute-start(bf16[512,1152]{1,0:T(8,128)(2,1)} %get-tuple-element.254.refs_9_.refs_2_), channel_id=1, source_target_pairs={{0,2},{2,0},{4,6},{6,4},{1,3},{3,1},{5,7},{7,5},{8,10},{10,8},{12,... | collective-permute-start | bytes 3538952 | tf_op jit(solution)/shard_map/normed_two_over_core/ppermute | solution.py:710
  137.2 20.5 %collective-permute-start.35 = (bf16[4,128,768]{2,1,0:T(8,128)(2,1)S(1)}, bf16[4,128,768]{2,1,0:T(8,128)(2,1)}, u32[]{:S(2)}, u32[]{:S(2)}) collective-permute-start(bf16[4,128,768]{2,1,0:T(8,128)(2,1)S(1)} %copy-done.4), channel_id=1, source_target_pairs={{8,0},{16,8},{24,16},{28,24},{20,28},{12,20},{4,12},{0,4},{10,2},{... | collective-permute-start | bytes 2359304 | tf_op jit(solution)/shard_map/weights_1_step_1/ppermute | solution.py:600
  139.0 20.5 %collective-permute-start.34 = (bf16[4,128,768]{2,1,0:T(8,128)(2,1)S(1)}, bf16[4,128,768]{2,1,0:T(8,128)(2,1)}, u32[]{:S(2)}, u32[]{:S(2)}) collective-permute-start(bf16[4,128,768]{2,1,0:T(8,128)(2,1)S(1)} %copy-done.4), channel_id=1, source_target_pairs={{0,8},{8,16},{16,24},{24,28},{28,20},{20,12},{12,4},{4,0},{2,10},{... | collective-permute-start | bytes 2359304 | tf_op jit(solution)/shard_map/weights_1_step_1/ppermute | solution.py:600
  141.4 24.3 %collective-permute-start.33 = (bf16[4,64,768]{2,1,0:T(8,128)(2,1)S(1)}, bf16[4,64,768]{2,1,0:T(8,128)(2,1)}, u32[]{:S(2)}, u32[]{:S(2)}) collective-permute-start(bf16[4,64,768]{2,1,0:T(8,128)(2,1)S(1)} %slice.143), channel_id=1, source_target_pairs={{8,0},{16,8},{24,16},{28,24},{20,28},{12,20},{4,12},{0,4},{10,2},{... | collective-permute-start | bytes 1179656 | tf_op jit(solution)/shard_map/weights_0_step_4/ppermute | solution.py:600
  143.2 24.0 %collective-permute-start.32 = (bf16[4,64,768]{2,1,0:T(8,128)(2,1)S(1)}, bf16[4,64,768]{2,1,0:T(8,128)(2,1)}, u32[]{:S(2)}, u32[]{:S(2)}) collective-permute-start(bf16[4,64,768]{2,1,0:T(8,128)(2,1)S(1)} %slice.142), channel_id=1, source_target_pairs={{0,8},{8,16},{16,24},{24,28},{28,20},{20,12},{12,4},{4,0},{2,10},{... | collective-permute-start | bytes 1179656 | tf_op jit(solution)/shard_map/weights_0_step_4/ppermute | solution.py:600
  186.4 23.7 %collective-permute-start.39 = (bf16[4,128,768]{2,1,0:T(8,128)(2,1)}, bf16[4,128,768]{2,1,0:T(8,128)(2,1)S(1)}, u32[]{:S(2)}, u32[]{:S(2)}) collective-permute-start(bf16[4,128,768]{2,1,0:T(8,128)(2,1)} %collective-permute-done.37.refs_3_.refs_12_), channel_id=1, source_target_pairs={{0,8},{8,16},{16,24},{24,28},{28,20},{20,12},{12,4},{4,0},{2,10},{... | collective-permute-start | bytes 2359304 | tf_op jit(solution)/shard_map/weights_1_step_3/ppermute | solution.py:600
  188.0 22.2 %collective-permute-start.40 = (bf16[4,128,768]{2,1,0:T(8,128)(2,1)}, bf16[4,128,768]{2,1,0:T(8,128)(2,1)}, u32[]{:S(2)}, u32[]{:S(2)}) collective-permute-start(bf16[4,128,768]{2,1,0:T(8,128)(2,1)} %collective-permute-done.38.refs_4_.refs_13_), channel_id=1, source_target_pairs={{8,0},{16,8},{24,16},{28,24},{20,28},{12,20},{4,12},{0,4},{10,2},{... | collective-permute-start | bytes 2359304 | tf_op jit(solution)/shard_map/weights_1_step_3/ppermute | solution.py:600
  188.5 20.1 %collective-permute-start.41 = (bf16[2,64,768]{2,1,0:T(8,128)(2,1)}, bf16[2,64,768]{2,1,0:T(8,128)(2,1)S(1)}, u32[]{:S(2)}, u32[]{:S(2)}) collective-permute-start(bf16[2,64,768]{2,1,0:T(8,128)(2,1)} %get-tuple-element.269), channel_id=1, source_target_pairs={{0,8},{8,16},{16,24},{24,28},{28,20},{20,12},{12,4},{4,0},{2,10},{... | collective-permute-start | bytes 589832 | tf_op jit(solution)/shard_map/sums_0_step_1/ppermute | solution.py:600
  190.0 20.1 %collective-permute-start.42 = (bf16[2,64,768]{2,1,0:T(8,128)(2,1)}, bf16[2,64,768]{2,1,0:T(8,128)(2,1)}, u32[]{:S(2)}, u32[]{:S(2)}) collective-permute-start(bf16[2,64,768]{2,1,0:T(8,128)(2,1)} %get-tuple-element.270), channel_id=1, source_target_pairs={{8,0},{16,8},{24,16},{28,24},{20,28},{12,20},{4,12},{0,4},{10,2},{... | collective-permute-start | bytes 589832 | tf_op jit(solution)/shard_map/sums_0_step_1/ppermute | solution.py:600
  229.2 22.6 %collective-permute-start.48 = (bf16[2,128,768]{2,1,0:T(8,128)(2,1)}, bf16[2,128,768]{2,1,0:T(8,128)(2,1)S(1)}, u32[]{:S(2)}, u32[]{:S(2)}) collective-permute-start(bf16[2,128,768]{2,1,0:T(8,128)(2,1)} %add.539), channel_id=1, source_target_pairs={{8,0},{16,8},{24,16},{28,24},{20,28},{12,20},{4,12},{0,4},{10,2},{... | collective-permute-start | bytes 1179656 | tf_op jit(solution)/shard_map/sums_0_step_3/ppermute | solution.py:600
  231.5 20.3 %collective-permute-start.47 = (bf16[2,128,768]{2,1,0:T(8,128)(2,1)}, bf16[2,128,768]{2,1,0:T(8,128)(2,1)}, u32[]{:S(2)}, u32[]{:S(2)}) collective-permute-start(bf16[2,128,768]{2,1,0:T(8,128)(2,1)} %add.538), channel_id=1, source_target_pairs={{0,8},{8,16},{16,24},{24,28},{28,20},{20,12},{12,4},{4,0},{2,10},{... | collective-permute-start | bytes 1179656 | tf_op jit(solution)/shard_map/sums_0_step_3/ppermute | solution.py:600
  232.1 19.6 %collective-permute-start.49 = (bf16[2,64,768]{2,1,0:T(8,128)(2,1)}, bf16[2,64,768]{2,1,0:T(8,128)(2,1)S(1)}, u32[]{:S(2)}, u32[]{:S(2)}) collective-permute-start(bf16[2,64,768]{2,1,0:T(8,128)(2,1)} %get-tuple-element.284), channel_id=1, source_target_pairs={{0,8},{8,16},{16,24},{24,28},{28,20},{20,12},{12,4},{4,0},{2,10},{... | collective-permute-start | bytes 589832 | tf_op jit(solution)/shard_map/sums_1_step_1/ppermute | solution.py:600
  253.0 24.3 %collective-permute-start.54 = (bf16[2,128,768]{2,1,0:T(8,128)(2,1)S(1)}, bf16[2,128,768]{2,1,0:T(8,128)(2,1)}, u32[]{:S(2)}, u32[]{:S(2)}) collective-permute-start(bf16[2,128,768]{2,1,0:T(8,128)(2,1)S(1)} %pad_maximum_fusion.4), channel_id=1, source_target_pairs={{8,0},{16,8},{24,16},{28,24},{20,28},{12,20},{4,12},{0,4},{10,2},{... | collective-permute-start | bytes 1179656 | tf_op jit(solution)/shard_map/sums_1_step_2/ppermute | solution.py:600
  254.5 22.8 %collective-permute-start.53 = (bf16[2,128,768]{2,1,0:T(8,128)(2,1)S(1)}, bf16[2,128,768]{2,1,0:T(8,128)(2,1)}, u32[]{:S(2)}, u32[]{:S(2)}) collective-permute-start(bf16[2,128,768]{2,1,0:T(8,128)(2,1)S(1)} %pad_maximum_fusion.3), channel_id=1, source_target_pairs={{0,8},{8,16},{16,24},{24,28},{28,20},{20,12},{12,4},{4,0},{2,10},{... | collective-permute-start | bytes 1179656 | tf_op jit(solution)/shard_map/sums_1_step_2/ppermute | solution.py:600
  256.1 21.3 %collective-permute-start.52 = (bf16[2,128,768]{2,1,0:T(8,128)(2,1)}, bf16[2,128,768]{2,1,0:T(8,128)(2,1)}, u32[]{:S(2)}, u32[]{:S(2)}) collective-permute-start(bf16[2,128,768]{2,1,0:T(8,128)(2,1)} %add.542), channel_id=1, source_target_pairs={{8,0},{16,8},{24,16},{28,24},{20,28},{12,20},{4,12},{0,4},{10,2},{... | collective-permute-start | bytes 1179656 | tf_op jit(solution)/shard_map/sums_0_step_4/ppermute | solution.py:600
  294.2 27.5 %collective-permute-start.62 = (bf16[512,1152]{1,0:T(8,128)(2,1)}, bf16[512,1152]{1,0:T(8,128)(2,1)}, u32[]{:S(2)}, u32[]{:S(2)}) collective-permute-start(bf16[512,1152]{1,0:T(8,128)(2,1)} %add_terms.1.sa_ref), channel_id=1, source_target_pairs={{0,1},{1,0},{2,3},{3,2},{4,5},{5,4},{6,7},{7,6},{8,9},{9,8},{10,11... | collective-permute-start | bytes 3538952 | tf_op jit(solution)/shard_map/part_over_tp/ppermute | solution.py:714
  296.9 20.1 %collective-permute-start.56 = (bf16[2,128,768]{2,1,0:T(8,128)(2,1)S(1)}, bf16[2,128,768]{2,1,0:T(8,128)(2,1)S(1)}, u32[]{:S(2)}, u32[]{:S(2)}) collective-permute-start(bf16[2,128,768]{2,1,0:T(8,128)(2,1)S(1)} %add.547), channel_id=1, source_target_pairs={{8,0},{16,8},{24,16},{28,24},{20,28},{12,20},{4,12},{0,4},{10,2},{... | collective-permute-start | bytes 1179656 | tf_op jit(solution)/shard_map/sums_1_step_3/ppermute | solution.py:600
  301.3 47.8 %collective-permute-start.66 = (bf16[2,128,768]{2,1,0:T(8,128)(2,1)S(1)}, bf16[2,128,768]{2,1,0:T(8,128)(2,1)S(1)}, u32[]{:S(2)}, u32[]{:S(2)}) collective-permute-start(bf16[2,128,768]{2,1,0:T(8,128)(2,1)S(1)} %pad_maximum_fusion.6), channel_id=1, source_target_pairs={{8,0},{16,8},{24,16},{28,24},{20,28},{12,20},{4,12},{0,4},{10,2},{... | collective-permute-start | bytes 1179656 | tf_op jit(solution)/shard_map/sums_2_step_2/ppermute | solution.py:600
  302.2 47.0 %collective-permute-start.65 = (bf16[2,128,768]{2,1,0:T(8,128)(2,1)S(1)}, bf16[2,128,768]{2,1,0:T(8,128)(2,1)S(1)}, u32[]{:S(2)}, u32[]{:S(2)}) collective-permute-start(bf16[2,128,768]{2,1,0:T(8,128)(2,1)S(1)} %pad_maximum_fusion.5), channel_id=1, source_target_pairs={{0,8},{8,16},{16,24},{24,28},{28,20},{20,12},{12,4},{4,0},{2,10},{... | collective-permute-start | bytes 1179656 | tf_op jit(solution)/shard_map/sums_2_step_2/ppermute | solution.py:600
  321.8 28.1 %collective-permute-start.63 = (bf16[2,128,768]{2,1,0:T(8,128)(2,1)S(1)}, bf16[2,128,768]{2,1,0:T(8,128)(2,1)}, u32[]{:S(2)}, u32[]{:S(2)}) collective-permute-start(bf16[2,128,768]{2,1,0:T(8,128)(2,1)S(1)} %add.548), channel_id=1, source_target_pairs={{0,8},{8,16},{16,24},{24,28},{28,20},{20,12},{12,4},{4,0},{2,10},{... | collective-permute-start | bytes 1179656 | tf_op jit(solution)/shard_map/sums_1_step_4/ppermute | solution.py:600
  323.4 27.2 %collective-permute-start.64 = (bf16[2,128,768]{2,1,0:T(8,128)(2,1)S(1)}, bf16[2,128,768]{2,1,0:T(8,128)(2,1)}, u32[]{:S(2)}, u32[]{:S(2)}) collective-permute-start(bf16[2,128,768]{2,1,0:T(8,128)(2,1)S(1)} %add.549), channel_id=1, source_target_pairs={{8,0},{16,8},{24,16},{28,24},{20,28},{12,20},{4,12},{0,4},{10,2},{... | collective-permute-start | bytes 1179656 | tf_op jit(solution)/shard_map/sums_1_step_4/ppermute | solution.py:600
  361.7 22.8 %collective-permute-start.72 = (bf16[512,512]{1,0:T(8,128)(2,1)S(1)}, bf16[512,512]{1,0:T(8,128)(2,1)S(1)}, u32[]{:S(2)}, u32[]{:S(2)}) collective-permute-start(bf16[512,512]{1,0:T(8,128)(2,1)S(1)} %get-tuple-element.354), channel_id=1, source_target_pairs={{0,4},{2,6},{4,0},{6,2},{1,5},{3,7},{5,1},{7,3},{8,12},{10,14},{12... | collective-permute-start | bytes 1572872 | tf_op jit(solution)/shard_map/grad_kv_over_y/ppermute | solution.py:721
  362.8 21.7 %collective-permute-start.73 = (bf16[512,512]{1,0:T(8,128)(2,1)S(1)}, bf16[512,512]{1,0:T(8,128)(2,1)S(1)}, u32[]{:S(2)}, u32[]{:S(2)}) collective-permute-start(bf16[512,512]{1,0:T(8,128)(2,1)S(1)} %dynamic-slice_convert_fusion), channel_id=1, source_target_pairs={{0,1},{1,0},{2,3},{3,2},{4,5},{5,4},{6,7},{7,6},{8,9},{9,8},{10,11... | collective-permute-start | bytes 1572872 | tf_op jit(solution)/shard_map/moe_send_over_tp/ppermute | solution.py:714
  364.5 19.7 %collective-permute-start.70 = (bf16[2,128,768]{2,1,0:T(8,128)(2,1)S(1)}, bf16[2,128,768]{2,1,0:T(8,128)(2,1)S(1)}, u32[]{:S(2)}, u32[]{:S(2)}) collective-permute-start(bf16[2,128,768]{2,1,0:T(8,128)(2,1)S(1)} %add.554), channel_id=1, source_target_pairs={{0,8},{8,16},{16,24},{24,28},{28,20},{20,12},{12,4},{4,0},{2,10},{... | collective-permute-start | bytes 1179656 | tf_op jit(solution)/shard_map/sums_2_step_3/ppermute | solution.py:600
  366.8 25.8 %collective-permute-start.77 = (bf16[2,128,768]{2,1,0:T(8,128)(2,1)S(1)}, bf16[2,128,768]{2,1,0:T(8,128)(2,1)S(1)}, u32[]{:S(2)}, u32[]{:S(2)}) collective-permute-start(bf16[2,128,768]{2,1,0:T(8,128)(2,1)S(1)} %pad_maximum_fusion.8), channel_id=1, source_target_pairs={{8,0},{16,8},{24,16},{28,24},{20,28},{12,20},{4,12},{0,4},{10,2},{... | collective-permute-start | bytes 1179656 | tf_op jit(solution)/shard_map/sums_3_step_2/ppermute | solution.py:600
  (188 other events, 1528.0 us)

commit v3 on v2

--- a/solution.py
+++ b/solution.py
@@ -59,42 +59,49 @@
     return nt(jnp.where(lane == column, 1.0, 0.0).astype(BF), ref[...])[:1]
 
 
-def pack_kernel(q_ref, k_ref, v_ref, out_ref, router_ref, one_ref, two_ref, packed_ref):
+def pack_kernel(q_ref, k_ref, v_ref, out_ref, router_ref, one_ref, two_ref, packed_ref, *scratch):
+    stage, sem = scratch
     rows, q_width = q_ref.shape
-    packed_ref[0, :, :q_width] = q_ref[...]
-    at = q_width
+    copies, at = [], 0
+
+    def copy(source, width):
+        nonlocal at
+        copies.append(pltpu.make_async_copy(source, packed_ref.at[0, :, pl.ds(at, width)], sem))
+        copies[-1].start()
+        at += width
+
+    copy(q_ref, q_width)
     for pair in range(k_ref.shape[1] // LANES):
-        cols = slice(pair * LANES, (pair + 1) * LANES)
-        packed_ref[0, :, at : at + LANES] = k_ref[:, cols]
-        packed_ref[0, :, at + LANES : at + 2 * LANES] = v_ref[:, cols]
-        at += 2 * LANES
-    packed_ref[0, :, at : at + q_width] = out_ref[...].T
-    at += q_width
-    experts = router_ref.shape[1]
-    square = (rows, rows)
-    diagonal = lax.broadcasted_iota(jnp.int32, square, 0) == lax.broadcasted_iota(
-        jnp.int32, square, 1
-    )
-    gains = [
-        jnp.sum(jnp.where(diagonal, r[...].astype(F32), 0.0), axis=1, keepdims=True)
-        for r in (one_ref, two_ref)
-    ]
-    lane = lax.broadcasted_iota(jnp.int32, (rows, LANES), 1)
-    wide = jnp.where(lane == experts, gains[0], 0.0)
-    wide = jnp.where(lane == experts + 1, gains[1], wide)
-    packed_ref[0, :, at:] = wide.astype(BF)
-    packed_ref[0, :, at : at + experts] = router_ref[...]
-
-
-def pack_experts_kernel(core_ref, gate_ref, up_ref, down_ref, mine_ref, other_ref):
+        cols = pl.ds(pair * LANES, LANES)
+        copy(k_ref.at[:, cols], LANES)
+        copy(v_ref.at[:, cols], LANES)
+    copy(out_ref, q_width)
+    experts = router_ref.shape[0]
+    stage[...] = jnp.zeros(stage.shape, F32)
+    stage[:experts, :rows] = router_ref[...].astype(F32)
+    stage[experts : experts + 1, :rows] = one_ref[...].astype(F32)
+    stage[experts + 1 : experts + 2, :rows] = two_ref[...].astype(F32)
+    packed_ref[0, :, at:] = stage[...].T[:rows].astype(BF)
+    for each in copies:
+        each.wait()
+
+
+def pack_experts_kernel(core_ref, gate_ref, up_ref, down_ref, mine_ref, other_ref, sem):
     count, _, cols = mine_ref.shape
     hid = cols // 3
+    copies = []
     for out_ref, core in ((mine_ref, core_ref[0]), (other_ref, 1 - core_ref[0])):
-        for i in range(count):
-            e = core * count + i
-            out_ref[i, :, :hid] = gate_ref[e]
-            out_ref[i, :, hid : 2 * hid] = up_ref[e]
-            out_ref[i, :, 2 * hid :] = down_ref[e].T
+        for i, source in enumerate((gate_ref, up_ref, down_ref)):
+            copies.append(
+                pltpu.make_async_copy(
+                    source.at[pl.ds(core * count, count)],
+                    out_ref.at[:, :, pl.ds(i * hid, hid)],
+                    sem,
+                )
+            )
+            copies[-1].start()
+    for copy in copies:
+        copy.wait()
 
 
 def join_kernel(core_ref, mine_ref, other_ref, *groups):
@@ -285,11 +292,12 @@
     return jnp.where(lane < experts, both, 0.0)
 
 
-def moe_kernel(first_call, last_call, experts, start, group, places, where_ref, *refs):
+def moe_kernel(first_call, last_call, joins, experts, column, start, group, places, where_ref, *refs):
     count = len(places)
     w_parts, refs = refs[:count], refs[count:]
     sources, refs = refs[:4], refs[4:]
     inits, refs = ((), refs) if first_call else (refs[:2], refs[2:])
+    refs = refs[count:] if joins else refs
     outs, mixed_out, dw_parts, refs = refs[:2], refs[2], refs[3 : 3 + count], refs[3 + count :]
     here, accs, refs = refs[:4], refs[4:6], refs[6:]
     mixed_all, narrow, w_all, dw_all, w_sem, dw_sem, near_sem, acc_sem, out_sem, mixed_sem = refs
@@ -307,7 +315,7 @@
 
     def store(e, j):
         return pltpu.make_async_copy(
-            dw_all.at[e % 2, window(j)], dw_parts[j].at[e], dw_sem.at[e % 2]
+            dw_all.at[e % 2, window(j)], dw_parts[j].at[start + e], dw_sem.at[e % 2]
         )
 
     nears = [
@@ -330,7 +338,7 @@
                 copy.wait()
             for copy in [*fetches[:1], *nears[2:], *fetches[1:]]:
                 copy.start()
-        expert = where_ref[0] + e
+        expert = where_ref[0] + column + e
         w_gu, w_d = w_all[e, :, : 2 * hid], w_all[e, :, 2 * hid :]
         kept = []
         for side, (x_ref, y_ref) in enumerate(((xa_ref, ya_ref), (xb_ref, yb_ref))):
@@ -400,55 +408,55 @@
     w_sets = [refs[k * count : (k + 1) * count] for k in range(sets)]
     refs = refs[sets * count :]
     mixed_parts, refs = refs[:calls], refs[calls:]
-    own_ref, peer_ref, w_all, mixed_all, total, w_sem, mixed_sem = refs
-    hid = w_all.shape[2]
+    own_ref, peer_ref, w_all, mixed_all, w_sem, mixed_sem = refs
     rows = own_ref.shape[0]
-    experts = calls * group
-    set_size = experts // sets
-
-    def loads(e):
-        for j in range(count):
+    size = calls * group // sets
+    hid = w_all.shape[2] // size
+
+    def loads(k):
+        for i in range(size):
+            cols = pl.ds(i * hid, hid)
+            for j in range(count):
+                yield pltpu.make_async_copy(
+                    w_sets[k][j].at[i, :, pl.ds(2 * hid, hid)],
+                    w_all.at[k, pl.ds(pl.multiple_of(where_ref[1 + j], 16), places[j][2]), cols],
+                    w_sem.at[k],
+                )
+            e = k * size + i
             yield pltpu.make_async_copy(
-                w_sets[e // set_size][j].at[e % set_size, :, pl.ds(2 * hid, hid)],
-                w_all.at[e % 2, pl.ds(pl.multiple_of(where_ref[1 + j], 16), places[j][2])],
-                w_sem.at[e % 2],
+                mixed_parts[e // group].at[e % group], mixed_all.at[k, :, cols], mixed_sem.at[k]
             )
-        yield pltpu.make_async_copy(
-            mixed_parts[e // group].at[e % group], mixed_all.at[e % 2], mixed_sem.at[e % 2]
-        )
-
-    for copy in loads(0):
-        copy.start()
-    for e in range(experts):
-        for copy in loads(e):
+
+    for k in range(sets):
+        for copy in loads(k):
+            copy.start()
+    total = None
+    for k in range(sets):
+        for copy in loads(k):
             copy.wait()
-        if e + 1 < experts:
-            for copy in loads(e + 1):
-                copy.start()
-        term = nt(mixed_all[e % 2], w_all[e % 2])
-        if e == 0:
-            total[...] = term
-        else:
-            total[...] += term
+        term = nt(mixed_all[k], w_all[k])
+        total = term if total is None else total + term
     own_ref[...] = total[:rows]
     peer_ref[...] = total[rows:].astype(BF)
 
 
-def weight_grad_kernel(count, gain_at, core_ref, *refs):
-    pairs, refs = refs[: 2 * count], refs[2 * count :]
-    gain_ref, kept_ref, sent_ref = refs
+def weight_grad_kernel(counts, gain_at, core_ref, *refs):
+    sides = []
+    for size in counts:
+        sides.append(jnp.concatenate([ref[...] for ref in refs[:size]], axis=0))
+        refs = refs[size:]
+    gain_refs, (kept_ref, sent_ref) = refs[:-2], refs[-2:]
     n, shard, _ = kept_ref.shape
-    width = gain_ref.shape[1]
-    terms = [tn(pairs[2 * i][:, :width], pairs[2 * i + 1][...]) for i in range(count)]
-    if gain_at is not None:
+    width = 2 * n * shard
+    terms = [tn(left[:, :width], right) for left, right in zip(sides[::2], sides[1::2])]
+    if gain_refs:
+        if terms[-1].shape[1] != LANES:
+            terms.append(jnp.zeros((width, LANES), F32))
         row = lax.broadcasted_iota(jnp.int32, (8, LANES), 0)
         lane = lax.broadcasted_iota(jnp.int32, (8, LANES), 1)
         place = jnp.where((row == 0) & (lane == gain_at), 1.0, 0.0)
-        gains = tn(jnp.broadcast_to(gain_ref[...], (8, gain_ref.shape[1])), place)
-        if terms[-1].shape[1] == LANES:
-            terms[-1] = terms[-1] + gains
-        else:
-            terms.append(gains)
+        gain = sum(ref[...] for ref in gain_refs)
+        terms[-1] = terms[-1] + tn(jnp.broadcast_to(gain, (8, width)), place)
     first = 0
     for term in terms:
         cols = term.shape[1]
@@ -478,9 +486,60 @@
 
 def add_terms_kernel(experts, own_ref, peer_ref, sum_ref):
     width = own_ref.shape[1] - LANES
-    sum_ref[:, :width] = (own_ref[:, :width] + peer_ref[:, :width].astype(F32)).astype(BF)
+    total = own_ref[:, :width] + peer_ref[:, :width].astype(F32)
+    sum_ref[:, :width] = total.astype(BF)
     pull = own_ref[:, width:] + in_one(peer_ref[:, width:], experts)
     sum_ref[:, width:] = in_two(pull, experts)
+
+
+def close_experts_kernel(core_ref, own_ref, ahead_ref, back_ref, kept_ref, sent_ref):
+    rows = kept_ref.shape[1]
+    total = own_ref[...].astype(F32) + ahead_ref[...].astype(F32) + back_ref[...].astype(F32)
+    is_first = core_ref[0] == 0
+    kept_ref[...] = jnp.where(is_first, total[:, :rows], total[:, rows:])
+    sent_ref[...] = jnp.where(is_first, total[:, rows:], total[:, :rows]).astype(BF)
+
+
+def expert_grads_kernel(chains, core_ref, *refs):
+    kept_refs, sent_refs, outs = refs[:chains], refs[chains : 2 * chains], refs[2 * chains :]
+    count, _, cols = kept_refs[0].shape
+    hid = cols // 3
+    for k in range(chains):
+        for ref, core in ((kept_refs[k], core_ref[0]), (sent_refs[k], 1 - core_ref[0])):
+            for i in range(count):
+                at = core * chains * count + k * count + i
+                for part, out in enumerate(outs):
+                    out[at] = ref[i, :, part * hid : (part + 1) * hid].astype(F32)
+
+
+def close_weights_kernel(widths, own_ref, ahead_ref, back_ref, *outs):
+    def total(cols):
+        return (
+            own_ref[0, :, cols].astype(F32)
+            + ahead_ref[0, :, cols].astype(F32)
+            + back_ref[0, :, cols].astype(F32)
+        )
+
+    first = 0
+    for kind, width in widths:
+        if kind == "pairs":
+            for pair in range(width // (2 * LANES)):
+                for side in range(2):
+                    lo = first + (2 * pair + side) * LANES
+                    outs[side][:, pair * LANES : (pair + 1) * LANES] = total(slice(lo, lo + LANES))
+            outs = outs[2:]
+        else:
+            outs[0][...] = total(slice(first, first + width))
+            outs = outs[1:]
+        first += width
+
+
+def token_grads_kernel(x_ref, own_ref, dot_ref, other_ref, middle_ref, out_ref):
+    feature = x_ref.shape[1]
+    other = other_ref[...]
+    dot = dot_ref[:, :1] + in_one(other[:, feature:], 1)[:, :1]
+    total = middle_ref[...] + own_ref[...] + other[:, :feature].astype(F32)
+    out_ref[...] = total - x_ref[...].astype(F32) * dot
 
 
 def middle_back_kernel(
@@ -525,51 +584,42 @@
     att_ref[...] = nn(branch, wo_ref[...]).astype(BF)
 
 
-def project_back_kernel(
-    pairs,
-    gain_col,
-    tp_ref,
-    dq_ref,
-    kva_ref,
-    kvb_ref,
-    kvc_ref,
-    cos_ref,
-    sin_ref,
-    w_ref,
-    x_ref,
-    small_ref,
-    d_ref,
-    own_ref,
-    other_ref,
-    dot_ref,
-    dgain_ref,
-):
-    @pl.when(pl.program_id(0) == 0)
-    def _():
-        dgain_ref[...] = jnp.zeros(dgain_ref.shape, F32)
-
-    cosine, sine = cos_ref[...], sin_ref[...]
-    q_width = dq_ref.shape[1]
-    kv = kva_ref[...].astype(F32) + kvb_ref[...].astype(F32) + kvc_ref[...].astype(F32)
-    for pair in range(pairs):
-        lo = pair * 2 * LANES
-        part = kv[:, lo : lo + LANES]
-        d_ref[:, lo : lo + LANES] = (part * cosine - swap_halves(part) * sine).astype(BF)
-        d_ref[:, lo + LANES : lo + 2 * LANES] = kv[:, lo + LANES : lo + 2 * LANES].astype(BF)
-    grad = nt(dq_ref[...], w_ref[:, :q_width]) + nt(d_ref[...], w_ref[:, q_width:])
-    x = x_ref[...].astype(F32)
-    width = x.shape[1]
-    scale = lax.rsqrt(jnp.mean(x * x, axis=1, keepdims=True) + EPSILON)
-    unit = x * scale
-    dgain_ref[...] += jnp.sum(grad * unit, axis=0, keepdims=True)
-    scaled = grad * column_as_row(small_ref, gain_col)
-    inner = jnp.sum(scaled * unit, axis=1, keepdims=True) * (1.0 / width) * scale * scale
-    dot_ref[...] = jnp.broadcast_to(inner, dot_ref.shape)
-    scaled = scaled * scale
-    half = width // 2
+def project_back_kernel(pairs, gain_col, seqs, tp_ref, *refs):
+    dq_ref, kva_ref, kvb_ref, kvc_ref, cos_ref, sin_ref, w_ref, x_ref, small_ref = refs[:9]
+    d_ref, own_ref, other_ref, dot_ref, dgain_ref = refs[9:]
+    gain = column_as_row(small_ref, gain_col)
     is_first = tp_ref[0] == 0
-    own_ref[...] = jnp.where(is_first, scaled[:, :half], scaled[:, half:])
-    other_ref[...] = jnp.where(is_first, scaled[:, half:], scaled[:, :half]).astype(BF)
+    rows, q_width = dq_ref.shape
+    span = rows // seqs
+    for s in range(seqs):
+        at = slice(s * span, (s + 1) * span)
+        cosine, sine = cos_ref[at], sin_ref[at]
+        kv = kva_ref[0, at].astype(F32) + kvb_ref[0, at].astype(F32) + kvc_ref[at].astype(F32)
+        for pair in range(pairs):
+            lo = pair * 2 * LANES
+            part = kv[:, lo : lo + LANES]
+            d_ref[at, lo : lo + LANES] = (part * cosine - swap_halves(part) * sine).astype(BF)
+            d_ref[at, lo + LANES : lo + 2 * LANES] = kv[:, lo + LANES : lo + 2 * LANES].astype(BF)
+        grad = nt(dq_ref[at], w_ref[:, :q_width]) + nt(d_ref[at], w_ref[:, q_width:])
+        x = x_ref[at].astype(F32)
+        width = x.shape[1]
+        scale = lax.rsqrt(jnp.mean(x * x, axis=1, keepdims=True) + EPSILON)
+        unit = x * scale
+        term = jnp.sum(grad * unit, axis=0, keepdims=True)
+        if s == 0:
+            dgain_ref[...] = term
+        else:
+            dgain_ref[...] += term
+        scaled = grad * gain
+        inner = jnp.sum(scaled * unit, axis=1, keepdims=True) * (1.0 / width) * scale * scale
+        lane = lax.broadcasted_iota(jnp.int32, (span, LANES), 1)
+        dot = jnp.where(lane == 0, inner, 0.0)
+        dot_ref[at] = dot
+        scaled = scaled * scale
+        half = width // 2
+        own_ref[at] = jnp.where(is_first, scaled[:, :half], scaled[:, half:])
+        other_ref[at, :half] = jnp.where(is_first, scaled[:, half:], scaled[:, :half]).astype(BF)
+        other_ref[at, half:] = in_two(dot, 1)
 
 
 class Ring:
@@ -615,17 +665,18 @@
         self.moving = (block, block)
         self.parts = [block]
 
-    def tick(self):
+    def prepare(self):
+        if self.step == self.ring.size // 2 - 1:
+            half = self.rows // 2
+            ahead, back = self.moving
+            self.moving = (ahead[:, :half], back[:, half:]) if half % 16 == 0 else (ahead,)
+
+    def send(self):
         self.step += 1
-        ahead, back = self.moving
-        if self.done():
-            half = self.rows // 2
-            if half % 16:
-                self.parts.append(self.ring.send(ahead))
-                return
-            ahead, back = ahead[:, :half], back[:, half:]
         with jax.named_scope(f"{self.name}_step_{self.step}"):
-            self.moving = (self.ring.send(ahead), self.ring.send(back, False))
+            self.moving = tuple(
+                self.ring.send(array, i == 0) for i, array in enumerate(self.moving)
+            )
         self.parts += self.moving
 
     def done(self):
@@ -639,22 +690,13 @@
         self.halved = len(parts) == ring.size + 1
         self.moving = (parts[-2], parts[-1]) if self.halved else (parts[-1],)
 
-    def tick(self):
+    def prepare(self):
+        if self.step:
+            s = self.far - self.step
+            self.moving = add_pair(self.parts[2 * s], self.parts[2 * s - 1], *self.moving)
+
+    def send(self):
         self.step += 1
-        if self.step > 1:
-            s = self.far - self.step + 1
-            behind, near = self.parts[2 * s - 1], self.parts[2 * s]
-            if self.step > 2:
-                ahead, back = near + self.moving[0], behind + self.moving[1]
-            elif self.halved:
-                half = near.shape[1] // 2
-                ahead = jnp.concatenate([near[:, :half] + self.moving[0], near[:, half:]], axis=1)
-                back = jnp.concatenate(
-                    [behind[:, :half], behind[:, half:] + self.moving[1]], axis=1
-                )
-            else:
-                ahead, back = near + self.moving[0], behind
-            self.moving = (ahead, back)
         with jax.named_scope(f"{self.name}_step_{self.step}"):
             self.moving = tuple(
                 self.ring.send(array, i == 0) for i, array in enumerate(self.moving)
@@ -663,9 +705,55 @@
     def done(self):
         return self.step == self.far
 
-    def result(self):
-        ahead, back = self.moving
-        return self.parts[0].astype(F32) + ahead.astype(F32) + back.astype(F32)
+
+def add_pair_kernel(near_ref, behind_ref, *refs):
+    moved, outs = refs[:-2], refs[-2:]
+    rows = near_ref.shape[1]
+    for i, (mine, out) in enumerate(zip((near_ref, behind_ref), outs)):
+        if i >= len(moved):
+            out[...] = mine[...]
+            continue
+        came = moved[i]
+        size = came.shape[1]
+        at = slice(0, size) if i == 0 else slice(rows - size, rows)
+        total = (mine[:, at].astype(F32) + came[...].astype(F32)).astype(BF)
+        if size == rows:
+            out[...] = total
+        else:
+            rest = slice(size, rows) if i == 0 else slice(0, rows - size)
+            out[:, at] = total
+            out[:, rest] = mine[:, rest]
+
+
+def add_pair(near, behind, *moved):
+    def spec(array):
+        return pl.BlockSpec((1,) + array.shape[1:], lambda i: (i, 0, 0))
+
+    arrays = (near, behind, *moved)
+    out = jax.ShapeDtypeStruct(near.shape, BF)
+    return pl.pallas_call(
+        add_pair_kernel,
+        grid=(near.shape[0],),
+        in_specs=[spec(array) for array in arrays],
+        out_specs=[spec(near)] * 2,
+        out_shape=[out] * 2,
+        compiler_params=params("arbitrary"),
+        name="add_pair",
+    )(*arrays)
+
+
+def pinned(call):
+    def run(*args):
+        return call(
+            *[
+                pltpu.with_memory_space_constraint(a, pltpu.HBM)
+                if a.ndim > 1 and a.dtype != jnp.int32
+                else a
+                for a in args
+            ]
+        )
+
+    return run
 
 
 def lock(*values):
@@ -733,30 +821,67 @@
     smem = pl.BlockSpec(memory_space=pltpu.SMEM)
     any_spec = pl.BlockSpec(memory_space=pl.ANY)
     qkv_width = q_width + 2 * kv_width
+    in_hbm = lambda array: pltpu.with_memory_space_constraint(array, pltpu.HBM)
+    small_rows = max(shard, LANES)
     bundle = pl.pallas_call(
         pack_kernel,
-        in_specs=[vmem] * 7,
+        in_specs=[any_spec] * 4 + [vmem] * 3,
         out_specs=vmem,
         out_shape=jax.ShapeDtypeStruct((1, shard, qkv_width + q_width + LANES), BF),
+        scratch_shapes=[pltpu.VMEM((LANES, small_rows), F32), pltpu.SemaphoreType.DMA(())],
         compiler_params=params(),
         name="pack",
-    )(w_query, w_key, w_value, w_out, w_router, gain_attn[None], gain_ffn[None])
+    )(
+        *[in_hbm(w) for w in (w_query, w_key, w_value, w_out.T)],
+        w_router.T,
+        gain_attn[None],
+        gain_ffn[None],
+    )
     own_tokens = tokens.reshape(rows, feature)
     own_cot = cotangent.reshape(rows, feature)
-    other_tokens = swap_tp(own_tokens, "own_tokens")
+    core_scalar = core.astype(jnp.int32).reshape(1)
+    def segment(ticks, *values):
+        chains = [chain for chain in ticks if not chain.done()]
+
+        values = together(chains, *values)
+        if any(chain.step for chain in chains):
+            for chain in chains:
+                chain.prepare()
+            values = together(chains, *values)
+        for chain in chains:
+            chain.send()
+        return values
+
+    def together(chains, *values):
+        held = [array for chain in chains for array in chain.moving]
+        out = lock(*held, *values)
+        at = 0
+        for chain in chains:
+            size = len(chain.moving)
+            chain.moving = tuple(out[at : at + size])
+            at += size
+        return out[at:]
+
+    def arrive(chain, *values):
+        return together([chain], *values)
+
     first = Gather(ring, bundle, "bundle")
-    from_core = [swap_core(bundle, "bundle")]
-    core_scalar = core.astype(jnp.int32).reshape(1)
     half_shape = jax.ShapeDtypeStruct((per_core, shard, 3 * hid), BF)
-    first.tick()
+    *raw_w, own_tokens, bundle = segment(
+        [first], w_gate, w_up, w_down.transpose(0, 2, 1), own_tokens, bundle
+    )
     mine_w, other_w = pl.pallas_call(
         pack_experts_kernel,
-        in_specs=[smem] + [vmem] * 3,
+        in_specs=[smem] + [any_spec] * 3,
         out_specs=[vmem] * 2,
         out_shape=[half_shape] * 2,
+        scratch_shapes=[pltpu.SemaphoreType.DMA(())],
         compiler_params=params(),
         name="pack_experts",
-    )(core_scalar, *lock(w_gate, w_up, w_down, bundle)[:3])
+    )(core_scalar, *[in_hbm(w) for w in raw_w])
+    from_core = [swap_core(bundle, "bundle")]
+    other_w = swap_core(other_w, "experts")
+    from_core[0], other_w, mine_w = segment([first], from_core[0], other_w, mine_w)
     blocks_w = list(
         pl.pallas_call(
             join_kernel,
@@ -768,15 +893,15 @@
             * GATHERS,
             compiler_params=params(),
             name="join",
-        )(core_scalar, mine_w, swap_core(other_w, "other_w"))
-    )
-    first.tick()
-    *first.moving, mine_w = lock(*first.moving, mine_w)
-    first.tick()
-    *first.moving, blocks_w[0] = lock(*first.moving, blocks_w[0])
-    while not first.done():
-        first.tick()
-    from_core += [swap_core(part, "part") for part in first.parts[1:]]
+        )(core_scalar, mine_w, other_w)
+    )
+    half_width = HD // 2
+    freqs = 10000.0 ** (-jnp.arange(half_width, dtype=F32) / half_width)
+    local_pos = c * span + jnp.arange(span, dtype=jnp.int32)
+    angles = local_pos.astype(F32)[:, None] * freqs[None, :]
+    cosine, sine = jnp.cos(angles), jnp.sin(angles)
+    cosine = jnp.tile(jnp.concatenate([cosine] * 4, axis=1), (seqs, 1))
+    sine = jnp.tile(jnp.concatenate([-sine, sine, -sine, sine], axis=1), (seqs, 1))
     chips = [ring.chip(d) for d, _, _ in ring.places(shard)]
     chip_list = jnp.stack(chips).astype(jnp.int32)
     bundle_places = ring.places(shard)
@@ -785,7 +910,46 @@
         for side in (core, 1 - core)
         for j, (_, row, _) in enumerate(bundle_places)
     ]
-    in_hbm = lambda array: pltpu.with_memory_space_constraint(array, pltpu.HBM)
+    bundle_where = jnp.stack(bundle_rows).astype(jnp.int32)
+    places = ring.places(2 * shard)
+    part_rows = [ring.chip(d) * 2 * shard + row for d, row, _ in places]
+    part_where = jnp.stack([core * per_core] + part_rows).astype(jnp.int32)
+    base = jnp.stack(
+        [(((y - k) % deep) * 2 + core) * span for k in range(deep)]
+        + [(((y - k) % deep) * 2 + 1 - core) * span for k in range(deep)]
+    ).astype(jnp.int32)
+    other_tokens = swap_tp(own_tokens, "tokens")
+    shared = 1
+    while not first.done():
+        fresh = [swap_core(part, "part") for part in first.parts[shared : first.step * 2 - 1]]
+        shared += len(fresh)
+        last_step = first.step == ring.size // 2 - 1
+        *fresh, blocks_w[0], cosine, sine, chip_list, bundle_where, part_where, base, tokens_here = segment(
+            [first],
+            *fresh,
+            blocks_w[0],
+            cosine,
+            sine,
+            chip_list,
+            bundle_where,
+            part_where,
+            base,
+            other_tokens if last_step else own_tokens,
+        )
+        if last_step:
+            other_tokens = tokens_here
+        from_core += fresh
+    weights = [Gather(ring, block, f"weights_{i}") for i, block in enumerate(blocks_w)]
+    rest = [swap_core(part, "part") for part in first.parts[shared:-2]]
+    other_cot = swap_tp(own_cot, "cotangent")
+    *rest, other_cot, weights[0].moving = arrive(
+        first, *rest, other_cot, weights[0].moving[0]
+    )
+    weights[0].moving = (weights[0].moving,) * 2
+    weights[0].send()
+    from_core += rest
+    rest = [swap_core(part, "part") for part in first.parts[shared + len(rest) :]]
+    from_core += rest
     w_qkv, wo_mine, w_small = pl.pallas_call(
         functools.partial(assemble_kernel, bundle_places * 2),
         in_specs=[smem] + [any_spec] * len(bundle_rows),
@@ -797,39 +961,13 @@
         compiler_params=params(),
         name="assemble",
     )(
-        jnp.stack(bundle_rows).astype(jnp.int32),
+        bundle_where,
         *[in_hbm(part) for part in first.parts + from_core],
     )
-    weights = [Gather(ring, block, f"weights_{i}") for i, block in enumerate(blocks_w)]
-    under_way = []
-
-    def segment(ticks, *values):
-        held = [array for chain in under_way for array in chain.moving]
-        out = lock(*held, *values)
-        at = 0
-        for chain in under_way:
-            size = len(chain.moving)
-            chain.moving = tuple(out[at : at + size])
-            at += size
-        under_way[:] = [chain for chain in ticks if not chain.done()]
-        for chain in under_way:
-            chain.tick()
-        return out[at:]
-
-    start_block = lock(blocks_w[0], *first.parts[-2:])[0]
-    weights[0].moving = (start_block, start_block)
-    segment(weights[:1], start_block)
-    half_width = HD // 2
-    freqs = 10000.0 ** (-jnp.arange(half_width, dtype=F32) / half_width)
-    local_pos = c * span + jnp.arange(span, dtype=jnp.int32)
-    angles = local_pos.astype(F32)[:, None] * freqs[None, :]
-    cosine, sine = jnp.cos(angles), jnp.sin(angles)
-    cosine = jnp.tile(jnp.concatenate([cosine] * 4, axis=1), (seqs, 1))
-    sine = jnp.tile(jnp.concatenate([-sine, sine, -sine, sine], axis=1), (seqs, 1))
     step_rows = min(rows, 256)
     steps = rows // step_rows
     row_spec = lambda cols: pl.BlockSpec((step_rows, cols), lambda i, *_: (i, 0))
-    full_tokens, normed, queries, kv = pl.pallas_call(
+    full_tokens, normed, queries, kv = (pl.pallas_call(
         functools.partial(project_kernel, pairs, q_width, experts),
         grid=(steps,),
         in_specs=[
@@ -843,34 +981,28 @@
         ],
         out_specs=[row_spec(width), row_spec(width), row_spec(q_width), row_spec(2 * kv_width)],
         out_shape=[
-            jax.ShapeDtypeStruct((rows, width), BF),
-            jax.ShapeDtypeStruct((rows, width), BF),
+            pltpu.HBM((rows, width), BF),
+            pltpu.HBM((rows, width), BF),
             jax.ShapeDtypeStruct((rows, q_width), BF),
             jax.ShapeDtypeStruct((rows, 2 * kv_width), BF),
         ],
         compiler_params=params("arbitrary"),
         name="project",
-    )(tp_scalar, own_tokens, other_tokens, w_small, w_qkv, cosine, sine)
+    ))(tp_scalar, own_tokens, other_tokens, w_small, w_qkv, cosine, sine)
 
     own_side = [kv]
     for _ in range(deep - 1):
         own_side.append(shift_y(own_side[-1], up_y, "kv"))
-    other_side = [swap_core(block, "block") for block in own_side]
+    other_side = [swap_core(kv, "kv")]
+    wo_other = swap_tp(wo_mine, "w_out")
+    length = ctx * span
+
+    queries, *own_side = segment(weights[:1], queries, *own_side)
+    other_side += [swap_core(block, "kv") for block in own_side[1:]]
     kv_blocks = own_side + other_side
-    base = jnp.stack(
-        [(((y - k) % deep) * 2 + core) * span for k in range(deep)]
-        + [(((y - k) % deep) * 2 + 1 - core) * span for k in range(deep)]
-    ).astype(jnp.int32)
-    length = ctx * span
-
-    other_cot = swap_tp(own_cot, "own_cot")
-    queries, other_cot, wo_mine, *kv_blocks = segment(
-        weights[:1], queries, other_cot, wo_mine, *kv_blocks
-    )
-    wo_other = swap_tp(wo_mine, "wo_mine")
     head_spec = lambda: pl.BlockSpec((span, 2 * LANES), lambda s, p, *_: (s, p))
     prob_spec = pl.BlockSpec((1, 2, 2 * span, length), lambda s, p, *_: (s, p, 0, 0))
-    attended, probs = pl.pallas_call(
+    attended, probs = (pl.pallas_call(
         functools.partial(attend_kernel, ctx, span),
         grid_spec=pltpu.PrefetchScalarGridSpec(
             num_scalar_prefetch=2,
@@ -884,25 +1016,26 @@
         ],
         compiler_params=params("arbitrary", "arbitrary"),
         name="attend",
-    )(prefix, base, queries, *kv_blocks)
-
-    full_cot = pl.pallas_call(
-        features_kernel,
-        in_specs=[smem] + [vmem] * 2,
-        out_specs=vmem,
-        out_shape=pltpu.HBM((rows, width), BF),
-        compiler_params=params(),
-        name="features",
-    )(tp_scalar, own_cot, other_cot)
-    attended, wo_other, full_cot = segment(weights[:1], attended, wo_other, full_cot)
+    ))(prefix, base, queries, *kv_blocks)
+
+    attended, wo_other = segment(weights[:1], attended, wo_other)
     for _ in range(ring.size // 2 - 4):
         (attended,) = segment(weights[:1], attended)
 
     attended_other = swap_tp(attended, "attended")
+    full_cot = (pl.pallas_call(
+            features_kernel,
+            in_specs=[smem] + [vmem] * 2,
+            out_specs=vmem,
+            out_shape=pltpu.HBM((rows, width), BF),
+            compiler_params=params(),
+            name="features",
+        )
+    )(tp_scalar, own_cot, other_cot)
     peer_cot = swap_core(full_cot, "full_cot")
-    attended_other, peer_cot = segment(weights, attended_other, peer_cot)
+    (attended_other,) = segment(weights[:1], attended_other)
     route_rows = routes.reshape(rows, TOP)
-    middle, normed_two, gates = pl.pallas_call(
+    middle, normed_two, gates = (pinned(pl.pallas_call(
         functools.partial(middle_kernel, experts + 1),
         grid=(steps,),
         in_specs=[
@@ -922,44 +1055,46 @@
         out_shape=[
             pltpu.HBM((rows, width), F32),
             pltpu.HBM((rows, width + LANES), BF),
-            jax.ShapeDtypeStruct((rows, LANES), F32),
+            pltpu.HBM((rows, LANES), F32),
         ],
         compiler_params=params("arbitrary"),
         name="middle",
-    )(attended, attended_other, wo_mine, wo_other, full_tokens, w_small, route_rows)
+    )))(attended, attended_other, wo_mine, wo_other, full_tokens, w_small, route_rows)
+    normed_two, peer_cot = arrive(weights[0], normed_two, peer_cot)
+    (normed_two,) = segment(weights[1:], normed_two)
     peer_two = swap_core(normed_two, "normed_two")
-    (peer_two,) = segment(weights[1:], peer_two)
 
     near = [(normed_two, BF), (full_cot, BF), (peer_two, BF), (peer_cot, BF)]
     sources = [in_hbm(array) for array, _ in near]
     wide_acc, acc_shape = (rows, width), (rows, width + LANES)
-    places = ring.places(2 * shard)
     count = len(places)
-    part_rows = [ring.chip(d) * 2 * shard + row for d, row, _ in places]
     calls = GATHERS * CALLS
     call_size = per_core // calls
 
-    def run_experts(call, accs):
-        where = jnp.stack([core * per_core + call * call_size] + part_rows)
+    def run_experts(call, accs, dw_parts):
+        lead = 1 + count + 4 + len(accs)
         first_call, last_call = call == 0, call == calls - 1
         outs = pl.pallas_call(
             functools.partial(
                 moe_kernel,
                 first_call,
                 last_call,
+                bool(dw_parts),
                 experts,
+                call * call_size,
                 call % CALLS * call_size,
                 call_size,
                 places,
             ),
-            in_specs=[smem] + [any_spec] * (count + 4 + len(accs)),
+            in_specs=[smem] + [any_spec] * (lead - 1 + len(dw_parts)),
             out_specs=[any_spec] * (3 + count),
             out_shape=[
                 pltpu.HBM(acc_shape, F32),
                 pltpu.HBM(acc_shape, BF if last_call else F32),
                 pltpu.HBM((call_size, 2 * rows, hid), BF),
             ]
-            + [pltpu.HBM((call_size, r, 3 * hid), BF) for _, _, r in places],
+            + [pltpu.HBM((call_size * CALLS, r, 3 * hid), BF) for _, _, r in places],
+            input_output_aliases={lead + j: 3 + j for j in range(len(dw_parts))},
             scratch_shapes=[pltpu.VMEM(array.shape, kind) for array, kind in near]
             + [pltpu.VMEM(acc_shape, F32)] * 2
             + [
@@ -977,62 +1112,65 @@
             compiler_params=pltpu.CompilerParams(vmem_limit_bytes=MOE_VMEM),
             name="experts",
         )(
-            where.astype(jnp.int32),
+            part_where,
             *[in_hbm(block) for block in weights[call // CALLS].parts],
             *sources,
             *accs,
+            *dw_parts,
         )
         return outs[:2], outs[2], outs[3:]
 
     accs, mixed_parts, sums = (), [], []
 
-    for call in range(calls):
-        for chain in weights[call // CALLS : call // CALLS + 1]:
-            while not chain.done():
-                accs = segment([chain, *sums[:1]], *accs)
-        if call:
-            accs = segment([*weights[1:], *sums][:2] if not weights[-1].done() else sums[:2], *accs)
-        accs, mixed, dw_parts = run_experts(call, accs)
-        mixed_parts.append(mixed)
-        sums.append(Scatter(ring, dw_parts, f"sums_{call}"))
-
-    grad_two, grad_two_peer = segment(sums[2:], *accs)
-    grad_two, from_peer = segment([], grad_two, swap_core(grad_two_peer, "grad_two"))
+    for g in range(GATHERS):
+        dw_parts = ()
+        if g:
+            while not weights[g].done():
+                accs = segment(weights[g : g + 1], *accs)
+            accs = arrive(weights[g], *accs)
+        for call in range(g * CALLS, (g + 1) * CALLS):
+            if call:
+                accs = segment([*weights[g + 1 : g + 2], *sums][:1], *accs)
+            accs, mixed, dw_parts = run_experts(call, accs, dw_parts)
+            mixed_parts.append(mixed)
+        sums.append(Scatter(ring, dw_parts, f"sums_{g}"))
+
+    grad_two, grad_two_peer = arrive(sums[0], *accs)
+    sums[0].prepare()
     part = pl.pallas_call(
         functools.partial(add_terms_kernel, experts),
-        grid=(steps,),
-        in_specs=[row_spec(width + LANES)] * 2,
-        out_specs=row_spec(width + LANES),
+        in_specs=[vmem] * 2,
+        out_specs=vmem,
         out_shape=jax.ShapeDtypeStruct(acc_shape, BF),
-        compiler_params=params("arbitrary"),
+        compiler_params=params(),
         name="add_terms",
-    )(grad_two, from_peer)
-    (part,) = segment(sums[:2], part)
+    )(grad_two, swap_core(grad_two_peer, "grad_two"))
+    (part,) = together(sums[:1], part)
     part_other = swap_tp(part, "part")
+    sums[0].send()
 
     moe, moe_peer = pl.pallas_call(
         functools.partial(moe_sum_kernel, places, GATHERS, calls, call_size),
         in_specs=[smem] + [any_spec] * (count * GATHERS + calls),
         out_specs=[vmem] * 2,
-        out_shape=[
-            jax.ShapeDtypeStruct(wide_acc, F32),
-            jax.ShapeDtypeStruct(wide_acc, BF),
+        out_shape=[pltpu.HBM(wide_acc, F32), pltpu.HBM(wide_acc, BF)],
+        scratch_shapes=[
+            pltpu.VMEM((GATHERS, width, per_core // GATHERS * hid), BF),
+            pltpu.VMEM((GATHERS, 2 * rows, per_core // GATHERS * hid), BF),
+            pltpu.SemaphoreType.DMA((GATHERS,)),
+            pltpu.SemaphoreType.DMA((GATHERS,)),
         ],
-        scratch_shapes=[
-            pltpu.VMEM((2, width, hid), BF),
-            pltpu.VMEM((2, 2 * rows, hid), BF),
-            pltpu.VMEM((2 * rows, width), F32),
-            pltpu.SemaphoreType.DMA((2,)),
-            pltpu.SemaphoreType.DMA((2,)),
-        ],
-        compiler_params=params(),
+        compiler_params=pltpu.CompilerParams(vmem_limit_bytes=MOE_VMEM),
         name="experts_output",
     )(
-        jnp.stack([core * 0] + part_rows).astype(jnp.int32),
+        part_where,
         *[in_hbm(block) for chain in weights for block in chain.parts],
-        *lock(*[in_hbm(mixed) for mixed in mixed_parts], part)[:-1],
-    )
-    part_other, moe, moe_peer = segment(sums[1:3], part_other, moe, moe_peer)
+        *lock(*[in_hbm(mixed) for mixed in mixed_parts], part)[:calls],
+    )
+
+    moe, moe_peer = segment(sums[:1], moe, moe_peer)
+    from_core_moe = swap_core(moe_peer, "moe")
+
     grad_middle, grad_branch, grad_attended, grad_logits, gain_two_term = pl.pallas_call(
         functools.partial(middle_back_kernel, experts + 1),
         grid=(steps,),
@@ -1054,7 +1192,7 @@
             whole((1, width)),
         ],
         out_shape=[
-            jax.ShapeDtypeStruct((rows, feature), F32),
+            pltpu.HBM((rows, feature), F32),
             jax.ShapeDtypeStruct((rows, width), BF),
             jax.ShapeDtypeStruct((rows, q_width), BF),
             jax.ShapeDtypeStruct((rows, LANES), BF),
@@ -1062,17 +1200,7 @@
         ],
         compiler_params=params("arbitrary"),
         name="middle_back",
-    )(
-        tp_scalar,
-        part,
-        part_other,
-        gates,
-        middle,
-        full_cot,
-        w_small,
-        wo_mine,
-    )
-
+    )(tp_scalar, part, part_other, gates, middle, full_cot, w_small, wo_mine)
     back_spec = pl.BlockSpec((deep, span, 2 * LANES), lambda s, p: (0, s, p))
     turn_spec = pl.BlockSpec((span, LANES), lambda s, p: (s, 0))
     grad_q, grad_kv_own, grad_kv_peer = pl.pallas_call(
@@ -1088,82 +1216,80 @@
         compiler_params=params("arbitrary", "arbitrary"),
         name="attend_back",
     )(in_hbm(probs), queries, grad_attended, cosine, sine, *kv_blocks)
-    def weight_grads(name, pair_list, gain_term, gain_at, cols):
-        shape = jax.ShapeDtypeStruct((n, shard, cols), BF)
-        flat = [array for pair in pair_list for array in pair]
+    grad_q, grad_kv_own, grad_kv_peer, from_core_moe = arrive(
+        sums[0], grad_q, grad_kv_own, grad_kv_peer, from_core_moe
+    )
+
+    def to_owner(grad_kv_own, from_peer):
+        travel = jnp.zeros(from_peer.shape[1:], BF)
+        for k in range(deep - 1, 0, -1):
+            piece = grad_kv_own[k] + from_peer[k]
+            if k < deep - 1:
+                piece = piece + travel
+            travel = shift_y(piece, down_y, "grad_kv")
+        return travel
+
+    def weight_grads(name, sides, gain_terms, gain_at, cols):
+        flat = [array for side in sides for array in side]
+        return (pl.pallas_call(
+                functools.partial(weight_grad_kernel, [len(side) for side in sides], gain_at),
+                in_specs=[smem] + [vmem] * (len(flat) + len(gain_terms)),
+                out_specs=[vmem] * 2,
+                out_shape=[jax.ShapeDtypeStruct((n, shard, cols), BF)] * 2,
+                compiler_params=params(),
+                name=f"{name}_weight_grads",
+            )
+        )(core_scalar, *flat, *gain_terms)
+
+    def close_experts(chain):
+        own = chain.parts[0]
+        shape = (own.shape[0], shard, 3 * hid)
         kept, sent = pl.pallas_call(
-            functools.partial(weight_grad_kernel, len(pair_list), gain_at),
-            in_specs=[smem] + [vmem] * (len(flat) + 1),
+            close_experts_kernel,
+            in_specs=[smem] + [vmem] * 3,
             out_specs=[vmem] * 2,
-            out_shape=[shape] * 2,
+            out_shape=[jax.ShapeDtypeStruct(shape, F32), jax.ShapeDtypeStruct(shape, BF)],
             compiler_params=params(),
-            name="weight_grads",
-        )(core_scalar, *flat, gain_term)
+            name="close_experts",
+        )(core_scalar, own, *chain.moving)
         return kept, sent
 
+    (grad_kv_peer,) = segment(sums[1:], grad_kv_peer)
+    from_peer = swap_core(grad_kv_peer, "grad_kv")
     early = weight_grads(
         "early",
-        [(grad_branch, attended), (normed_two, grad_logits)],
-        gain_two_term,
+        [[grad_branch], [attended], [normed], [grad_q], [normed_two], [grad_logits]],
+        [gain_two_term],
         experts,
-        q_width + LANES,
-    )
-    grad_q, grad_kv_own, grad_kv_peer, moe_peer, *early = segment(
-        [], grad_q, grad_kv_own, grad_kv_peer, moe_peer, *early
-    )
-    from_peer = swap_core(grad_kv_peer, "grad_kv")
+        2 * q_width + LANES,
+    )
+    travel = to_owner(grad_kv_own, from_peer)
+    early = segment(sums[1:], *early)
+    half_at = lambda array, side: lax.dynamic_slice_in_dim(array, side * feature, feature, 1)
     early_other = swap_core(early[1], "early")
-    from_core_moe = swap_core(moe_peer, "moe")
-    from_peer, early_other, from_core_moe = segment([], from_peer, early_other, from_core_moe)
-    half_at = lambda array, side: lax.dynamic_slice_in_dim(array, side * feature, feature, 1)
+    closed = [close_experts(sums[0])]
     moe_sum = moe + from_core_moe.astype(F32)
     moe_send = half_at(moe_sum, 1 - tp).astype(BF)
-    travel = jnp.zeros_like(kv)
-    for k in range(deep - 1, 0, -1):
-        piece = grad_kv_own[k] + from_peer[k]
-        if k < deep - 1:
-            piece = piece + travel
-        piece, moe_send = segment([sums[2]] if k == 1 else [], piece, moe_send)
-        travel = shift_y(piece, down_y, "grad_kv")
-    moe_other = swap_tp(moe_send, "moe_send")
-    travel, moe_other = segment(sums[2:], travel, moe_other)
-
+    travel, early_other, moe_send, *closed[0] = lock(travel, early_other, moe_send, *closed[0])
+    shapes = [
+        ((rows, 2 * kv_width), BF),
+        ((rows, feature), F32),
+        ((rows, feature + LANES), BF),
+        ((rows, LANES), F32),
+        ((1, width), F32),
+    ]
     grad_kv, grad_own, grad_send, inner, gain_one_term = pl.pallas_call(
-        functools.partial(project_back_kernel, pairs, experts),
-        grid=(steps,),
-        in_specs=[
-            smem,
-            row_spec(q_width),
-            row_spec(2 * kv_width),
-            row_spec(2 * kv_width),
-            row_spec(2 * kv_width),
-            row_spec(LANES),
-            row_spec(LANES),
-            whole((width, qkv_width)),
-            row_spec(width),
-            whole((width, LANES)),
-        ],
-        out_specs=[
-            row_spec(2 * kv_width),
-            row_spec(feature),
-            row_spec(feature),
-            row_spec(LANES),
-            whole((1, width)),
-        ],
-        out_shape=[
-            jax.ShapeDtypeStruct((rows, 2 * kv_width), BF),
-            jax.ShapeDtypeStruct((rows, feature), F32),
-            jax.ShapeDtypeStruct((rows, feature), BF),
-            jax.ShapeDtypeStruct((rows, LANES), F32),
-            jax.ShapeDtypeStruct((1, width), F32),
-        ],
-        compiler_params=params("arbitrary"),
+        functools.partial(project_back_kernel, pairs, experts, seqs),
+        in_specs=[smem] + [vmem] * 9,
+        out_specs=[vmem] * 5,
+        out_shape=[jax.ShapeDtypeStruct(shape, kind) for shape, kind in shapes],
+        compiler_params=params(),
         name="project_back",
     )(
         tp_scalar,
         grad_q,
-        grad_kv_own[0],
-        from_peer[0],
+        grad_kv_own,
+        from_peer,
         travel,
         cosine,
         sine,
@@ -1171,67 +1297,84 @@
         full_tokens,
         w_small,
     )
-    dots = inner[:, 0]
     late = weight_grads(
-        "late",
-        [(normed, grad_q), (normed, grad_kv)],
-        gain_one_term,
-        0,
-        q_width + 2 * kv_width + LANES,
-    )
-    grad_send, dots, *late = segment(sums[3:], grad_send, dots, *late)
+        "late", [[normed], [grad_kv]], [gain_one_term], 0, 2 * kv_width + LANES
+    )
     late_other = swap_core(late[1], "late")
-    dots_other = swap_tp(dots, "dots")
-    grad_other = swap_tp(grad_send, "grad_send")
-    late_other, dots_other, grad_other = segment([], late_other, dots_other, grad_other)
+    late_other, early_other = lock(late_other, early_other)
     cols = early_other.shape[2] + late_other.shape[2]
     last = Scatter(
         ring,
-        pl.pallas_call(
+        pinned(pl.pallas_call(
             functools.partial(order_kernel, bundle_places),
             in_specs=[smem] + [vmem] * 4,
             out_specs=[vmem] * len(bundle_places),
             out_shape=[jax.ShapeDtypeStruct((1, r, cols), BF) for _, _, r in bundle_places],
             compiler_params=params(),
             name="order",
-        )(chip_list, early[0], early_other, late[0], late_other),
+        ))(chip_list, early[0], early_other, late[0], late_other),
         "last",
     )
-    last.moving = lock(*last.moving, late_other)[:-1]
-    segment([last, sums[3]])
-    grad_tokens = (
-        grad_middle
-        + grad_own
-        + grad_other.astype(F32)
-        - own_tokens.astype(F32) * (dots + dots_other)[:, None]
-    )
+    (grad_send,) = together([last, sums[1]], grad_send)
+    last.send()
+    sums[1].prepare()
+    sums[1].send()
+    grad_other, moe_other = swap_tp(grad_send, "grad_normed"), swap_tp(moe_send, "moe_send")
+    segment([sums[1], last])
+    grad_other, moe_other = segment([last], grad_other, moe_other)
+    grad_tokens = pinned(
+        pl.pallas_call(
+            token_grads_kernel,
+            in_specs=[vmem] * 5,
+            out_specs=vmem,
+            out_shape=jax.ShapeDtypeStruct((rows, feature), F32),
+            compiler_params=params(),
+            name="token_grads",
+        )
+    )(own_tokens, grad_own, inner, grad_other, grad_middle)
     output = (half_at(middle, tp) + half_at(moe_sum, tp) + moe_other.astype(F32)).astype(BF)
-    while not all(chain.done() for chain in [last, *sums]):
-        segment([last, *[chain for chain in sums if not chain.done()][:1]])
-    last = last.result()[0]
-    early, late = last[:, : q_width + LANES], last[:, q_width + LANES :]
-    grad_out = early[:, :q_width].T
-    grad_router = early[:, q_width : q_width + experts]
-    grad_gain_ffn = early[:, q_width + experts]
-    grad_query = late[:, :q_width]
-    key_cols, value_cols = [], []
-    for pair in range(pairs):
-        lo = q_width + pair * 2 * LANES
-        key_cols.append(late[:, lo : lo + LANES])
-        value_cols.append(late[:, lo + LANES : lo + 2 * LANES])
-    grad_key = jnp.concatenate(key_cols, axis=1)
-    grad_value = jnp.concatenate(value_cols, axis=1)
-    gain_half = late[:, q_width + 2 * kv_width]
-    grad_gain_attn = gain_half + swap_tp(gain_half, "gain_half")
-
-    totals = jnp.concatenate([chain.result() for chain in sums], axis=0)
-    totals = totals.reshape(per_core, 2, shard, 3 * hid)
-    kept = lax.dynamic_index_in_dim(totals, core, 1, keepdims=False).astype(BF)
-    sent = swap_core(lax.dynamic_index_in_dim(totals, 1 - core, 1, keepdims=False).astype(BF))
-    all_experts = by_core(kept, sent, 0).astype(F32)
-    grad_gate = all_experts[:, :, :hid]
-    grad_up = all_experts[:, :, hid : 2 * hid]
-    grad_down = all_experts[:, :, 2 * hid :].transpose(0, 2, 1)
+    while not sums[1].done():
+        segment(sums[1:])
+    grad_tokens, output = together([sums[1], last], grad_tokens, output)
+    closed.append(close_experts(sums[1]))
+    closed = [[kept, swap_core(sent, "expert_grads")] for kept, sent in closed]
+    while not last.done():
+        segment([last])
+    arrive(last)
+    widths = (("one", q_width), ("one", q_width), ("one", LANES), ("pairs", 2 * kv_width), ("one", LANES))
+    out_term, grad_query, small_term, grad_key, grad_value, gain_term = (pinned(pl.pallas_call(
+            functools.partial(close_weights_kernel, widths),
+            in_specs=[vmem] * 3,
+            out_specs=[vmem] * 6,
+            out_shape=[
+                jax.ShapeDtypeStruct((shard, w), F32)
+                for w in (q_width, q_width, LANES, kv_width, kv_width, LANES)
+            ],
+            compiler_params=params(),
+            name="close_weights",
+        ))
+    )(last.parts[0], *last.moving)
+    grad_out = out_term.T
+    grad_router = small_term[:, :experts]
+    grad_gain_ffn = small_term[:, experts]
+    gain_half = gain_term[:, 0]
+    grad_gain_attn = gain_half + swap_tp(gain_half, "gain")
+    gain_half, *closed[1] = lock(gain_half, *closed[1])
+
+    grad_gate, grad_up, down_term = (pl.pallas_call(
+            functools.partial(expert_grads_kernel, len(sums)),
+            in_specs=[smem] + [vmem] * (2 * len(sums)),
+            out_specs=[vmem] * 3,
+            out_shape=[pltpu.HBM((experts, shard, hid), F32)] * 3,
+            compiler_params=params(),
+            name="expert_grads",
+        )
+    )(
+        core_scalar,
+        *[closed[k][0] for k in range(len(sums))],
+        *[closed[k][1] for k in range(len(sums))],
+    )
+    grad_down = down_term.transpose(0, 2, 1)
 
     return (
         output.reshape(seqs, span, feature),

time: 475 us -> 415 us (0.87)
  local copies, waits for them, and re-layouts: 43.7 us -> 22.3 us
  other arithmetic: 26.5 us -> 5.16 us
  starting transfers between devices: 84.8 us -> 65.6 us
  Pallas kernels: 135 us -> 151 us
  waiting for transfers between devices: 173 us -> 161 us
    pallas_call x12 -> x26, Pallas kernels: 82.4 us -> 101 us  [the longest x4 64.6 us: run_experts(): pl.pallas_call(functools.partial(moe_kernel, first_call, last_call, bool(...]
    ppermute x2, waiting for transfers between devices: 8.81 us -> 26.1 us  [shift_y(): return lax.ppermute(array, 'ctx', perm)]
    ppermute x64 -> x48, starting transfers between devices: 67.3 us -> 50.1 us  [send(): return lax.ppermute(array, RING, self.forward if forward else self.backward)]
    ppermute x64 -> x48, waiting for transfers between devices: 128 us -> 112 us  [send(): return lax.ppermute(array, RING, self.forward if forward else self.backward)]
    ppermute x9 -> x8, waiting for transfers between devices: 31 us -> 17 us  [swap_tp(): return lax.ppermute(array, 'tp', [(0, 1), (1, 0)])]
    unnamed x254 -> x218, local copies, waits for them, and re-layouts: 32 us -> 18 us
    add x31 -> x2, other arithmetic: 13.8 us -> 1.49 us  [the longest x1 0.98 us: to_owner(): piece = grad_kv_own[k] + from_peer[k]]
    ppermute x9 -> x8, starting transfers between devices: 12.5 us -> 11.6 us  [swap_tp(): return lax.ppermute(array, 'tp', [(0, 1), (1, 0)])]
  transfers between devices with their start and end apart: 95 -> 79, of which waited for: 44 -> 42; matrix products, arithmetic and copies ran while one was open for 6% -> 2% of each run, Pallas kernels for 27% -> 35%
where the time goes in v3:
time: 415 us; the launch traced here: 408 us
  waiting for transfers between devices  161 us (39%)
  Pallas kernels  151 us (36%)
  starting transfers between devices  65.6 us (16%)
  local copies, waits for them, and re-layouts  22.3 us (5%)
  other arithmetic  5.16 us (1%)
    ppermute x48, waiting for transfers between devices, send(): return lax.ppermute(array, RING, self.forward if forward else self.backward)  112 us
    pallas_call x4, Pallas kernels, run_experts(): pl.pallas_call(functools.partial(moe_kernel, first_call, last_call, bool(...  64.6 us
    ppermute x48, starting transfers between devices, send(): return lax.ppermute(array, RING, self.forward if forward else self.backward)  50.1 us
    ppermute x2, waiting for transfers between devices, shift_y(): return lax.ppermute(array, 'ctx', perm)  26.1 us
    unnamed x218, local copies, waits for them, and re-layouts  18 us
    ppermute x8, waiting for transfers between devices, swap_tp(): return lax.ppermute(array, 'tp', [(0, 1), (1, 0)])  17 us
    pallas_call x4, Pallas kernels, run(): call(*[pltpu.with_memory_space_constraint(a, pltpu.HBM) if a.ndim > 1 and...  13.2 us
    pallas_call x1, Pallas kernels, per_device(): pl.pallas_call(functools.partial(attend_kernel, ctx, span), grid_spec=plt...  13.2 us
  transfers between devices with their start and end apart: 79, of which 42 were waited for; matrix products, arithmetic and copies ran while one was open for 2% of the time, Pallas kernels for 35%

profile of v3, /device:TPU:0, one launch (start us, length us, event | category | flops | bytes accessed | tf_op | source)
XLA Modules:
  0.0 407.6 jit_solution(8076339464755677509)
XLA Ops:
  5.6 2.6 collective-permute-start
  10.2 3.8 collective-permute-done.refs_1_
  28.3 4.1 collective-permute-done.8.refs_5_
  36.6 2.6 collective-permute-done.13.refs_7_
  49.2 3.4 project.1
  54.8 16.6 %collective-permute-done.22.refs_1_ = bf16[512,512]{1,0:T(8,128)(2,1)S(1)} collective-permute-done((bf16[512,512]{1,0:T(8,128)(2,1)S(1)}, bf16[512,512]{1,0:T(8,128)(2,1)S(1)}, u32[]{:S(2)}, u32[]{:S(2)}) %collective-permute-start.22) | collective-permute-done | bytes 524320 | tf_op jit(solution)/shard_map/kv_over_y/ppermute | solution.py:809
  76.1 13.2 %attend.1 = (bf16[512,512]{1,0:T(8,128)(2,1)S(1)}, bf16[2,4,512,1024]{3,2,1,0:T(8,128)(2,1)}) custom-call(s32[2]{0:T(128)S(1)} %copy-done.68, s32[4]{0:T(128)S(1)} %pad_add_fusion.base_ref, bf16[512,512]{1,0:T(8,128)(2,1)S(1)} %get-tuple-element.404.q_ref, bf16[512,512]{1,0:T(8,128)(2,1)S(1)} %get-tuple-element.405.refs_0_, ...), custom_call_target="tpu_custom_call" | custom-call | tf_op jit(solution)/shard_map/attend/pallas_call | solution.py:1005
  96.1 12.8 %collective-permute-done.30.b_ref = bf16[512,512]{1,0:T(8,128)(2,1)S(1)} collective-permute-done((bf16[512,512]{1,0:T(8,128)(2,1)S(1)}, bf16[512,512]{1,0:T(8,128)(2,1)S(1)}, u32[]{:S(2)}, u32[]{:S(2)}) %collective-permute-start.30) | collective-permute-done | bytes 524320 | tf_op jit(solution)/shard_map/attended_over_tp/ppermute | solution.py:802
  113.8 5.7 %middle.1 = (f32[512,1024]{1,0:T(8,128)}, bf16[512,1152]{1,0:T(8,128)(2,1)}, f32[512,128]{1,0:T(8,128)}) custom-call(bf16[512,512]{1,0:T(8,128)(2,1)} %copy-done.46, bf16[512,512]{1,0:T(8,128)(2,1)} %copy-done.91, bf16[1024,512]{1,0:T(8,128)(2,1)} %copy-done.10, bf16[1024,512]{1,0:T(8,128)(2,1)} %copy-done.89, ...), custom_call_target="tpu_custom_call" | custom-call | tf_op jit(solution)/shard_map/middle/pallas_call | solution.py:747
  119.5 2.7 collective-permute-done.31.refs_7_
  126.7 15.5 %experts.4 = (f32[512,1152]{1,0:T(8,128)}, f32[512,1152]{1,0:T(8,128)}, bf16[2,1024,256]{2,1,0:T(8,128)(2,1)}, bf16[4,128,768]{2,1,0:T(8,128)(2,1)}, bf16[4,128,...) custom-call(s32[10]{0:T(128)} %stack.174.where_ref, ...), custom_call_target="tpu_custom_call" | custom-call | tf_op jit(solution)/shard_map/experts/pallas_call | solution.py:1077
  146.0 16.3 %experts.5 = (f32[512,1152]{1,0:T(8,128)}, f32[512,1152]{1,0:T(8,128)}, bf16[2,1024,256]{2,1,0:T(8,128)(2,1)}, bf16[4,128,768]{2,1,0:T(8,128)(2,1)}, bf16[4,128,...) custom-call(s32[10]{0:T(128)} %stack.174.where_ref, ...), custom_call_target="tpu_custom_call", output_to_operand_aliasing={{3}: (16, {}), {4}: (17, {}), {5}: (18, {}), {6}: (19, {}),... | custom-call | tf_op jit(solution)/shard_map/experts/pallas_call | solution.py:1077
  165.2 15.7 %collective-permute-done.39.refs_5_.refs_14_ = bf16[4,128,768]{2,1,0:T(8,128)(2,1)S(1)} collective-permute-done((bf16[4,128,768]{2,1,0:T(8,128)(2,1)S(1)}, bf16[4,128,768]{2,1,0:T(8,128)(2,1)S(1)}, u32[]{:S(2)}, u32[]{:S(2)}) %collective-permute-start.39) | collective-permute-done | bytes 786464 | tf_op jit(solution)/shard_map/weights_1_step_3/ppermute | solution.py:650
  184.5 6.9 %collective-permute-done.41.refs_7_.refs_16_ = bf16[4,64,768]{2,1,0:T(8,128)(2,1)S(1)} collective-permute-done((bf16[4,64,768]{2,1,0:T(8,128)(2,1)S(1)}, bf16[4,64,768]{2,1,0:T(8,128)(2,1)S(1)}, u32[]{:S(2)}, u32[]{:S(2)}) %collective-permute-start.41) | collective-permute-done | bytes 393248 | tf_op jit(solution)/shard_map/weights_1_step_4/ppermute | solution.py:650
  193.9 16.4 %experts.6 = (f32[512,1152]{1,0:T(8,128)}, f32[512,1152]{1,0:T(8,128)}, bf16[2,1024,256]{2,1,0:T(8,128)(2,1)}, bf16[4,128,768]{2,1,0:T(8,128)(2,1)}, bf16[4,128,...) custom-call(s32[10]{0:T(128)} %stack.174.where_ref, ...), custom_call_target="tpu_custom_call" | custom-call | tf_op jit(solution)/shard_map/experts/pallas_call | solution.py:1077
  214.3 16.4 %experts.7 = (f32[512,1152]{1,0:T(8,128)}, bf16[512,1152]{1,0:T(8,128)(2,1)}, bf16[2,1024,256]{2,1,0:T(8,128)(2,1)}, bf16[4,128,768]{2,1,0:T(8,128)(2,1)}, bf16[...) custom-call(s32[10]{0:T(128)} %stack.174.where_ref, ...), custom_call_target="tpu_custom_call", output_to_operand_aliasing={{3}: (16, {}), {4}: (17, {}), {5}: (18, {}), {6}: (19, {}),... | custom-call | tf_op jit(solution)/shard_map/experts/pallas_call | solution.py:1077
  232.9 3.5 add_pair.10
  240.7 10.6 %experts_output.1 = (f32[512,1024]{1,0:T(8,128)}, bf16[512,1024]{1,0:T(8,128)(2,1)}) custom-call(s32[10]{0:T(128)} %stack.174.where_ref, bf16[4,128,768]{2,1,0:T(8,128)(2,1)} %get-tuple-element.385.refs_0_, bf16[4,128,768]{2,1,0:T(8,128)(2,1)} %collective-permute-done.18.refs_1_, bf16[4,128,768]{2,1,0:T(8,128)(2,1)} %collective-permute-done.19.refs_2_, ...), custom_call_target="tpu_custom_call" | custom-call | tf_op jit(solution)/shard_map/experts_output/pallas_call | solution.py:1152
  251.3 5.8 %collective-permute-done.48.refs_0_ = bf16[4,128,768]{2,1,0:T(8,128)(2,1)} collective-permute-done((bf16[4,128,768]{2,1,0:T(8,128)(2,1)}, bf16[4,128,768]{2,1,0:T(8,128)(2,1)}, u32[]{:S(2)}, u32[]{:S(2)}) %collective-permute-start.48) | collective-permute-done | bytes 786464 | tf_op jit(solution)/shard_map/sums_0_step_3/ppermute | solution.py:650
  263.7 3.5 collective-permute-done.52.sb_ref
  268.2 3.7 middle_back.1
  272.0 12.9 %attend_back.1 = (bf16[512,512]{1,0:T(8,128)(2,1)S(1)}, bf16[2,512,512]{2,1,0:T(8,128)(2,1)S(1)}, bf16[2,512,512]{2,1,0:T(8,128)(2,1)S(1)}) custom-call(bf16[2,4,512,1024]{3,2,1,0:T(8,128)(2,1)} %get-tuple-element.529.p_ref, bf16[512,512]{1,0:T(8,128)(2,1)S(1)} %copy-done.35, bf16[512,512]{1,0:T(8,128)(2,1)S(1)} %get-tuple-element.532.g_ref, ...), custom_call_target="tpu_custom_call" | custom-call | tf_op jit(solution)/shard_map/attend_back/pallas_call | solution.py:1206
  288.0 2.9 early_weight_grads.1
  292.0 5.5 %collective-permute-done.54.refs_0_ = bf16[4,64,768]{2,1,0:T(8,128)(2,1)S(1)} collective-permute-done((bf16[4,64,768]{2,1,0:T(8,128)(2,1)S(1)}, bf16[4,64,768]{2,1,0:T(8,128)(2,1)S(1)}, u32[]{:S(2)}, u32[]{:S(2)}) %collective-permute-start.54) | collective-permute-done | bytes 393248 | tf_op jit(solution)/shard_map/sums_1_step_1/ppermute | solution.py:650
  306.1 9.6 %collective-permute-done.57.refs_3_ = bf16[512,512]{1,0:T(8,128)(2,1)S(1)} collective-permute-done((bf16[512,512]{1,0:T(8,128)(2,1)}, bf16[512,512]{1,0:T(8,128)(2,1)S(1)}, u32[]{:S(2)}, u32[]{:S(2)}) %collective-permute-start.57) | collective-permute-done | bytes 524320 | tf_op jit(solution)/shard_map/grad_kv_over_y/ppermute | solution.py:809
  315.8 3.0 project_back.1
  326.5 5.3 %collective-permute-done.60.refs_0_ = bf16[4,128,768]{2,1,0:T(8,128)(2,1)S(1)} collective-permute-done((bf16[4,128,768]{2,1,0:T(8,128)(2,1)}, bf16[4,128,768]{2,1,0:T(8,128)(2,1)S(1)}, u32[]{:S(2)}, u32[]{:S(2)}) %collective-permute-start.60) | collective-permute-done | bytes 786464 | tf_op jit(solution)/shard_map/sums_1_step_2/ppermute | solution.py:650
  336.4 17.1 %collective-permute-done.64.refs_0_ = bf16[1,32,1792]{2,1,0:T(8,128)(2,1)S(1)} collective-permute-done((bf16[1,32,1792]{2,1,0:T(8,128)(2,1)S(1)}, bf16[1,32,1792]{2,1,0:T(8,128)(2,1)S(1)}, u32[]{:S(2)}, u32[]{:S(2)}) %collective-permute-start.64) | collective-permute-done | bytes 114720 | tf_op jit(solution)/shard_map/last_step_1/ppermute | solution.py:650
  353.8 4.5 %collective-permute-done.65.refs_1_ = bf16[1,32,1792]{2,1,0:T(8,128)(2,1)S(1)} collective-permute-done((bf16[1,32,1792]{2,1,0:T(8,128)(2,1)S(1)}, bf16[1,32,1792]{2,1,0:T(8,128)(2,1)S(1)}, u32[]{:S(2)}, u32[]{:S(2)}) %collective-permute-start.65) | collective-permute-done | bytes 114720 | tf_op jit(solution)/shard_map/last_step_1/ppermute | solution.py:650
  365.0 17.5 %collective-permute-done.68.refs_0_ = bf16[1,64,1792]{2,1,0:T(8,128)(2,1)S(1)} collective-permute-done((bf16[1,64,1792]{2,1,0:T(8,128)(2,1)S(1)}, bf16[1,64,1792]{2,1,0:T(8,128)(2,1)S(1)}, u32[]{:S(2)}, u32[]{:S(2)}) %collective-permute-start.68) | collective-permute-done | bytes 229408 | tf_op jit(solution)/shard_map/last_step_2/ppermute | solution.py:650
  385.0 3.4 token_grads.1
  389.7 2.7 collective-permute-start.74
  (403 shorter events, 138.6 us)
Async XLA Ops:
  8.4 19.4 %collective-permute-start.12 = (bf16[512,512]{1,0:T(8,128)(2,1)}, bf16[512,512]{1,0:T(8,128)(2,1)}, u32[]{:S(2)}, u32[]{:S(2)}) collective-permute-start(bf16[512,512]{1,0:T(8,128)(2,1)} %bitcast.66), channel_id=1, source_target_pairs={{0,1},{1,0},{2,3},{3,2},{4,5},{5,4},{6,7},{7,6},{8,9},{9,8},{10,11... | collective-permute-start | bytes 1572872 | tf_op jit(solution)/shard_map/tokens_over_tp/ppermute | solution.py:802
  41.0 30.3 %collective-permute-start.18 = (bf16[4,128,768]{2,1,0:T(8,128)(2,1)}, bf16[4,128,768]{2,1,0:T(8,128)(2,1)}, u32[]{:S(2)}, u32[]{:S(2)}) collective-permute-start(bf16[4,128,768]{2,1,0:T(8,128)(2,1)} %get-tuple-element.385.refs_0_), channel_id=1, source_target_pairs={{0,8},{8,16},{16,24},{24,28},{28,20},{20,12},{12,4},{4,0},{2,10},{... | collective-permute-start | bytes 2359304 | tf_op jit(solution)/shard_map/weights_0_step_1/ppermute | solution.py:650
  42.1 29.3 %collective-permute-start.19 = (bf16[4,128,768]{2,1,0:T(8,128)(2,1)}, bf16[4,128,768]{2,1,0:T(8,128)(2,1)}, u32[]{:S(2)}, u32[]{:S(2)}) collective-permute-start(bf16[4,128,768]{2,1,0:T(8,128)(2,1)} %get-tuple-element.385.refs_0_), channel_id=1, source_target_pairs={{8,0},{16,8},{24,16},{28,24},{20,28},{12,20},{4,12},{0,4},{10,2},{... | collective-permute-start | bytes 2359304 | tf_op jit(solution)/shard_map/weights_0_step_1/ppermute | solution.py:650
  52.6 18.7 %collective-permute-start.22 = (bf16[512,512]{1,0:T(8,128)(2,1)S(1)}, bf16[512,512]{1,0:T(8,128)(2,1)S(1)}, u32[]{:S(2)}, u32[]{:S(2)}) collective-permute-start(bf16[512,512]{1,0:T(8,128)(2,1)S(1)} %get-tuple-element.405.refs_0_), channel_id=1, source_target_pairs={{0,4},{2,6},{4,0},{6,2},{1,5},{3,7},{5,1},{7,3},{8,12},{10,14},{12... | collective-permute-start | bytes 1572872 | tf_op jit(solution)/shard_map/kv_over_y/ppermute | solution.py:809
  53.3 36.0 %collective-permute-start.27 = (bf16[1024,512]{1,0:T(8,128)(2,1)S(1)}, bf16[1024,512]{1,0:T(8,128)(2,1)S(1)}, u32[]{:S(2)}, u32[]{:S(2)}) collective-permute-start(bf16[1024,512]{1,0:T(8,128)(2,1)S(1)} %get-tuple-element.408.wa_ref.wo_ref), channel_id=1, source_target_pairs={{0,1},{1,0},{2,3},{3,2},{4,5},{5,4},{6,7},{7,6},{8,9},{9,8},{10,11... | collective-permute-start | bytes 3145736 | tf_op jit(solution)/shard_map/w_out_over_tp/ppermute | solution.py:802
  71.3 18.2 %collective-permute-start.23 = (bf16[4,128,768]{2,1,0:T(8,128)(2,1)}, bf16[4,128,768]{2,1,0:T(8,128)(2,1)S(1)}, u32[]{:S(2)}, u32[]{:S(2)}) collective-permute-start(bf16[4,128,768]{2,1,0:T(8,128)(2,1)} %collective-permute-done.18.refs_1_), channel_id=1, source_target_pairs={{0,8},{8,16},{16,24},{24,28},{28,20},{20,12},{12,4},{4,0},{2,10},{... | collective-permute-start | bytes 2359304 | tf_op jit(solution)/shard_map/weights_0_step_2/ppermute | solution.py:650
  90.3 19.6 %collective-permute-start.28 = (bf16[4,128,768]{2,1,0:T(8,128)(2,1)S(1)}, bf16[4,128,768]{2,1,0:T(8,128)(2,1)S(1)}, u32[]{:S(2)}, u32[]{:S(2)}) collective-permute-start(bf16[4,128,768]{2,1,0:T(8,128)(2,1)S(1)} %collective-permute-done.23.refs_3_), channel_id=1, source_target_pairs={{0,8},{8,16},{16,24},{24,28},{28,20},{20,12},{12,4},{4,0},{2,10},{... | collective-permute-start | bytes 2359304 | tf_op jit(solution)/shard_map/weights_0_step_3/ppermute | solution.py:650
  90.4 19.5 %collective-permute-start.29 = (bf16[4,128,768]{2,1,0:T(8,128)(2,1)S(1)}, bf16[4,128,768]{2,1,0:T(8,128)(2,1)S(1)}, u32[]{:S(2)}, u32[]{:S(2)}) collective-permute-start(bf16[4,128,768]{2,1,0:T(8,128)(2,1)S(1)} %collective-permute-done.24.refs_4_), channel_id=1, source_target_pairs={{8,0},{16,8},{24,16},{28,24},{20,28},{12,20},{4,12},{0,4},{10,2},{... | collective-permute-start | bytes 2359304 | tf_op jit(solution)/shard_map/weights_0_step_3/ppermute | solution.py:650
  94.5 25.0 %collective-permute-start.33 = (bf16[512,1024]{1,0:T(8,128)(2,1)}, bf16[512,1024]{1,0:T(8,128)(2,1)}, u32[]{:S(2)}, u32[]{:S(2)}) collective-permute-start(bf16[512,1024]{1,0:T(8,128)(2,1)} %features.1.refs_10_.y_ref), channel_id=1, source_target_pairs={{0,2},{2,0},{4,6},{6,4},{1,3},{3,1},{5,7},{7,5},{8,10},{10,8},{12,... | collective-permute-start | bytes 3145736 | tf_op jit(solution)/shard_map/full_cot_over_core/ppermute | solution.py:798
  122.5 20.0 %collective-permute-start.34 = (bf16[4,128,768]{2,1,0:T(8,128)(2,1)S(1)}, bf16[4,128,768]{2,1,0:T(8,128)(2,1)S(1)}, u32[]{:S(2)}, u32[]{:S(2)}) collective-permute-start(bf16[4,128,768]{2,1,0:T(8,128)(2,1)S(1)} %get-tuple-element.424.refs_0_.refs_9_), channel_id=1, source_target_pairs={{0,8},{8,16},{16,24},{24,28},{28,20},{20,12},{12,4},{4,0},{2,10},{... | collective-permute-start | bytes 2359304 | tf_op jit(solution)/shard_map/weights_1_step_1/ppermute | solution.py:650
  123.9 19.8 %collective-permute-start.35 = (bf16[4,128,768]{2,1,0:T(8,128)(2,1)S(1)}, bf16[4,128,768]{2,1,0:T(8,128)(2,1)S(1)}, u32[]{:S(2)}, u32[]{:S(2)}) collective-permute-start(bf16[4,128,768]{2,1,0:T(8,128)(2,1)S(1)} %get-tuple-element.424.refs_0_.refs_9_), channel_id=1, source_target_pairs={{8,0},{16,8},{24,16},{28,24},{20,28},{12,20},{4,12},{0,4},{10,2},{... | collective-permute-start | bytes 2359304 | tf_op jit(solution)/shard_map/weights_1_step_1/ppermute | solution.py:650
  143.7 18.9 %collective-permute-start.37 = (bf16[4,128,768]{2,1,0:T(8,128)(2,1)S(1)}, bf16[4,128,768]{2,1,0:T(8,128)(2,1)S(1)}, u32[]{:S(2)}, u32[]{:S(2)}) collective-permute-start(bf16[4,128,768]{2,1,0:T(8,128)(2,1)S(1)} %collective-permute-done.34.refs_1_.refs_10_), channel_id=1, source_target_pairs={{0,8},{8,16},{16,24},{24,28},{28,20},{20,12},{12,4},{4,0},{2,10},{... | collective-permute-start | bytes 2359304 | tf_op jit(solution)/shard_map/weights_1_step_2/ppermute | solution.py:650
  144.3 18.8 %collective-permute-start.38 = (bf16[4,128,768]{2,1,0:T(8,128)(2,1)S(1)}, bf16[4,128,768]{2,1,0:T(8,128)(2,1)S(1)}, u32[]{:S(2)}, u32[]{:S(2)}) collective-permute-start(bf16[4,128,768]{2,1,0:T(8,128)(2,1)S(1)} %collective-permute-done.35.refs_2_.refs_11_), channel_id=1, source_target_pairs={{8,0},{16,8},{24,16},{28,24},{20,28},{12,20},{4,12},{0,4},{10,2},{... | collective-permute-start | bytes 2359304 | tf_op jit(solution)/shard_map/weights_1_step_2/ppermute | solution.py:650
  191.4 18.9 %collective-permute-start.43 = (bf16[4,64,768]{2,1,0:T(8,128)(2,1)}, bf16[4,64,768]{2,1,0:T(8,128)(2,1)S(1)}, u32[]{:S(2)}, u32[]{:S(2)}) collective-permute-start(bf16[4,64,768]{2,1,0:T(8,128)(2,1)} %get-tuple-element.462), channel_id=1, source_target_pairs={{0,8},{8,16},{16,24},{24,28},{28,20},{20,12},{12,4},{4,0},{2,10},{... | collective-permute-start | bytes 1179656 | tf_op jit(solution)/shard_map/sums_0_step_1/ppermute | solution.py:650
  212.1 18.6 %collective-permute-start.45 = (bf16[4,128,768]{2,1,0:T(8,128)(2,1)}, bf16[4,128,768]{2,1,0:T(8,128)(2,1)S(1)}, u32[]{:S(2)}, u32[]{:S(2)}) collective-permute-start(bf16[4,128,768]{2,1,0:T(8,128)(2,1)} %get-tuple-element.498), channel_id=1, source_target_pairs={{0,8},{8,16},{16,24},{24,28},{28,20},{20,12},{12,4},{4,0},{2,10},{... | collective-permute-start | bytes 2359304 | tf_op jit(solution)/shard_map/sums_0_step_2/ppermute | solution.py:650
  236.9 20.3 %collective-permute-start.48 = (bf16[4,128,768]{2,1,0:T(8,128)(2,1)}, bf16[4,128,768]{2,1,0:T(8,128)(2,1)}, u32[]{:S(2)}, u32[]{:S(2)}) collective-permute-start(bf16[4,128,768]{2,1,0:T(8,128)(2,1)} %get-tuple-element.508), channel_id=1, source_target_pairs={{0,8},{8,16},{16,24},{24,28},{28,20},{20,12},{12,4},{4,0},{2,10},{... | collective-permute-start | bytes 2359304 | tf_op jit(solution)/shard_map/sums_0_step_3/ppermute | solution.py:650
  238.9 20.1 %collective-permute-start.49 = (bf16[4,128,768]{2,1,0:T(8,128)(2,1)}, bf16[4,128,768]{2,1,0:T(8,128)(2,1)}, u32[]{:S(2)}, u32[]{:S(2)}) collective-permute-start(bf16[4,128,768]{2,1,0:T(8,128)(2,1)} %get-tuple-element.509), channel_id=1, source_target_pairs={{8,0},{16,8},{24,16},{28,24},{20,28},{12,20},{4,12},{0,4},{10,2},{... | collective-permute-start | bytes 2359304 | tf_op jit(solution)/shard_map/sums_0_step_3/ppermute | solution.py:650
  239.2 28.0 %collective-permute-start.52 = (bf16[512,1152]{1,0:T(8,128)(2,1)S(1)}, bf16[512,1152]{1,0:T(8,128)(2,1)S(1)}, u32[]{:S(2)}, u32[]{:S(2)}) collective-permute-start(bf16[512,1152]{1,0:T(8,128)(2,1)S(1)} %add_terms.1.sa_ref), channel_id=1, source_target_pairs={{0,1},{1,0},{2,3},{3,2},{4,5},{5,4},{6,7},{7,6},{8,9},{9,8},{10,11... | collective-permute-start | bytes 3538952 | tf_op jit(solution)/shard_map/part_over_tp/ppermute | solution.py:802
  261.5 24.3 %collective-permute-start.53 = (bf16[512,1024]{1,0:T(8,128)(2,1)}, bf16[512,1024]{1,0:T(8,128)(2,1)S(1)}, u32[]{:S(2)}, u32[]{:S(2)}) collective-permute-start(bf16[512,1024]{1,0:T(8,128)(2,1)} %get-tuple-element.536), channel_id=1, source_target_pairs={{0,2},{2,0},{4,6},{6,4},{1,3},{3,1},{5,7},{7,5},{8,10},{10,8},{12,... | collective-permute-start | bytes 3145736 | tf_op jit(solution)/shard_map/moe_over_core/ppermute | solution.py:798
  261.6 23.2 %collective-permute-start.50 = (bf16[4,128,768]{2,1,0:T(8,128)(2,1)S(1)}, bf16[4,128,768]{2,1,0:T(8,128)(2,1)S(1)}, u32[]{:S(2)}, u32[]{:S(2)}) collective-permute-start(bf16[4,128,768]{2,1,0:T(8,128)(2,1)S(1)} %get-tuple-element.527), channel_id=1, source_target_pairs={{0,8},{8,16},{16,24},{24,28},{28,20},{20,12},{12,4},{4,0},{2,10},{... | collective-permute-start | bytes 2359304 | tf_op jit(solution)/shard_map/sums_0_step_4/ppermute | solution.py:650
  262.3 22.6 %collective-permute-start.51 = (bf16[4,128,768]{2,1,0:T(8,128)(2,1)S(1)}, bf16[4,128,768]{2,1,0:T(8,128)(2,1)S(1)}, u32[]{:S(2)}, u32[]{:S(2)}) collective-permute-start(bf16[4,128,768]{2,1,0:T(8,128)(2,1)S(1)} %get-tuple-element.528), channel_id=1, source_target_pairs={{8,0},{16,8},{24,16},{28,24},{20,28},{12,20},{4,12},{0,4},{10,2},{... | collective-permute-start | bytes 2359304 | tf_op jit(solution)/shard_map/sums_0_step_4/ppermute | solution.py:650
  301.1 30.7 %collective-permute-start.60 = (bf16[4,128,768]{2,1,0:T(8,128)(2,1)}, bf16[4,128,768]{2,1,0:T(8,128)(2,1)S(1)}, u32[]{:S(2)}, u32[]{:S(2)}) collective-permute-start(bf16[4,128,768]{2,1,0:T(8,128)(2,1)} %copy-done.70), channel_id=1, source_target_pairs={{0,8},{8,16},{16,24},{24,28},{28,20},{20,12},{12,4},{4,0},{2,10},{... | collective-permute-start | bytes 2359304 | tf_op jit(solution)/shard_map/sums_1_step_2/ppermute | solution.py:650
  302.2 29.6 %collective-permute-start.61 = (bf16[4,128,768]{2,1,0:T(8,128)(2,1)}, bf16[4,128,768]{2,1,0:T(8,128)(2,1)S(1)}, u32[]{:S(2)}, u32[]{:S(2)}) collective-permute-start(bf16[4,128,768]{2,1,0:T(8,128)(2,1)} %copy-done.69), channel_id=1, source_target_pairs={{8,0},{16,8},{24,16},{28,24},{20,28},{12,20},{4,12},{0,4},{10,2},{... | collective-permute-start | bytes 2359304 | tf_op jit(solution)/shard_map/sums_1_step_2/ppermute | solution.py:650
  332.2 26.1 %collective-permute-start.62 = (bf16[4,128,768]{2,1,0:T(8,128)(2,1)S(1)}, bf16[4,128,768]{2,1,0:T(8,128)(2,1)S(1)}, u32[]{:S(2)}, u32[]{:S(2)}) collective-permute-start(bf16[4,128,768]{2,1,0:T(8,128)(2,1)S(1)} %get-tuple-element.579), channel_id=1, source_target_pairs={{0,8},{8,16},{16,24},{24,28},{28,20},{20,12},{12,4},{4,0},{2,10},{... | collective-permute-start | bytes 2359304 | tf_op jit(solution)/shard_map/sums_1_step_3/ppermute | solution.py:650
  332.3 26.0 %collective-permute-start.63 = (bf16[4,128,768]{2,1,0:T(8,128)(2,1)S(1)}, bf16[4,128,768]{2,1,0:T(8,128)(2,1)S(1)}, u32[]{:S(2)}, u32[]{:S(2)}) collective-permute-start(bf16[4,128,768]{2,1,0:T(8,128)(2,1)S(1)} %get-tuple-element.580), channel_id=1, source_target_pairs={{8,0},{16,8},{24,16},{28,24},{20,28},{12,20},{4,12},{0,4},{10,2},{... | collective-permute-start | bytes 2359304 | tf_op jit(solution)/shard_map/sums_1_step_3/ppermute | solution.py:650
  334.3 19.2 %collective-permute-start.64 = (bf16[1,32,1792]{2,1,0:T(8,128)(2,1)S(1)}, bf16[1,32,1792]{2,1,0:T(8,128)(2,1)S(1)}, u32[]{:S(2)}, u32[]{:S(2)}) collective-permute-start(bf16[1,32,1792]{2,1,0:T(8,128)(2,1)S(1)} %get-tuple-element.581), channel_id=1, source_target_pairs={{0,8},{8,16},{16,24},{24,28},{28,20},{20,12},{12,4},{4,0},{2,10},{... | collective-permute-start | bytes 344072 | tf_op jit(solution)/shard_map/last_step_1/ppermute | solution.py:650
  334.3 28.1 %collective-permute-start.71 = (bf16[512,512]{1,0:T(8,128)(2,1)S(1)}, bf16[512,512]{1,0:T(8,128)(2,1)S(1)}, u32[]{:S(2)}, u32[]{:S(2)}) collective-permute-start(bf16[512,512]{1,0:T(8,128)(2,1)S(1)} %dynamic-slice_convert_fusion), channel_id=1, source_target_pairs={{0,1},{1,0},{2,3},{3,2},{4,5},{5,4},{6,7},{7,6},{8,9},{9,8},{10,11... | collective-permute-start | bytes 1572872 | tf_op jit(solution)/shard_map/moe_send_over_tp/ppermute | solution.py:802
  335.8 29.2 %collective-permute-start.70 = (bf16[512,640]{1,0:T(8,128)(2,1)}, bf16[512,640]{1,0:T(8,128)(2,1)}, u32[]{:S(2)}, u32[]{:S(2)}) collective-permute-start(bf16[512,640]{1,0:T(8,128)(2,1)} %get-tuple-element.599), channel_id=1, source_target_pairs={{0,1},{1,0},{2,3},{3,2},{4,5},{5,4},{6,7},{7,6},{8,9},{9,8},{10,11... | collective-permute-start | bytes 1966088 | tf_op jit(solution)/shard_map/grad_normed_over_tp/ppermute | solution.py:802
  360.1 29.5 %collective-permute-start.66 = (bf16[4,128,768]{2,1,0:T(8,128)(2,1)}, bf16[4,128,768]{2,1,0:T(8,128)(2,1)S(1)}, u32[]{:S(2)}, u32[]{:S(2)}) collective-permute-start(bf16[4,128,768]{2,1,0:T(8,128)(2,1)} %get-tuple-element.593), channel_id=1, source_target_pairs={{0,8},{8,16},{16,24},{24,28},{28,20},{20,12},{12,4},{4,0},{2,10},{... | collective-permute-start | bytes 2359304 | tf_op jit(solution)/shard_map/sums_1_step_4/ppermute | solution.py:650
  360.4 29.2 %collective-permute-start.67 = (bf16[4,128,768]{2,1,0:T(8,128)(2,1)}, bf16[4,128,768]{2,1,0:T(8,128)(2,1)S(1)}, u32[]{:S(2)}, u32[]{:S(2)}) collective-permute-start(bf16[4,128,768]{2,1,0:T(8,128)(2,1)} %get-tuple-element.594), channel_id=1, source_target_pairs={{8,0},{16,8},{24,16},{28,24},{20,28},{12,20},{4,12},{0,4},{10,2},{... | collective-permute-start | bytes 2359304 | tf_op jit(solution)/shard_map/sums_1_step_4/ppermute | solution.py:650
  362.1 20.3 %collective-permute-start.68 = (bf16[1,64,1792]{2,1,0:T(8,128)(2,1)S(1)}, bf16[1,64,1792]{2,1,0:T(8,128)(2,1)S(1)}, u32[]{:S(2)}, u32[]{:S(2)}) collective-permute-start(bf16[1,64,1792]{2,1,0:T(8,128)(2,1)S(1)} %get-tuple-element.597), channel_id=1, source_target_pairs={{0,8},{8,16},{16,24},{24,28},{28,20},{20,12},{12,4},{4,0},{2,10},{... | collective-permute-start | bytes 688136 | tf_op jit(solution)/shard_map/last_step_2/ppermute | solution.py:650
  363.2 19.6 %collective-permute-start.69 = (bf16[1,64,1792]{2,1,0:T(8,128)(2,1)S(1)}, bf16[1,64,1792]{2,1,0:T(8,128)(2,1)S(1)}, u32[]{:S(2)}, u32[]{:S(2)}) collective-permute-start(bf16[1,64,1792]{2,1,0:T(8,128)(2,1)S(1)} %get-tuple-element.598), channel_id=1, source_target_pairs={{8,0},{16,8},{24,16},{28,24},{20,28},{12,20},{4,12},{0,4},{10,2},{... | collective-permute-start | bytes 688136 | tf_op jit(solution)/shard_map/last_step_2/ppermute | solution.py:650
  (155 other events, 1669.0 us)
